TPU v7x, 128 devices: a whole 4x4x4 slice. The times are simulated.
128 devices in a mesh: brick: 128 (over z, x, y, core).
Axes of the slice: x: 4, y: 4, z: 4, core: 2. Of those that a mesh axis runs over, the one named last changes fastest.
Arguments:
- positions: float32 [3, 65536], P(None, 'brick'), may hold values from 0 to 3
- species: int32 [65536], P('brick'), may hold values from 0 to 7
- pair_first: int32 [6144, 128], P('brick'), may hold values from 0 to 511
- pair_second: int32 [6144, 128], P('brick'), may hold values from 0 to 1535, as said below
- pair_valid: int32 [6144, 128], P('brick'), may hold values from 0 to 1, as said below
- send_list: int32 [512, 256], P('brick'), may hold values from 0 to 511, as said below
- w_radial: float32 [64, 8], replicated, may hold values from -2 to 2
- w_first: float32 [64, 8], replicated, may hold values from -3.5 to 3.5
- w_second: float32 [64, 8], replicated, may hold values from -3.5 to 3.5
- w_value: float32 [2, 32, 64], replicated, may hold values from -0.75 to 0.75
- w_env: float32 [2, 32, 64], replicated, may hold values from -0.75 to 0.75
- w_latent: float32 [2, 64, 64], replicated, may hold values from -0.75 to 0.75
- w_tensor: float32 [2, 64, 32], replicated, may hold values from -1 to 1
- w_mix: float32 [2, 64, 64], replicated, may hold values from -0.75 to 0.75
- w_read: float32 [64, 64], replicated, may hold values from -0.75 to 0.75
- read_vec: float32 [64], replicated, may hold values from -0.75 to 0.75
Outputs:
- forces: float32 [3, 65536], P(None, 'brick')
- energy: float32 [], replicated
Inputs may be any that keep to these rules, and one draw needn't show every extreme that they name: `pair_second`: below 512: an atom of the block's brick. Otherwise a ghost slot as in the first step, only toward bricks that exist. `pair_valid`: A brick's valid pairs fill whole blocks from its first block on; the last brick's blocks are all valid. `send_list`: each row holds 256 distinct atoms of its brick.
All inputs are finite; a program needn't handle non-finite values.
Results may differ from a plain program's by a relative error of at most 0.0003.
Values sent between devices are 32-bit elements; how exact they have to be, the bound alone decides.
No kernel may reach another device: no remote copies, remote signals or barrier semaphores. Data moves between devices by JAX's collectives and lax.ppermute only.
A program may use at most 128 MiB of HBM per device.

v0:
```python
import math

import jax
import jax.numpy as jnp
from jax import lax
from jax.sharding import PartitionSpec as P

CUTOFF = 6.0
SOFTENING = 0.25
ENV_SCALE = 0.25
PAIR_SHIFT = 1.0
OFFSETS = (1, -1, 2, -2)


def shifted(shard, axis, by):
    count = lax.axis_size(axis)
    pairs = [(i, i + by) for i in range(count) if 0 <= i + by < count]
    return lax.ppermute(shard, axis, pairs)


def matmul(left, right):
    return jnp.dot(left, right, precision=lax.Precision.HIGHEST, preferred_element_type=jnp.float32)


def geometry(coord_first, coord_second, nbasis):
    difference = coord_second - coord_first
    distance = jnp.sqrt(jnp.sum(difference * difference, axis=0) + SOFTENING)
    direction = difference / distance
    envelope = (1.0 - (distance / CUTOFF) ** 2) ** 2
    frequency = jnp.arange(1, nbasis + 1).astype(distance.dtype) * (math.pi / CUTOFF)
    radial_basis = (
        jnp.sin(frequency[:, None] * distance[None, :]) / distance[None, :] * envelope[None, :]
    )
    return (direction, envelope, radial_basis)


def embed_pairs(
    coord_first, coord_second, species_first, species_second, w_radial, w_first, w_second
):
    direction, envelope, radial_basis = geometry(coord_first, coord_second, w_radial.shape[1])
    species_kinds = jnp.arange(w_first.shape[1], dtype=jnp.int32)
    onehot_first = (species_first[None, :] == species_kinds[:, None]).astype(radial_basis.dtype)
    onehot_second = (species_second[None, :] == species_kinds[:, None]).astype(radial_basis.dtype)
    return jax.nn.silu(
        matmul(w_radial, radial_basis)
        + matmul(w_first, onehot_first)
        + matmul(w_second, onehot_second)
    )


def contributions(latent_in, coord_first, coord_second, env_weight, live_mask, incidence):
    direction, envelope, radial_basis = geometry(coord_first, coord_second, 1)
    scaled = matmul(env_weight, latent_in) * (envelope * live_mask)[None, :]
    vectors = (direction[:, None, :] * scaled[None, :, :]).reshape(-1, latent_in.shape[1])
    return matmul(vectors, incidence)


def update_latent(
    latent_in,
    coord_first,
    coord_second,
    table_in,
    value_weight,
    latent_weight,
    tensor_weight,
    mix_weight,
    incidence,
):
    direction, envelope, radial_basis = geometry(coord_first, coord_second, 1)
    channel_values = matmul(value_weight, latent_in)
    channels = channel_values.shape[0]
    gap_table = lax.dot_general(
        table_in,
        incidence,
        (((1,), (1,)), ((), ())),
        precision=lax.Precision.HIGHEST,
        preferred_element_type=jnp.float32,
    ).reshape(3, channels, -1)
    scalars = ENV_SCALE * jnp.sum(
        direction[:, None, :] * channel_values[None, :, :] * gap_table, axis=0
    )
    hidden = jax.nn.silu(matmul(latent_weight, latent_in) + matmul(tensor_weight, scalars))
    return latent_in + matmul(mix_weight, hidden)


def readout(latent_in, coord_first, coord_second, w_read, read_vec, live_mask):
    direction, envelope, radial_basis = geometry(coord_first, coord_second, 1)
    energies = matmul(read_vec, jax.nn.silu(matmul(w_read, latent_in)))
    return jnp.sum((energies + PAIR_SHIFT) * envelope * live_mask)


def copy_out(values, send_list):
    pieces = []
    for group_index, shift_by in enumerate(OFFSETS):
        pieces.append(shifted(values[:, send_list[group_index]], "brick", shift_by))
    return jnp.concatenate(pieces, axis=1)


def return_in(ghost_rows, send_list, own_count):
    width = send_list.shape[1]
    blocks = [
        ghost_rows[:, group_index * width : (group_index + 1) * width] for group_index in range(4)
    ]
    arrived = []
    for group_index, shift_by in enumerate(OFFSETS):
        arrived.append(shifted(blocks[group_index], "brick", -shift_by))
    summed = jnp.zeros((ghost_rows.shape[0], own_count), ghost_rows.dtype)
    for group_index in range(4):
        summed = summed.at[:, send_list[group_index]].add(arrived[group_index])
    return summed


def per_device(
    positions,
    species,
    pair_first,
    pair_second,
    pair_valid,
    send_list,
    w_radial,
    w_first,
    w_second,
    w_value,
    w_env,
    w_latent,
    w_tensor,
    w_mix,
    w_read,
    read_vec,
):
    own_count = positions.shape[1]
    ghost_count = send_list.shape[1]
    table_rows = own_count + 4 * ghost_count
    first_ids = pair_first.reshape(-1)
    second_ids = pair_second.reshape(-1)
    live_mask = pair_valid.reshape(-1).astype(jnp.float32)
    row_index = jnp.arange(table_rows, dtype=jnp.int32)
    incidence = (first_ids[:, None] == row_index[None, :]).astype(jnp.float32) - (
        second_ids[:, None] == row_index[None, :]
    ).astype(jnp.float32)
    coords_species = jnp.concatenate([positions, species[None, :].astype(jnp.float32)], axis=0)
    ghost_data = copy_out(coords_species, send_list)
    table_coords = jnp.concatenate([positions, ghost_data[:3]], axis=1)
    table_species = jnp.concatenate([species, ghost_data[3].astype(jnp.int32)])
    coord_first = table_coords[:, first_ids]
    coord_second = table_coords[:, second_ids]
    species_first = species[first_ids]
    species_second = table_species[second_ids]

    def complete_table(partial_table):
        owned = partial_table[:, :own_count] + return_in(
            partial_table[:, own_count:], send_list, own_count
        )
        return jnp.concatenate([owned, copy_out(owned, send_list)], axis=1)

    def embed_fn(coord_a, coord_b):
        return embed_pairs(
            coord_a, coord_b, species_first, species_second, w_radial, w_first, w_second
        )

    latent, embed_back = jax.vjp(embed_fn, coord_first, coord_second)
    saved_backs = []
    for layer_index in range(w_value.shape[0]):

        def contrib_fn(latent_in, coord_a, coord_b, env_weight=w_env[layer_index]):
            return contributions(latent_in, coord_a, coord_b, env_weight, live_mask, incidence)

        def update_fn(latent_in, coord_a, coord_b, table_in, depth=layer_index):
            return update_latent(
                latent_in,
                coord_a,
                coord_b,
                table_in,
                w_value[depth],
                w_latent[depth],
                w_tensor[depth],
                w_mix[depth],
                incidence,
            )

        partial_table, contrib_back = jax.vjp(contrib_fn, latent, coord_first, coord_second)
        completed = complete_table(partial_table)
        latent, update_back = jax.vjp(update_fn, latent, coord_first, coord_second, completed)
        saved_backs.append((contrib_back, update_back))

    def read_fn(latent_in, coord_a, coord_b):
        return readout(latent_in, coord_a, coord_b, w_read, read_vec, live_mask)

    energy_local, read_back = jax.vjp(read_fn, latent, coord_first, coord_second)
    grad_latent, grad_first, grad_second = read_back(jnp.ones((), energy_local.dtype))
    for contrib_back, update_back in reversed(saved_backs):
        grad_update, more_first, more_second, grad_table = update_back(grad_latent)
        grad_contrib = complete_table(grad_table)
        grad_inner, extra_first, extra_second = contrib_back(grad_contrib)
        grad_latent = grad_update + grad_inner
        grad_first = grad_first + more_first + extra_first
        grad_second = grad_second + more_second + extra_second
    embed_first, embed_second = embed_back(grad_latent)
    grad_first = grad_first + embed_first
    grad_second = grad_second + embed_second
    grad_table = (
        jnp.zeros((3, table_rows), jnp.float32)
        .at[:, first_ids]
        .add(grad_first)
        .at[:, second_ids]
        .add(grad_second)
    )
    grad_owned = grad_table[:, :own_count] + return_in(
        grad_table[:, own_count:], send_list, own_count
    )
    energy_total = lax.psum(energy_local, "brick")
    return (-grad_owned, energy_total / (lax.axis_size("brick") * live_mask.shape[0]))


def solution(mesh):
    return jax.shard_map(
        per_device,
        mesh=mesh,
        in_specs=(
            P(None, "brick"),
            P("brick"),
            P("brick", None),
            P("brick", None),
            P("brick", None),
            P("brick", None),
            P(),
            P(),
            P(),
            P(),
            P(),
            P(),
            P(),
            P(),
            P(),
            P(),
        ),
        out_specs=(P(None, "brick"), P()),
        check_vma=False,
    )
```

profile of v0, /device:TPU:1, one launch (start us, length us, event | category | flops | bytes accessed | tf_op | source)
XLA Modules:
  0.0 953.2 jit_solution(6972403210475872214)
XLA Ops:
  18.8 38.6 %gather_fusion.6 = s32[6144]{0:T(1024)S(1)} fusion(s32[512]{0:T(512)S(1)} %copy-done.2, s32[6144]{0:T(1024)S(1)} %get-tuple-element.72), kind=kCustom, calls=%fused_computation.6 | custom fusion | bytes 73728 | tf_op jit(solution)/shard_map/gather | solution.py:147
  59.0 34.3 %gather_fusion.7 = s32[6144]{0:T(1024)S(1)} fusion(s32[1536]{0:T(1024)S(1)} %pad_add_fusion, s32[6144]{0:T(1024)S(1)} %broadcast_clamp_fusion.2), kind=kCustom, calls=%fused_computation.7 | custom fusion | bytes 73728 | tf_op jit(solution)/shard_map/gather | solution.py:148
  93.3 20.9 %gather_fusion.4 = f32[6144,3]{1,0:T(8,128)} fusion(f32[3,1536]{0,1:T(8,128)S(1)} %copy.123, s32[6144]{0:T(1024)S(1)} %broadcast_clamp_fusion.2), kind=kCustom, calls=%fused_computation.4 | custom fusion | bytes 172032 | tf_op jit(solution)/shard_map/gather | solution.py:146
  114.2 20.9 %gather_fusion.5 = f32[6144,3]{1,0:T(8,128)} fusion(f32[3,1536]{0,1:T(8,128)S(1)} %copy.123, s32[6144]{0:T(1024)S(1)} %get-tuple-element.73), kind=kCustom, calls=%fused_computation.5 | custom fusion | bytes 172032 | tf_op jit(solution)/shard_map/gather | solution.py:145
  149.9 34.8 %fusion.7 = f32[96,1536]{1,0:T(8,128)S(1)} fusion(f32[96,6144]{1,0:T(8,128)S(1)} %bitcast.321, s32[6144]{0:T(1024)S(1)} %bitcast.371, s32[6144]{0:T(1024)S(1)} %bitcast.380), kind=kOutput, calls=%fused_computation.55 | convolution fusion | flops 10918821888 | bytes 2998272 | tf_op jit(solution)/shard_map/jvp()/dot_general | solution.py:22
  185.3 4.6 collective-permute-start.7
  191.2 4.3 collective-permute-start.5
  225.5 6.8 collective-permute-done.11
  232.3 46.0 %fusion.6 = f32[96,6144]{1,0:T(8,128)S(1)} fusion(f32[96,1536]{0,1:T(8,128)S(1)} %constant_dynamic-update-slice_fusion, s32[6144]{0:T(1024)S(1)} %bitcast.372, s32[6144]{0:T(1024)S(1)} %bitcast.381), kind=kOutput, calls=%fused_computation.54 | convolution fusion | flops 10918821888 | bytes 2998272 | tf_op jit(solution)/shard_map/jvp()/dot_general | solution.py:72
  289.1 34.8 %fusion.5 = f32[96,1536]{1,0:T(8,128)S(1)} fusion(f32[96,6144]{1,0:T(8,128)S(1)} %bitcast.322, s32[6144]{0:T(1024)S(1)} %bitcast.373, s32[6144]{0:T(1024)S(1)} %bitcast.382), kind=kOutput, calls=%fused_computation.53 | convolution fusion | flops 10918821888 | bytes 2998272 | tf_op jit(solution)/shard_map/jvp()/dot_general | solution.py:22
  324.7 7.9 collective-permute-start.15
  333.9 7.2 collective-permute-start.13
  368.0 3.8 collective-permute-start.16
  373.7 5.8 collective-permute-start.18
  382.3 4.5 collective-permute-done.19
  386.8 47.3 %fusion.4 = f32[96,6144]{1,0:T(8,128)S(1)} fusion(f32[96,1536]{0,1:T(8,128)S(1)} %constant_dynamic-update-slice_fusion.5, s32[6144]{0:T(1024)S(1)} %bitcast.374, s32[6144]{0:T(1024)S(1)} %bitcast.383), kind=kOutput, calls=%fused_computation.52 | convolution fusion | flops 10918821888 | bytes 2998272 | tf_op jit(solution)/shard_map/jvp()/dot_general | solution.py:72
  450.7 36.0 %fusion.3 = f32[96,1536]{1,0:T(8,128)S(1)} fusion(f32[96,6144]{1,0:T(8,128)} %bitcast.319, s32[6144]{0:T(1024)S(1)} %bitcast.375, s32[6144]{0:T(1024)S(1)} %bitcast.384), kind=kOutput, calls=%fused_computation.51 | convolution fusion | flops 10918821888 | bytes 2998272 | tf_op jit(solution)/shard_map/transpose(jvp())/dot_general | solution.py:72
  487.3 5.3 collective-permute-start.23
  493.9 7.2 collective-permute-start.21
  530.0 5.8 collective-permute-start.26
  538.6 4.6 collective-permute-done.27
  543.3 47.1 %fusion.2 = f32[96,6144]{1,0:T(8,128)S(1)} fusion(f32[96,1536]{0,1:T(8,128)S(1)} %constant_dynamic-update-slice_fusion.10, s32[6144]{0:T(1024)S(1)} %bitcast.376, s32[6144]{0:T(1024)S(1)} %bitcast.385), kind=kOutput, calls=%fused_computation.50 | convolution fusion | flops 10918821888 | bytes 2998272 | tf_op jit(solution)/shard_map/transpose(jvp())/dot_general | solution.py:22
  600.7 34.8 %fusion.1 = f32[96,1536]{1,0:T(8,128)S(1)} fusion(f32[96,6144]{1,0:T(8,128)S(1)} %bitcast.320, s32[6144]{0:T(1024)S(1)} %bitcast.377, s32[6144]{0:T(1024)S(1)} %bitcast.386), kind=kOutput, calls=%fused_computation.49 | convolution fusion | flops 10918821888 | bytes 2998272 | tf_op jit(solution)/shard_map/transpose(jvp())/dot_general | solution.py:72
  636.3 4.6 collective-permute-start.31
  642.2 8.2 collective-permute-start.29
  677.9 5.8 collective-permute-start.34
  686.2 4.6 collective-permute-done.35
  690.9 46.9 %fusion = f32[96,6144]{1,0:T(8,128)S(1)} fusion(f32[96,1536]{0,1:T(8,128)S(1)} %constant_dynamic-update-slice_fusion.15, s32[6144]{0:T(1024)S(1)} %bitcast.378, s32[6144]{0:T(1024)S(1)} %bitcast.387), kind=kOutput, calls=%fused_computation.48 | convolution fusion | flops 10918821888 | bytes 2998272 | tf_op jit(solution)/shard_map/transpose(jvp())/dot_general | solution.py:22
  748.5 33.7 %scatter_custom_fusion.16 = f32[3,1536]{0,1:T(8,128)S(1)} fusion(s32[6144]{0:T(1024)} %bitcast.330, f32[6144,3]{1,0:T(8,128)} %copy.147, f32[]{:T(128)} %constant.13.clone.1), kind=kCustom, calls=%fused_computation.165 | custom fusion | flops 18432 | bytes 18944 | tf_op jit(solution)/shard_map/scatter-add | solution.py:204
  782.2 33.8 %scatter_fusion.16 = f32[3,1536]{0,1:T(8,128)S(1)} fusion(f32[3,1536]{0,1:T(8,128)S(1)} %scatter_custom_fusion.16, s32[6144]{0:T(1024)S(1)} %bitcast.326, f32[6144,3]{1,0:T(8,128)} %copy.148), kind=kCustom, calls=%fused_computation.41 | custom fusion | flops 18432 | bytes 245760 | tf_op jit(solution)/shard_map/scatter-add | solution.py:206
  823.0 8.6 collective-permute-start.39
  831.6 110.5 %psum.7 = f32[]{:T(128)} all-reduce(f32[]{:T(128)} %get-tuple-element.51), channel_id=1, replica_groups=mesh['brick'=128] {'brick'}, use_global_device_ids=true, to_apply=%region_43.44 | all-reduce | flops 1 | bytes 8 | tf_op jit(solution)/shard_map/psum | solution.py:211
  (380 shorter events, 228.5 us)
Async XLA Ops:
  3.9 54.4 %collective-permute-start.1 = (f32[4,256]{0,1:T(8,128)S(1)}, f32[4,256]{0,1:T(8,128)S(1)}, u32[]{:S(2)}, u32[]{:S(2)}) collective-permute-start(f32[4,256]{0,1:T(8,128)S(1)} %bitcast.391), channel_id=1, source_target_pairs={{1,0},{2,1},{3,2},{4,3},{5,4},{6,5},{7,6},{8,7},{9,8},{10,9},{11,1... | collective-permute-start | bytes 12296 | tf_op jit(solution)/shard_map/ppermute | solution.py:18
  7.9 50.4 %collective-permute-start = (f32[4,256]{0,1:T(8,128)S(1)}, f32[4,256]{0,1:T(8,128)S(1)}, u32[]{:S(2)}, u32[]{:S(2)}) collective-permute-start(f32[4,256]{0,1:T(8,128)S(1)} %bitcast.392), channel_id=1, source_target_pairs={{0,1},{1,2},{2,3},{3,4},{4,5},{5,6},{6,7},{7,8},{8,9},{9,10},{10,1... | collective-permute-start | bytes 12296 | tf_op jit(solution)/shard_map/ppermute | solution.py:18
  11.9 46.5 %collective-permute-start.2 = (f32[4,256]{0,1:T(8,128)S(1)}, f32[4,256]{0,1:T(8,128)S(1)}, u32[]{:S(2)}, u32[]{:S(2)}) collective-permute-start(f32[4,256]{0,1:T(8,128)S(1)} %bitcast.393), channel_id=1, source_target_pairs={{0,2},{1,3},{2,4},{3,5},{4,6},{5,7},{6,8},{7,9},{8,10},{9,11},{10,... | collective-permute-start | bytes 12296 | tf_op jit(solution)/shard_map/ppermute | solution.py:18
  15.8 42.7 %collective-permute-start.3 = (f32[4,256]{0,1:T(8,128)S(1)}, f32[4,256]{0,1:T(8,128)S(1)}, u32[]{:S(2)}, u32[]{:S(2)}) collective-permute-start(f32[4,256]{0,1:T(8,128)S(1)} %bitcast.394), channel_id=1, source_target_pairs={{2,0},{3,1},{4,2},{5,3},{6,4},{7,5},{8,6},{9,7},{10,8},{11,9},{12,... | collective-permute-start | bytes 12296 | tf_op jit(solution)/shard_map/ppermute | solution.py:18
  185.3 14.2 %collective-permute-start.7 = (f32[96,256]{1,0:T(8,128)}, f32[96,256]{1,0:T(8,128)}, u32[]{:S(2)}, u32[]{:S(2)}) collective-permute-start(f32[96,256]{1,0:T(8,128)} %get-tuple-element.47), channel_id=1, source_target_pairs={{0,2},{1,3},{2,4},{3,5},{4,6},{5,7},{6,8},{7,9},{8,10},{9,11},{10,... | collective-permute-start | bytes 294920 | tf_op jit(solution)/shard_map/ppermute | solution.py:18
  189.9 10.7 %collective-permute-start.6 = (f32[96,256]{1,0:T(8,128)S(1)}, f32[96,256]{1,0:T(8,128)}, u32[]{:S(2)}, u32[]{:S(2)}) collective-permute-start(f32[96,256]{1,0:T(8,128)S(1)} %get-tuple-element.48), channel_id=1, source_target_pairs={{2,0},{3,1},{4,2},{5,3},{6,4},{7,5},{8,6},{9,7},{10,8},{11,9},{12,... | collective-permute-start | bytes 294920 | tf_op jit(solution)/shard_map/ppermute | solution.py:18
  191.2 10.4 %collective-permute-start.5 = (f32[96,256]{1,0:T(8,128)S(1)}, f32[96,256]{1,0:T(8,128)}, u32[]{:S(2)}, u32[]{:S(2)}) collective-permute-start(f32[96,256]{1,0:T(8,128)S(1)} %get-tuple-element.49), channel_id=1, source_target_pairs={{0,1},{1,2},{2,3},{3,4},{4,5},{5,6},{6,7},{7,8},{8,9},{9,10},{10,1... | collective-permute-start | bytes 294920 | tf_op jit(solution)/shard_map/ppermute | solution.py:18
  215.1 10.0 %collective-permute-start.8 = (f32[96,256]{0,1:T(8,128)S(1)}, f32[96,256]{0,1:T(8,128)S(1)}, u32[]{:S(2)}, u32[]{:S(2)}) collective-permute-start(f32[96,256]{0,1:T(8,128)S(1)} %bitcast.343), channel_id=1, source_target_pairs={{0,1},{1,2},{2,3},{3,4},{4,5},{5,6},{6,7},{7,8},{8,9},{9,10},{10,1... | collective-permute-start | bytes 294920 | tf_op jit(solution)/shard_map/ppermute | solution.py:18
  223.5 8.7 collective-permute-start.11
  324.7 21.2 %collective-permute-start.15 = (f32[96,256]{1,0:T(8,128)}, f32[96,256]{1,0:T(8,128)}, u32[]{:S(2)}, u32[]{:S(2)}) collective-permute-start(f32[96,256]{1,0:T(8,128)} %get-tuple-element.43), channel_id=1, source_target_pairs={{0,2},{1,3},{2,4},{3,5},{4,6},{5,7},{6,8},{7,9},{8,10},{9,11},{10,... | collective-permute-start | bytes 294920 | tf_op jit(solution)/shard_map/ppermute | solution.py:18
  332.6 15.0 %collective-permute-start.14 = (f32[96,256]{1,0:T(8,128)}, f32[96,256]{1,0:T(8,128)}, u32[]{:S(2)}, u32[]{:S(2)}) collective-permute-start(f32[96,256]{1,0:T(8,128)} %get-tuple-element.44), channel_id=1, source_target_pairs={{2,0},{3,1},{4,2},{5,3},{6,4},{7,5},{8,6},{9,7},{10,8},{11,9},{12,... | collective-permute-start | bytes 294920 | tf_op jit(solution)/shard_map/ppermute | solution.py:18
  333.9 15.3 %collective-permute-start.13 = (f32[96,256]{1,0:T(8,128)}, f32[96,256]{1,0:T(8,128)}, u32[]{:S(2)}, u32[]{:S(2)}) collective-permute-start(f32[96,256]{1,0:T(8,128)} %get-tuple-element.45), channel_id=1, source_target_pairs={{0,1},{1,2},{2,3},{3,4},{4,5},{5,6},{6,7},{7,8},{8,9},{9,10},{10,1... | collective-permute-start | bytes 294920 | tf_op jit(solution)/shard_map/ppermute | solution.py:18
  341.0 9.8 %collective-permute-start.12 = (f32[96,256]{1,0:T(8,128)}, f32[96,256]{1,0:T(8,128)}, u32[]{:S(2)}, u32[]{:S(2)}) collective-permute-start(f32[96,256]{1,0:T(8,128)} %get-tuple-element.46), channel_id=1, source_target_pairs={{1,0},{2,1},{3,2},{4,3},{5,4},{6,5},{7,6},{8,7},{9,8},{10,9},{11,1... | collective-permute-start | bytes 294920 | tf_op jit(solution)/shard_map/ppermute | solution.py:18
  368.0 12.8 %collective-permute-start.16 = (f32[96,256]{0,1:T(8,128)}, f32[96,256]{0,1:T(8,128)S(1)}, u32[]{:S(2)}, u32[]{:S(2)}) collective-permute-start(f32[96,256]{0,1:T(8,128)} %bitcast.344), channel_id=1, source_target_pairs={{0,1},{1,2},{2,3},{3,4},{4,5},{5,6},{6,7},{7,8},{8,9},{9,10},{10,1... | collective-permute-start | bytes 294920 | tf_op jit(solution)/shard_map/ppermute | solution.py:18
  371.8 9.0 collective-permute-start.17
  373.7 8.6 collective-permute-start.18
  487.3 19.3 %collective-permute-start.23 = (f32[96,256]{1,0:T(8,128)}, f32[96,256]{1,0:T(8,128)}, u32[]{:S(2)}, u32[]{:S(2)}) collective-permute-start(f32[96,256]{1,0:T(8,128)} %get-tuple-element.39), channel_id=1, source_target_pairs={{0,2},{1,3},{2,4},{3,5},{4,6},{5,7},{6,8},{7,9},{8,10},{9,11},{10,... | collective-permute-start | bytes 294920 | tf_op jit(solution)/shard_map/ppermute | solution.py:18
  492.7 14.9 %collective-permute-start.22 = (f32[96,256]{1,0:T(8,128)S(1)}, f32[96,256]{1,0:T(8,128)}, u32[]{:S(2)}, u32[]{:S(2)}) collective-permute-start(f32[96,256]{1,0:T(8,128)S(1)} %get-tuple-element.40), channel_id=1, source_target_pairs={{2,0},{3,1},{4,2},{5,3},{6,4},{7,5},{8,6},{9,7},{10,8},{11,9},{12,... | collective-permute-start | bytes 294920 | tf_op jit(solution)/shard_map/ppermute | solution.py:18
  493.9 14.6 %collective-permute-start.21 = (f32[96,256]{1,0:T(8,128)S(1)}, f32[96,256]{1,0:T(8,128)}, u32[]{:S(2)}, u32[]{:S(2)}) collective-permute-start(f32[96,256]{1,0:T(8,128)S(1)} %get-tuple-element.41), channel_id=1, source_target_pairs={{0,1},{1,2},{2,3},{3,4},{4,5},{5,6},{6,7},{7,8},{8,9},{9,10},{10,1... | collective-permute-start | bytes 294920 | tf_op jit(solution)/shard_map/ppermute | solution.py:18
  524.5 12.7 %collective-permute-start.24 = (f32[96,256]{0,1:T(8,128)}, f32[96,256]{0,1:T(8,128)S(1)}, u32[]{:S(2)}, u32[]{:S(2)}) collective-permute-start(f32[96,256]{0,1:T(8,128)} %bitcast.73), channel_id=1, source_target_pairs={{0,1},{1,2},{2,3},{3,4},{4,5},{5,6},{6,7},{7,8},{8,9},{9,10},{10,1... | collective-permute-start | bytes 294920 | tf_op jit(solution)/shard_map/ppermute | solution.py:18
  528.1 9.0 collective-permute-start.25
  530.0 8.6 collective-permute-start.26
  636.3 19.4 %collective-permute-start.31 = (f32[96,256]{1,0:T(8,128)}, f32[96,256]{1,0:T(8,128)S(1)}, u32[]{:S(2)}, u32[]{:S(2)}) collective-permute-start(f32[96,256]{1,0:T(8,128)} %get-tuple-element.35), channel_id=1, source_target_pairs={{0,2},{1,3},{2,4},{3,5},{4,6},{5,7},{6,8},{7,9},{8,10},{9,11},{10,... | collective-permute-start | bytes 294920 | tf_op jit(solution)/shard_map/ppermute | solution.py:18
  640.9 16.4 %collective-permute-start.30 = (f32[96,256]{1,0:T(8,128)}, f32[96,256]{1,0:T(8,128)S(1)}, u32[]{:S(2)}, u32[]{:S(2)}) collective-permute-start(f32[96,256]{1,0:T(8,128)} %get-tuple-element.36), channel_id=1, source_target_pairs={{2,0},{3,1},{4,2},{5,3},{6,4},{7,5},{8,6},{9,7},{10,8},{11,9},{12,... | collective-permute-start | bytes 294920 | tf_op jit(solution)/shard_map/ppermute | solution.py:18
  642.2 16.7 %collective-permute-start.29 = (f32[96,256]{1,0:T(8,128)S(1)}, f32[96,256]{1,0:T(8,128)}, u32[]{:S(2)}, u32[]{:S(2)}) collective-permute-start(f32[96,256]{1,0:T(8,128)S(1)} %get-tuple-element.37), channel_id=1, source_target_pairs={{0,1},{1,2},{2,3},{3,4},{4,5},{5,6},{6,7},{7,8},{8,9},{9,10},{10,1... | collective-permute-start | bytes 294920 | tf_op jit(solution)/shard_map/ppermute | solution.py:18
  650.5 9.5 collective-permute-start.28
  672.4 12.8 %collective-permute-start.32 = (f32[96,256]{0,1:T(8,128)S(1)}, f32[96,256]{0,1:T(8,128)S(1)}, u32[]{:S(2)}, u32[]{:S(2)}) collective-permute-start(f32[96,256]{0,1:T(8,128)S(1)} %bitcast.342), channel_id=1, source_target_pairs={{0,1},{1,2},{2,3},{3,4},{4,5},{5,6},{6,7},{7,8},{8,9},{9,10},{10,1... | collective-permute-start | bytes 294920 | tf_op jit(solution)/shard_map/ppermute | solution.py:18
  676.0 9.2 collective-permute-start.33
  816.1 126.7 %collective-permute-start.36 = (f32[3,256]{0,1:T(8,128)S(1)}, f32[3,256]{0,1:T(8,128)S(1)}, u32[]{:S(2)}, u32[]{:S(2)}) collective-permute-start(f32[3,256]{0,1:T(8,128)S(1)} %get-tuple-element.32), channel_id=1, source_target_pairs={{1,0},{2,1},{3,2},{4,3},{5,4},{6,5},{7,6},{8,7},{9,8},{10,9},{11,1... | collective-permute-start | bytes 9224 | tf_op jit(solution)/shard_map/ppermute | solution.py:18
  819.0 125.9 %collective-permute-start.37 = (f32[3,256]{0,1:T(8,128)S(1)}, f32[3,256]{0,1:T(8,128)S(1)}, u32[]{:S(2)}, u32[]{:S(2)}) collective-permute-start(f32[3,256]{0,1:T(8,128)S(1)} %get-tuple-element.31), channel_id=1, source_target_pairs={{0,1},{1,2},{2,3},{3,4},{4,5},{5,6},{6,7},{7,8},{8,9},{9,10},{10,1... | collective-permute-start | bytes 9224 | tf_op jit(solution)/shard_map/ppermute | solution.py:18
  821.7 125.2 %collective-permute-start.38 = (f32[3,256]{0,1:T(8,128)S(1)}, f32[3,256]{0,1:T(8,128)S(1)}, u32[]{:S(2)}, u32[]{:S(2)}) collective-permute-start(f32[3,256]{0,1:T(8,128)S(1)} %get-tuple-element.30), channel_id=1, source_target_pairs={{2,0},{3,1},{4,2},{5,3},{6,4},{7,5},{8,6},{9,7},{10,8},{11,9},{12,... | collective-permute-start | bytes 9224 | tf_op jit(solution)/shard_map/ppermute | solution.py:18
  823.0 126.0 %collective-permute-start.39 = (f32[3,256]{0,1:T(8,128)S(1)}, f32[3,256]{0,1:T(8,128)S(1)}, u32[]{:S(2)}, u32[]{:S(2)}) collective-permute-start(f32[3,256]{0,1:T(8,128)S(1)} %get-tuple-element.29), channel_id=1, source_target_pairs={{0,2},{1,3},{2,4},{3,5},{4,6},{5,7},{6,8},{7,9},{8,10},{9,11},{10,... | collective-permute-start | bytes 9224 | tf_op jit(solution)/shard_map/ppermute | solution.py:18
  (87 other events, 1999.3 us)
where the time goes:
time: 964 us; the launch traced here: 953 us
  matrix products  376 us (39%)
  local copies, waits for them, and re-layouts  178 us (18%)
  starting transfers between devices  137 us (14%)
  other arithmetic  122 us (13%)
  blocking collectives  110 us (11%)
  waiting for transfers between devices  24.8 us (3%)
    dot_general x31, matrix products, matmul(): jnp.dot(left, right, precision=lax.Precision.HIGHEST, preferred_element_t...  212 us
    dot_general x4, matrix products, update_latent(): lax.dot_general(table_in, incidence, (((1,), (1,)), ((), ())), precision=...  164 us
    ppermute x40, starting transfers between devices, shifted(): return lax.ppermute(shard, axis, pairs)  137 us
    psum x1, blocking collectives, per_device(): energy_total = lax.psum(energy_local, 'brick')  110 us
    scatter-add x2, other arithmetic, per_device(): grad_table = jnp.zeros((3, table_rows), jnp.float32).at[:, first_ids].add...  67.5 us
    scatter-add x20, other arithmetic, return_in(): summed = summed.at[:, send_list[group_index]].add(arrived[group_index])  42.5 us
    gather x1, local copies, waits for them, and re-layouts, per_device(): species_first = species[first_ids]  38.6 us
    gather x1, local copies, waits for them, and re-layouts, per_device(): species_second = table_species[second_ids]  34.3 us
  transfers between devices with their start and end apart: 40, of which 8 were waited for; matrix products, arithmetic and copies ran while one was open for 8% of the time, Pallas kernels for 0%

commit v1 on v0

v1 whole, which is shorter than its diff:
```python
import math

import jax
import jax.numpy as jnp
import numpy as np
from jax import lax
from jax.experimental import pallas as pl
from jax.experimental.pallas import tpu as pltpu
from jax.sharding import PartitionSpec as P

F32 = jnp.float32
BF16 = jnp.bfloat16

CUTOFF = 6.0
SOFTENING = 0.25
ENV_SCALE = 0.25
PAIR_SHIFT = 1.0

LAT = 64
CH = 32
NB = 8
VEC = 3 * CH
OWN = 512
GHOST = 256
ROWS = OWN + 4 * GHOST
WIN = 256
BRICK_BLOCKS = 48
PAIRS = BRICK_BLOCKS * 128
CHUNK = 512
CHUNKS = PAIRS // CHUNK

VMEM_LIMIT = 56 * 1024 * 1024


def fit_trig():
    r = np.cos(np.linspace(0.0, np.pi, 4001)) * 0.5
    x = r * r
    base = np.polynomial.chebyshev.Chebyshev
    safe = np.where(r == 0.0, 1.0, r)
    sine = np.where(r == 0.0, 2 * np.pi, np.sin(2 * np.pi * safe) / safe)
    s = base.fit(x, sine, 8, domain=[0.0, 0.25]).convert(kind=np.polynomial.Polynomial)
    c = base.fit(x, np.cos(2 * np.pi * r), 8, domain=[0.0, 0.25]).convert(kind=np.polynomial.Polynomial)
    return [float(v) for v in s.coef], [float(v) for v in c.coef]


SIN_COEF, COS_COEF = fit_trig()


def horner(coef, x):
    out = jnp.full_like(x, coef[-1])
    for c in coef[-2::-1]:
        out = out * x + c
    return out


def dot(a, b):
    return lax.dot_general(a, b, (((1,), (0,)), ((), ())), preferred_element_type=F32)


def dot_nt(a, b):
    return lax.dot_general(a, b, (((1,), (1,)), ((), ())), preferred_element_type=F32)


def split2(x):
    hi = x.astype(BF16)
    lo = (x - hi.astype(F32)).astype(BF16)
    return hi, lo


def split3(x):
    hi = x.astype(BF16).astype(F32)
    rest = x - hi
    mid = rest.astype(BF16).astype(F32)
    return hi, mid, (rest - mid)


def stack2(x):
    hi, lo = split2(x)
    return jnp.concatenate([hi, lo], axis=0)


def weight3(w):
    hi, lo = split2(w)
    return jnp.concatenate([hi.astype(F32), hi.astype(F32), lo.astype(F32)], axis=1).astype(BF16)


def dense(w3, x):
    hi, lo = split2(x)
    return dot(w3, jnp.concatenate([hi, lo, hi], axis=0))


def sigmoid(x):
    return 1.0 / (1.0 + jnp.exp(-x))


def silu_and_slope(x):
    s = sigmoid(x)
    y = x * s
    return y, s + y * (1.0 - s)


def hot(ids, start, rows):
    at = lax.broadcasted_iota(jnp.int32, (rows, ids.shape[1]), 0)
    return jnp.where(at == ids - start, 1.0, 0.0)


def hot_first(first):
    return hot(first, 0, OWN).astype(BF16)


def incidence(first, second):
    own = hot(first, 0, OWN) - hot(second, 0, OWN)
    return jnp.concatenate([own.astype(BF16), (-hot(second, OWN, 4 * GHOST)).astype(BF16)], axis=0)


def fold2(x):
    half = x.shape[0] // 2
    return x[:half] + x[half:]


def radial(dist):
    k = (lax.broadcasted_iota(jnp.int32, (NB, dist.shape[1]), 0) + 1).astype(F32)
    turns = k * (dist * (1.0 / (2.0 * CUTOFF)))
    r = turns - jnp.round(turns)
    x = r * r
    return r * horner(SIN_COEF, x), horner(COS_COEF, x), k * (math.pi / CUTOFF)


def lanes(c):
    return pl.ds(pl.multiple_of(c * CHUNK, CHUNK), CHUNK)


def ids_of(ref, c):
    return ref[0:1, lanes(c)]


def gap_vectors(table_ref, oh):
    return fold2(dot(table_ref[...], oh))


def weigh(geo, values):
    return jnp.concatenate([geo[m : m + 1] * values for m in range(3)], axis=0)


def project(geo, vectors):
    return (
        geo[0:1] * vectors[:CH]
        + geo[1:2] * vectors[CH : 2 * CH]
        + geo[2:3] * vectors[2 * CH :]
    )


def put_rows(rows, n):
    at = lax.broadcasted_iota(jnp.int32, (8, n), 0)
    out = jnp.zeros((8, n), F32)
    for i, row in enumerate(rows):
        out = jnp.where(at == i, row, out)
    return out


def dir_grad(dq, vectors):
    return [jnp.sum(dq * vectors[m * CH : (m + 1) * CH], axis=0, keepdims=True) for m in range(3)]


def fill_table(table_ref, own_ref, ghost_refs):
    hi, lo = split2(own_ref[...])
    table_ref[:VEC, :OWN] = hi
    table_ref[VEC:, :OWN] = lo
    for m, ghost in enumerate(ghost_refs):
        hi, lo = split2(ghost[...])
        at = OWN + m * GHOST
        table_ref[:VEC, at : at + GHOST] = hi
        table_ref[VEC:, at : at + GHOST] = lo


def emit(acc_ref, own_out, ghost_outs):
    own_out[...] = acc_ref[:, :OWN]
    for m, out in enumerate(ghost_outs):
        at = OWN + m * GHOST
        out[...] = acc_ref[:, at : at + GHOST]


def send_kernel(pos_ref, spec_ref, send_ref, m0, m1, m2, m3, ohs_ref):
    oh = jnp.concatenate([hot(send_ref[m : m + 1, :], 0, OWN).astype(BF16) for m in range(4)], axis=1)
    ohs_ref[...] = oh
    hi, mid, lo = split3(pos_ref[...])
    rows = jnp.concatenate(
        [
            put_rows([hi[i : i + 1] for i in range(3)] + [spec_ref[...].astype(F32)], OWN),
            put_rows([mid[i : i + 1] for i in range(3)], OWN),
            put_rows([lo[i : i + 1] for i in range(3)], OWN),
            jnp.zeros((8, OWN), F32),
        ],
        axis=0,
    ).astype(BF16)
    got = dot(rows, oh)
    got = got[0:8] + got[8:16] + got[16:24]
    for m, out in enumerate((m0, m1, m2, m3)):
        out[...] = got[:, m * GHOST : (m + 1) * GHOST]


def weights_kernel(
    w_radial, w_first, w_second, w_value, w_env, w_latent, w_tensor, w_mix, w_read, embed, evl, tens, mix, read, read_t,
    mix_t, lt_t, val_t, env_t, rad_t,
):
    def parts(w):
        hi, lo = split2(w)
        return hi.astype(F32), lo.astype(F32)

    rh, rl = parts(w_radial[...])
    fh, fl = parts(w_first[...])
    sh, sl = parts(w_second[...])
    embed[...] = jnp.concatenate([rh, rh, rl, fh, sh, fl, sl, jnp.zeros_like(rh)], axis=1).astype(BF16)
    for l in range(2):
        evl[l] = weight3(jnp.concatenate([w_env[l], w_value[l], w_latent[l]], axis=0))
        tens[l] = weight3(w_tensor[l])
        mix[l] = weight3(w_mix[l])
        mix_t[l] = weight3(w_mix[l].T)
        lt_t[l] = weight3(jnp.concatenate([w_latent[l].T, w_tensor[l].T], axis=0))
        val_t[l] = weight3(w_value[l].T)
        env_t[l] = weight3(w_env[l].T)
    read[...] = weight3(w_read[...])
    read_t[...] = weight3(w_read[...].T)
    rad_t[...] = weight3(w_radial[...].T)


def embed_kernel(
    live_ref, pos_ref, spec_ref, c0, c1, c2, c3, first_ref, second_ref, valid_ref, w_embed, w_evl,
    geo_out, slope_out, lat_out, evh_out, own_out, g0, g1, g2, g3, atoms_ref, acc_ref,
):
    def put(at, width, coords):
        hi, mid, lo = split3(coords)
        atoms_ref[:, at : at + width] = jnp.concatenate([hi, mid, lo, jnp.zeros_like(hi)], axis=0).astype(BF16)

    put(0, OWN, put_rows([pos_ref[i : i + 1, :] for i in range(3)] + [spec_ref[...].astype(F32)], OWN))
    for m, c in enumerate((c0, c1, c2, c3)):
        put(OWN + m * GHOST, GHOST, c[...])
    acc_ref[...] = jnp.zeros_like(acc_ref)

    def body(c, carry):
        at = lanes(c)
        first, second = first_ref[0:1, at], second_ref[0:1, at]
        mask = valid_ref[0:1, at].astype(F32)
        hf = hot(first, 0, OWN)
        hs = hot(second, 0, OWN)
        ghost = hot(second, OWN, 4 * GHOST).astype(BF16)
        oh = jnp.concatenate([(hf - hs).astype(BF16), -ghost], axis=0)
        a = dot(atoms_ref[:, :OWN], hf.astype(BF16))
        b = dot(atoms_ref[...], jnp.concatenate([hs.astype(BF16), ghost], axis=0))
        a = a[0:8] + a[8:16] + a[16:24]
        b = b[0:8] + b[8:16] + b[16:24]
        row = lax.broadcasted_iota(jnp.int32, (8, CHUNK), 0)
        diff = jnp.where(row < 3, b - a, 0.0)
        sq = jnp.sum(diff * diff, axis=0, keepdims=True) + SOFTENING
        dist = jnp.sqrt(sq)
        inv = 1.0 / dist
        shrink = 1.0 - sq * (1.0 / CUTOFF**2)
        env = shrink * shrink
        direction = diff * inv
        weight = env * mask
        geo = direction + jnp.where(row == 3, weight, 0.0) + jnp.where(row == 4, dist, 0.0)
        geo = geo + jnp.where(row == 5, mask, 0.0)
        geo_out[:, at] = geo
        sines, _, _ = radial(dist)
        basis = sines * (inv * env)
        bh = basis.astype(BF16).astype(F32)
        bl = basis - bh
        rowf = row.astype(F32)
        sf = jnp.where(rowf == a[3:4], 1.0, 0.0)
        ss = jnp.where(rowf == b[3:4], 1.0, 0.0)
        pre = dot(
            w_embed[...],
            jnp.concatenate([bh, bl, bh, sf, ss, sf, ss, jnp.zeros_like(bh)], axis=0).astype(BF16),
        )
        lat, slope = silu_and_slope(pre)
        slope_out[:, at] = slope
        lat_out[:, at] = lat
        evh = dense(w_evl[0], lat)
        evh_out[:, at] = evh
        vec = weigh(geo, evh[:CH] * weight)
        acc_ref[...] += fold2(dot_nt(stack2(vec), oh))
        return carry

    lax.fori_loop(0, live_ref[0, 0], body, 0)
    emit(acc_ref, own_out, (g0, g1, g2, g3))


def combine_kernel(own_ref, r0, r1, r2, r3, ohs_ref, own_out, g0, g1, g2, g3):
    arrived = jnp.concatenate([r[...] for r in (r0, r1, r2, r3)], axis=1)
    owned = own_ref[...] + fold2(dot_nt(stack2(arrived), ohs_ref[...]))
    own_out[...] = owned
    ghosts = fold2(dot(stack2(owned), ohs_ref[...]))
    for m, out in enumerate((g0, g1, g2, g3)):
        out[...] = ghosts[:, m * GHOST : (m + 1) * GHOST]


def middle_kernel(
    live_ref, own_ref, t0, t1, t2, t3, first_ref, second_ref, geo_ref, lat_ref, evh_ref, w_evl, w_tens, w_mix,
    gap_out, hid_out, lat_out, evh_out, own_out, g0, g1, g2, g3, table_ref, acc_ref,
):
    fill_table(table_ref, own_ref, (t0, t1, t2, t3))
    acc_ref[...] = jnp.zeros_like(acc_ref)

    def body(c, carry):
        at = lanes(c)
        oh = incidence(first_ref[0:1, at], second_ref[0:1, at])
        gap = gap_vectors(table_ref, oh)
        gap_out[:, at] = gap
        geo = geo_ref[:, at]
        scalars = (ENV_SCALE * evh_ref[CH : 2 * CH, at]) * project(geo, gap)
        hid = evh_ref[2 * CH :, at] + dense(w_tens[0], scalars)
        hid_out[:, at] = hid
        lat = lat_ref[:, at] + dense(w_mix[0], hid * sigmoid(hid))
        lat_out[:, at] = lat
        evh = dense(w_evl[1], lat)
        evh_out[:, at] = evh
        vec = weigh(geo, evh[:CH] * geo[3:4])
        acc_ref[...] += fold2(dot_nt(stack2(vec), oh))
        return carry

    lax.fori_loop(0, live_ref[0, 0], body, 0)
    emit(acc_ref, own_out, (g0, g1, g2, g3))


def update_back(geo, gap, values, hid_slope, dlat, w_mix_t, w_lt_t, w_val_t):
    dhid = dense(w_mix_t, dlat) * hid_slope
    both = dense(w_lt_t, dhid)
    dscal = both[LAT:] * ENV_SCALE
    dval = project(geo, gap) * dscal
    dq = values * dscal
    return dlat + both[:LAT] + dense(w_val_t, dval), dq


def turn_kernel(
    live_ref, own_ref, t0, t1, t2, t3, first_ref, second_ref, geo_ref, lat_ref, evh_ref, read_vec, w_tens, w_mix, w_read,
    w_read_t, w_mix_t, w_lt_t, w_val_t,
    energy_out, dlat_out, dgeo_out, own_out, g0, g1, g2, g3, table_ref, acc_ref,
):
    fill_table(table_ref, own_ref, (t0, t1, t2, t3))
    acc_ref[...] = jnp.zeros_like(acc_ref)
    rv = read_vec[...]

    def body(c, energy):
        at = lanes(c)
        oh = incidence(first_ref[0:1, at], second_ref[0:1, at])
        gap = gap_vectors(table_ref, oh)
        geo = geo_ref[:, at]
        weight = geo[3:4]
        values = evh_ref[CH : 2 * CH, at]
        scalars = (ENV_SCALE * values) * project(geo, gap)
        hid = evh_ref[2 * CH :, at] + dense(w_tens[1], scalars)
        act, hid_slope = silu_and_slope(hid)
        lat = lat_ref[:, at] + dense(w_mix[1], act)
        out, out_slope = silu_and_slope(dense(w_read[...], lat))
        pair_energy = jnp.sum(rv * out, axis=0, keepdims=True) + PAIR_SHIFT
        dlat = dense(w_read_t[...], out_slope * (rv * weight))
        dlat, dq = update_back(geo, gap, values, hid_slope, dlat, w_mix_t[1], w_lt_t[1], w_val_t[1])
        dlat_out[:, at] = dlat
        dgeo_out[:, at] = put_rows(dir_grad(dq, gap) + [pair_energy], CHUNK)
        acc_ref[...] += fold2(dot_nt(stack2(weigh(geo, dq)), oh))
        return energy + pair_energy * weight

    energy = lax.fori_loop(0, live_ref[0, 0], body, jnp.zeros((1, CHUNK), F32))
    energy_out[...] = jnp.broadcast_to(jnp.sum(energy, axis=1, keepdims=True), energy_out.shape)
    emit(acc_ref, own_out, (g0, g1, g2, g3))


def environment_back(geo, dvec, env_values, dlat, dgeo, w_env_t):
    weight = geo[3:4]
    dscaled = project(geo, dvec)
    rows = dir_grad(env_values * weight, dvec)
    rows.append(jnp.sum(env_values * dscaled, axis=0, keepdims=True))
    return dlat + dense(w_env_t, dscaled * weight), dgeo + put_rows(rows, CHUNK)


def back_kernel(
    live_ref, own_ref, t0, t1, t2, t3, first_ref, second_ref, geo_ref, evh1_ref, dlat_ref, dgeo_ref, gap_ref, hid_ref,
    evh0_ref, w_mix_t, w_lt_t, w_val_t, w_env_t,
    dlat_out, dgeo_out, own_out, g0, g1, g2, g3, table_ref, acc_ref,
):
    fill_table(table_ref, own_ref, (t0, t1, t2, t3))
    acc_ref[...] = jnp.zeros_like(acc_ref)

    def body(c, carry):
        at = lanes(c)
        oh = incidence(first_ref[0:1, at], second_ref[0:1, at])
        dvec = gap_vectors(table_ref, oh)
        geo = geo_ref[:, at]
        dlat, dgeo = environment_back(geo, dvec, evh1_ref[:CH, at], dlat_ref[:, at], dgeo_ref[:, at], w_env_t[1])
        gap = gap_ref[:, at]
        _, hid_slope = silu_and_slope(hid_ref[:, at])
        dlat, dq = update_back(geo, gap, evh0_ref[CH : 2 * CH, at], hid_slope, dlat, w_mix_t[0], w_lt_t[0], w_val_t[0])
        dlat_out[:, at] = dlat
        dgeo_out[:, at] = dgeo + put_rows(dir_grad(dq, gap), CHUNK)
        acc_ref[...] += fold2(dot_nt(stack2(weigh(geo, dq)), oh))
        return carry

    lax.fori_loop(0, live_ref[0, 0], body, 0)
    emit(acc_ref, own_out, (g0, g1, g2, g3))


def force_kernel(
    live_ref, own_ref, t0, t1, t2, t3, first_ref, second_ref, geo_ref, evh0_ref, dlat_ref, dgeo_ref, slope_ref,
    w_env_t, w_rad_t,
    own_out, g0, g1, g2, g3, table_ref, acc_ref,
):
    fill_table(table_ref, own_ref, (t0, t1, t2, t3))
    acc_ref[...] = jnp.zeros_like(acc_ref)

    def body(c, carry):
        at = lanes(c)
        oh = incidence(first_ref[0:1, at], second_ref[0:1, at])
        dvec = gap_vectors(table_ref, oh)
        geo = geo_ref[:, at]
        dlat, dgeo = environment_back(geo, dvec, evh0_ref[:CH, at], dlat_ref[:, at], dgeo_ref[:, at], w_env_t[0])
        dbasis = dense(w_rad_t[...], dlat * slope_ref[:, at])
        dist, mask = geo[4:5], geo[5:6]
        inv = 1.0 / dist
        shrink = 1.0 - dist * dist * (1.0 / CUTOFF**2)
        env = shrink * shrink
        sines, cosines, freq = radial(dist)
        along = jnp.sum(dbasis * sines, axis=0, keepdims=True) * inv
        ddist = (jnp.sum(dbasis * (freq * cosines), axis=0, keepdims=True) - along) * (inv * env)
        denv = along + mask * dgeo[3:4]
        ddist = ddist - denv * shrink * dist * (4.0 / CUTOFF**2)
        row = lax.broadcasted_iota(jnp.int32, (8, CHUNK), 0)
        unit = jnp.where(row < 3, geo, 0.0)
        dunit = jnp.where(row < 3, dgeo, 0.0)
        radial_part = ddist - jnp.sum(unit * dunit, axis=0, keepdims=True) * inv
        ddiff = dunit * inv + unit * radial_part
        hi = ddiff.astype(BF16).astype(F32)
        both = jnp.concatenate([hi, ddiff - hi], axis=0).astype(BF16)
        acc_ref[...] += fold2(dot_nt(both, oh))
        return carry

    lax.fori_loop(0, live_ref[0, 0], body, 0)
    emit(acc_ref, own_out, (g0, g1, g2, g3))


def final_kernel(own_ref, r0, r1, r2, r3, ohs_ref, out_ref):
    arrived = jnp.concatenate([r[...] for r in (r0, r1, r2, r3)], axis=1)
    hi, mid, lo = split3(arrived)
    parts = jnp.concatenate([hi, mid, lo, jnp.zeros_like(hi)], axis=0).astype(BF16)
    got = dot_nt(parts, ohs_ref[...])
    out_ref[...] = (own_ref[...] + got[0:8] + got[8:16] + got[16:24])[0:3]


def call(kernel, outs, *args, scratch=(), smem=0):
    vmem = pl.BlockSpec(memory_space=pltpu.VMEM)
    specs = [pl.BlockSpec(memory_space=pltpu.SMEM)] * smem + [vmem] * (len(args) - smem)
    return pl.pallas_call(
        kernel,
        out_shape=[jax.ShapeDtypeStruct(s, d) for s, d in outs],
        in_specs=specs,
        out_specs=[vmem] * len(outs),
        scratch_shapes=[pltpu.VMEM(s, d) for s, d in scratch],
        compiler_params=pltpu.CompilerParams(vmem_limit_bytes=VMEM_LIMIT),
    )(*args)


def matching(m, count):
    pairs = []
    for i in range(count):
        j = (i ^ 1, ((i + 1) ^ 1) - 1, i ^ 2, ((i + 2) ^ 2) - 2)[m]
        if 0 <= j < count:
            pairs.append((i, j))
    return pairs


def swap(blocks):
    count = lax.axis_size("brick")
    return [lax.ppermute(block, "brick", matching(m, count)) for m, block in enumerate(blocks)]


def total_of(value):
    count = lax.axis_size("brick")
    step = 1
    while step < count:
        value = value + lax.ppermute(value, "brick", [(i, i ^ step) for i in range(count)])
        step *= 2
    return value


def per_device(
    positions, species, pair_first, pair_second, pair_valid, send_list, w_radial, w_first, w_second, w_value, w_env,
    w_latent, w_tensor, w_mix, w_read, read_vec,
):
    brick = lax.axis_index("brick")
    flip_near = brick & 1
    flip_far = (brick >> 1) & 1
    send = jnp.concatenate(
        [
            jnp.where(flip_near == 1, send_list[1::-1], send_list[0:2]),
            jnp.where(flip_far == 1, send_list[3:1:-1], send_list[2:4]),
        ],
        axis=0,
    )
    spec = species[None, :]
    first = pair_first.reshape(1, PAIRS)
    second = pair_second.reshape(1, PAIRS)
    valid = pair_valid.reshape(1, PAIRS)
    slot = second - OWN
    group = slot // GHOST
    group = group ^ jnp.where(group < 2, 1 - flip_near, 1 - flip_far)
    second = jnp.where(second < OWN, second, OWN + group * GHOST + slot % GHOST)
    live_blocks = jnp.sum(pair_valid[:, 0])
    live = ((live_blocks * 128 + CHUNK - 1) // CHUNK).reshape(1, 1)

    message = ((8, GHOST), F32)
    *messages, ohs = call(send_kernel, [message] * 4 + [((OWN, 4 * GHOST), BF16)], positions, spec, send)
    coords = swap(messages)
    embed, evl, tens, mix, read, read_t, mix_t, lt_t, val_t, env_t, rad_t = call(
        weights_kernel,
        [
            (s, BF16)
            for s in (
                (LAT, 64), (2, 2 * CH + LAT, 3 * LAT), (2, LAT, 3 * CH), (2, LAT, 3 * LAT), (LAT, 3 * LAT), (LAT, 3 * LAT),
                (2, LAT, 3 * LAT), (2, LAT + CH, 3 * LAT), (2, LAT, 3 * CH), (2, LAT, 3 * CH), (NB, 3 * LAT),
            )
        ],
        w_radial, w_first, w_second, w_value, w_env, w_latent, w_tensor, w_mix, w_read,
    )

    def rows(n):
        return ((n, PAIRS), F32)

    partials = [((VEC, OWN), F32)] + [((VEC, GHOST), F32)] * 4
    scratch = [((2 * VEC, ROWS), BF16), ((VEC, ROWS), F32)]

    def complete(own, ghosts):
        own, *listed = call(combine_kernel, partials, own, *swap(ghosts), ohs)
        return [own] + swap(listed)

    geo, slope, lat0, evh0, own, *ghosts = call(
        embed_kernel,
        [rows(8), rows(LAT), rows(LAT), rows(2 * CH + LAT)] + partials,
        live, positions, spec, *coords, first, second, valid, embed, evl,
        scratch=[((32, ROWS), BF16), ((VEC, ROWS), F32)],
        smem=1,
    )
    table = complete(own, ghosts)
    gap0, hid0, lat1, evh1, own, *ghosts = call(
        middle_kernel,
        [rows(VEC), rows(LAT), rows(LAT), rows(2 * CH + LAT)] + partials,
        live, *table, first, second, geo, lat0, evh0, evl, tens, mix,
        scratch=scratch, smem=1,
    )
    table = complete(own, ghosts)
    energy, dlat, dgeo, own, *ghosts = call(
        turn_kernel,
        [((8, 128), F32), rows(LAT), rows(8)] + partials,
        live, *table, first, second, geo, lat1, evh1, read_vec[:, None], tens, mix, read, read_t, mix_t, lt_t, val_t,
        scratch=scratch, smem=1,
    )
    table = complete(own, ghosts)
    dlat, dgeo, own, *ghosts = call(
        back_kernel,
        [rows(LAT), rows(8)] + partials,
        live, *table, first, second, geo, evh1, dlat, dgeo, gap0, hid0, evh0, mix_t, lt_t, val_t, env_t,
        scratch=scratch, smem=1,
    )
    table = complete(own, ghosts)
    own, *ghosts = call(
        force_kernel,
        [((8, OWN), F32)] + [((8, GHOST), F32)] * 4,
        live, *table, first, second, geo, evh0, dlat, dgeo, slope, env_t, rad_t,
        scratch=[scratch[0], ((8, ROWS), F32)], smem=1,
    )
    (forces,) = call(final_kernel, [((3, OWN), F32)], own, *swap(ghosts), ohs)
    total = total_of(energy)
    return (forces, total[0, 0] / (lax.axis_size("brick") * PAIRS))


def solution(mesh):
    line = P("brick", None)
    return jax.shard_map(
        per_device,
        mesh=mesh,
        in_specs=(P(None, "brick"), P("brick"), line, line, line, line) + (P(),) * 10,
        out_specs=(P(None, "brick"), P()),
        check_vma=False,
    )
```

time: 964 us -> 342 us (0.35); the launches traced: 953 us -> 343 us
  matrix products: 376 us -> 0 us
  local copies, waits for them, and re-layouts: 178 us -> 14.3 us
  other arithmetic: 122 us -> 4.35 us
  blocking collectives: 110 us -> 0 us
  Pallas kernels: 0 us -> 102 us
  starting transfers between devices: 137 us -> 201 us
    dot_general x35 -> x0, matrix products: 376 us -> none  [the longest x31 212 us: matmul(): jnp.dot(left, right, precision=lax.Precision.HIGHEST, preferred_element_t...]
    gather x26 -> x0, local copies, waits for them, and re-layouts: 140 us -> none  [the longest x1 38.6 us: per_device(): species_first = species[first_ids]]
    psum x1 -> x0, blocking collectives: 110 us -> none  [per_device(): energy_total = lax.psum(energy_local, 'brick')]
    scatter-add x22 -> x0, other arithmetic: 110 us -> none  [the longest x2 67.5 us: per_device(): grad_table = jnp.zeros((3, table_rows), jnp.float32).at[:, first_ids].add...]
    pallas_call x0 -> x12, Pallas kernels: none -> 102 us  [call(): pl.pallas_call(kernel, out_shape=[jax.ShapeDtypeStruct(s, d) for s, d in...]
    ppermute x40 -> x47, starting transfers between devices: 137 us -> 201 us  [the longest x7 101 us: total_of(): lax.ppermute(value, 'brick', [(i, i ^ step) for i in range(count)])]
    ppermute x20 -> x0, local copies, waits for them, and re-layouts: 18.8 us -> none  [shifted(): return lax.ppermute(shard, axis, pairs)]
    ppermute x40 -> x47, waiting for transfers between devices: 24.8 us -> 18.2 us  [the longest x40 11.6 us: swap(): lax.ppermute(block, 'brick', matching(m, count))]
  transfers between devices with their start and end apart: 40 -> 47, of which waited for: 8 -> 13; matrix products, arithmetic and copies ran while one was open for 8% -> 3% of each run, Pallas kernels for 0% -> 4%
where the time goes in v1:
time: 342 us; the launch traced here: 343 us
  starting transfers between devices  201 us (59%)
  Pallas kernels  102 us (30%)
  waiting for transfers between devices  18.2 us (5%)
  local copies, waits for them, and re-layouts  14.3 us (4%)
  other arithmetic  4.35 us (1%)
  between operations  3.85 us (1%)
    pallas_call x12, Pallas kernels, call(): pl.pallas_call(kernel, out_shape=[jax.ShapeDtypeStruct(s, d) for s, d in...  102 us
    ppermute x7, starting transfers between devices, total_of(): lax.ppermute(value, 'brick', [(i, i ^ step) for i in range(count)])  101 us
    ppermute x40, starting transfers between devices, swap(): lax.ppermute(block, 'brick', matching(m, count))  100 us
    unnamed x88, local copies, waits for them, and re-layouts  12.2 us
    ppermute x40, waiting for transfers between devices, swap(): lax.ppermute(block, 'brick', matching(m, count))  11.6 us
  transfers between devices with their start and end apart: 47, of which 13 were waited for; matrix products, arithmetic and copies ran while one was open for 3% of the time, Pallas kernels for 4%

profile of v1, /device:TPU:1, one launch (start us, length us, event | category | flops | bytes accessed | tf_op | source)
XLA Modules:
  0.0 343.4 jit_solution(12459919937573334548)
XLA Ops:
  6.4 3.2 collective-permute-start.1
  20.8 2.1 shard_map.168
  23.6 14.4 %shard_map.169 = (f32[8,6144]{1,0:T(8,128)}, f32[64,6144]{1,0:T(8,128)}, f32[64,6144]{1,0:T(8,128)}, f32[128,6144]{1,0:T(8,128)}, f32[96,512]{1,0:T(8,128)}, /*i...) custom-call(s32[1,1]{1,0:T(1,128)} %bitcast.live_ref, f32[3,512]{1,0:T(4,128)} %pos_ref.3, ...), custom_call_target="tpu_custom_call" | custom-call | tf_op jit(solution)/shard_map/pallas_call | solution.py:451
  38.0 3.8 %collective-permute-start.5 = (f32[96,256]{1,0:T(8,128)}, f32[96,256]{1,0:T(8,128)S(1)}, u32[]{:S(2)}, u32[]{:S(2)}) collective-permute-start(f32[96,256]{1,0:T(8,128)} %get-tuple-element.84), channel_id=1, source_target_pairs={{1,2},{2,1},{3,4},{4,3},{5,6},{6,5},{7,8},{8,7},{9,10},{10,9},{11,... | collective-permute-start | bytes 294920 | tf_op jit(solution)/shard_map/ppermute | solution.py:472
  41.9 3.4 collective-permute-start.6
  48.2 3.0 shard_map.170
  51.2 7.2 %collective-permute-start.9 = (f32[96,256]{1,0:T(8,128)}, f32[96,256]{1,0:T(8,128)S(1)}, u32[]{:S(2)}, u32[]{:S(2)}) collective-permute-start(f32[96,256]{1,0:T(8,128)} %get-tuple-element.90), channel_id=1, source_target_pairs={{1,2},{2,1},{3,4},{4,3},{5,6},{6,5},{7,8},{8,7},{9,10},{10,9},{11,... | collective-permute-start | bytes 294920 | tf_op jit(solution)/shard_map/ppermute | solution.py:472
  63.7 17.5 %shard_map.171 = (f32[96,6144]{1,0:T(8,128)}, f32[64,6144]{1,0:T(8,128)}, f32[64,6144]{1,0:T(8,128)}, f32[128,6144]{1,0:T(8,128)}, f32[96,512]{1,0:T(8,128)}, /*...) custom-call(s32[1,1]{1,0:T(1,128)} %bitcast.live_ref, ...), custom_call_target="tpu_custom_call" | custom-call | tf_op jit(solution)/shard_map/pallas_call | solution.py:451
  81.4 4.7 %collective-permute-start.13 = (f32[96,256]{1,0:T(8,128)}, f32[96,256]{1,0:T(8,128)S(1)}, u32[]{:S(2)}, u32[]{:S(2)}) collective-permute-start(f32[96,256]{1,0:T(8,128)} %get-tuple-element.100), channel_id=1, source_target_pairs={{1,2},{2,1},{3,4},{4,3},{5,6},{6,5},{7,8},{8,7},{9,10},{10,9},{11,... | collective-permute-start | bytes 294920 | tf_op jit(solution)/shard_map/ppermute | solution.py:472
  86.0 6.7 %collective-permute-start.14 = (f32[96,256]{1,0:T(8,128)}, f32[96,256]{1,0:T(8,128)S(1)}, u32[]{:S(2)}, u32[]{:S(2)}) collective-permute-start(f32[96,256]{1,0:T(8,128)} %get-tuple-element.101), channel_id=1, source_target_pairs={{0,2},{1,3},{2,0},{3,1},{4,6},{5,7},{6,4},{7,5},{8,10},{9,11},{10,... | collective-permute-start | bytes 294920 | tf_op jit(solution)/shard_map/ppermute | solution.py:472
  95.6 3.0 shard_map.172
  98.7 7.3 %collective-permute-start.17 = (f32[96,256]{1,0:T(8,128)}, f32[96,256]{1,0:T(8,128)S(1)}, u32[]{:S(2)}, u32[]{:S(2)}) collective-permute-start(f32[96,256]{1,0:T(8,128)} %get-tuple-element.105), channel_id=1, source_target_pairs={{1,2},{2,1},{3,4},{4,3},{5,6},{6,5},{7,8},{8,7},{9,10},{10,9},{11,... | collective-permute-start | bytes 294920 | tf_op jit(solution)/shard_map/ppermute | solution.py:472
  111.3 19.4 %shard_map.173 = (f32[8,128]{1,0:T(8,128)}, f32[64,6144]{1,0:T(8,128)}, f32[8,6144]{1,0:T(8,128)}, f32[96,512]{1,0:T(8,128)}, f32[96,256]{1,0:T(8,128)}, /*index...) custom-call(s32[1,1]{1,0:T(1,128)} %bitcast.live_ref, f32[96,512]{1,0:T(8,128)} %get-tuple-element.103.own_ref, ...), custom_call_target="tpu_custom_call" | custom-call | tf_op jit(solution)/shard_map/pallas_call | solution.py:451
  130.8 3.8 %collective-permute-start.21 = (f32[96,256]{1,0:T(8,128)}, f32[96,256]{1,0:T(8,128)S(1)}, u32[]{:S(2)}, u32[]{:S(2)}) collective-permute-start(f32[96,256]{1,0:T(8,128)} %get-tuple-element.117), channel_id=1, source_target_pairs={{1,2},{2,1},{3,4},{4,3},{5,6},{6,5},{7,8},{8,7},{9,10},{10,9},{11,... | collective-permute-start | bytes 294920 | tf_op jit(solution)/shard_map/ppermute | solution.py:472
  134.6 8.5 %collective-permute-start.22 = (f32[96,256]{1,0:T(8,128)}, f32[96,256]{1,0:T(8,128)S(1)}, u32[]{:S(2)}, u32[]{:S(2)}) collective-permute-start(f32[96,256]{1,0:T(8,128)} %get-tuple-element.118), channel_id=1, source_target_pairs={{0,2},{1,3},{2,0},{3,1},{4,6},{5,7},{6,4},{7,5},{8,10},{9,11},{10,... | collective-permute-start | bytes 294920 | tf_op jit(solution)/shard_map/ppermute | solution.py:472
  146.0 3.0 shard_map.174
  149.0 7.1 %collective-permute-start.25 = (f32[96,256]{1,0:T(8,128)}, f32[96,256]{1,0:T(8,128)S(1)}, u32[]{:S(2)}, u32[]{:S(2)}) collective-permute-start(f32[96,256]{1,0:T(8,128)} %get-tuple-element.122), channel_id=1, source_target_pairs={{1,2},{2,1},{3,4},{4,3},{5,6},{6,5},{7,8},{8,7},{9,10},{10,9},{11,... | collective-permute-start | bytes 294920 | tf_op jit(solution)/shard_map/ppermute | solution.py:472
  161.4 18.3 %shard_map.175 = (f32[64,6144]{1,0:T(8,128)}, f32[8,6144]{1,0:T(8,128)}, f32[96,512]{1,0:T(8,128)}, f32[96,256]{1,0:T(8,128)}, f32[96,256]{1,0:T(8,128)}, /*index=5*/f32[96,256]{1,0:T(8,128)}, f32[96,256]{1,0:T(8,128)}) custom-call(s32[1,1]{1,0:T(1,128)} %bitcast.live_ref, f32[96,512]{1,0:T(8,128)} %get-tuple-element.120.own_ref, f32[96,256]{1,0:T(8,128)} %copy-done.4, ...), custom_call_target="tpu_custom_call" | custom-call | tf_op jit(solution)/shard_map/pallas_call | solution.py:451
  179.9 4.9 %collective-permute-start.29 = (f32[96,256]{1,0:T(8,128)}, f32[96,256]{1,0:T(8,128)S(1)}, u32[]{:S(2)}, u32[]{:S(2)}) collective-permute-start(f32[96,256]{1,0:T(8,128)} %get-tuple-element.132), channel_id=1, source_target_pairs={{1,2},{2,1},{3,4},{4,3},{5,6},{6,5},{7,8},{8,7},{9,10},{10,9},{11,... | collective-permute-start | bytes 294920 | tf_op jit(solution)/shard_map/ppermute | solution.py:472
  184.7 6.7 %collective-permute-start.30 = (f32[96,256]{1,0:T(8,128)}, f32[96,256]{1,0:T(8,128)S(1)}, u32[]{:S(2)}, u32[]{:S(2)}) collective-permute-start(f32[96,256]{1,0:T(8,128)} %get-tuple-element.133), channel_id=1, source_target_pairs={{0,2},{1,3},{2,0},{3,1},{4,6},{5,7},{6,4},{7,5},{8,10},{9,11},{10,... | collective-permute-start | bytes 294920 | tf_op jit(solution)/shard_map/ppermute | solution.py:472
  194.3 3.0 shard_map.176
  197.3 7.1 %collective-permute-start.33 = (f32[96,256]{1,0:T(8,128)}, f32[96,256]{1,0:T(8,128)S(1)}, u32[]{:S(2)}, u32[]{:S(2)}) collective-permute-start(f32[96,256]{1,0:T(8,128)} %get-tuple-element.137), channel_id=1, source_target_pairs={{1,2},{2,1},{3,4},{4,3},{5,6},{6,5},{7,8},{8,7},{9,10},{10,9},{11,... | collective-permute-start | bytes 294920 | tf_op jit(solution)/shard_map/ppermute | solution.py:472
  208.2 12.4 %collective-permute-start.41 = (f32[8,128]{1,0:T(8,128)S(1)}, f32[8,128]{1,0:T(8,128)S(1)}, u32[]{:S(2)}, u32[]{:S(2)}) collective-permute-start(f32[8,128]{1,0:T(8,128)S(1)} %add.83), channel_id=1, source_target_pairs={{0,2},{1,3},{2,0},{3,1},{4,6},{5,7},{6,4},{7,5},{8,10},{9,11},{10,... | collective-permute-start | bytes 12296 | tf_op jit(solution)/shard_map/ppermute | solution.py:479
  221.6 2.5 collective-permute-start.42
  225.6 13.0 %collective-permute-start.43 = (f32[8,128]{1,0:T(8,128)S(1)}, f32[8,128]{1,0:T(8,128)S(1)}, u32[]{:S(2)}, u32[]{:S(2)}) collective-permute-start(f32[8,128]{1,0:T(8,128)S(1)} %add.85), channel_id=1, source_target_pairs={{0,8},{1,9},{2,10},{3,11},{4,12},{5,13},{6,14},{7,15},{8,0},{9,1},... | collective-permute-start | bytes 12296 | tf_op jit(solution)/shard_map/ppermute | solution.py:479
  239.6 21.5 %collective-permute-start.44 = (f32[8,128]{1,0:T(8,128)S(1)}, f32[8,128]{1,0:T(8,128)S(1)}, u32[]{:S(2)}, u32[]{:S(2)}) collective-permute-start(f32[8,128]{1,0:T(8,128)S(1)} %add.86), channel_id=1, source_target_pairs={{0,16},{1,17},{2,18},{3,19},{4,20},{5,21},{6,22},{7,23},{8,24},{9,... | collective-permute-start | bytes 12296 | tf_op jit(solution)/shard_map/ppermute | solution.py:479
  262.1 17.4 %collective-permute-start.45 = (f32[8,128]{1,0:T(8,128)S(1)}, f32[8,128]{1,0:T(8,128)S(1)}, u32[]{:S(2)}, u32[]{:S(2)}) collective-permute-start(f32[8,128]{1,0:T(8,128)S(1)} %add.87), channel_id=1, source_target_pairs={{0,32},{1,33},{2,34},{3,35},{4,36},{5,37},{6,38},{7,39},{8,40},{9,... | collective-permute-start | bytes 12296 | tf_op jit(solution)/shard_map/ppermute | solution.py:479
  280.2 13.2 %shard_map.177 = (f32[8,512]{1,0:T(8,128)}, f32[8,256]{1,0:T(8,128)}, f32[8,256]{1,0:T(8,128)}, f32[8,256]{1,0:T(8,128)}, f32[8,256]{1,0:T(8,128)}) custom-call(s32[1,1]{1,0:T(1,128)} %bitcast.live_ref, f32[96,512]{1,0:T(8,128)} %get-tuple-element.135.own_ref, f32[96,256]{1,0:T(8,128)} %copy-done, f32[96,256]{1,0:T(8,128)} %copy-done.1, ...), custom_call_target="tpu_custom_call" | custom-call | tf_op jit(solution)/shard_map/pallas_call | solution.py:451
  294.5 5.1 %collective-permute-start.37 = (f32[8,256]{1,0:T(8,128)}, f32[8,256]{1,0:T(8,128)S(1)}, u32[]{:S(2)}, u32[]{:S(2)}) collective-permute-start(f32[8,256]{1,0:T(8,128)} %get-tuple-element.146), channel_id=1, source_target_pairs={{1,2},{2,1},{3,4},{4,3},{5,6},{6,5},{7,8},{8,7},{9,10},{10,9},{11,... | collective-permute-start | bytes 24584 | tf_op jit(solution)/shard_map/ppermute | solution.py:472
  299.5 2.9 collective-permute-start.38
  303.1 34.1 %collective-permute-start.46 = (f32[8,128]{1,0:T(8,128)S(1)}, f32[8,128]{1,0:T(8,128)S(1)}, u32[]{:S(2)}, u32[]{:S(2)}) collective-permute-start(f32[8,128]{1,0:T(8,128)S(1)} %add.88), channel_id=1, source_target_pairs={{0,64},{1,65},{2,66},{3,67},{4,68},{5,69},{6,70},{7,71},{8,72},{9,... | collective-permute-start | bytes 12296 | tf_op jit(solution)/shard_map/ppermute | solution.py:479
  340.0 2.3 shard_map.178
  (178 shorter events, 56.9 us)
Async XLA Ops:
  5.0 17.9 %collective-permute-start = (f32[8,256]{1,0:T(8,128)}, f32[8,256]{1,0:T(8,128)S(1)}, u32[]{:S(2)}, u32[]{:S(2)}) collective-permute-start(f32[8,256]{1,0:T(8,128)} %get-tuple-element.76), channel_id=1, source_target_pairs={{0,1},{1,0},{2,3},{3,2},{4,5},{5,4},{6,7},{7,6},{8,9},{9,8},{10,11... | collective-permute-start | bytes 24584 | tf_op jit(solution)/shard_map/ppermute | solution.py:472
  6.4 16.5 %collective-permute-start.1 = (f32[8,256]{1,0:T(8,128)}, f32[8,256]{1,0:T(8,128)S(1)}, u32[]{:S(2)}, u32[]{:S(2)}) collective-permute-start(f32[8,256]{1,0:T(8,128)} %get-tuple-element.77), channel_id=1, source_target_pairs={{1,2},{2,1},{3,4},{4,3},{5,6},{6,5},{7,8},{8,7},{9,10},{10,9},{11,... | collective-permute-start | bytes 24584 | tf_op jit(solution)/shard_map/ppermute | solution.py:472
  9.6 13.4 %collective-permute-start.2 = (f32[8,256]{1,0:T(8,128)}, f32[8,256]{1,0:T(8,128)S(1)}, u32[]{:S(2)}, u32[]{:S(2)}) collective-permute-start(f32[8,256]{1,0:T(8,128)} %get-tuple-element.78), channel_id=1, source_target_pairs={{0,2},{1,3},{2,0},{3,1},{4,6},{5,7},{6,4},{7,5},{8,10},{9,11},{10,... | collective-permute-start | bytes 24584 | tf_op jit(solution)/shard_map/ppermute | solution.py:472
  11.0 12.0 %collective-permute-start.3 = (f32[8,256]{1,0:T(8,128)}, f32[8,256]{1,0:T(8,128)S(1)}, u32[]{:S(2)}, u32[]{:S(2)}) collective-permute-start(f32[8,256]{1,0:T(8,128)} %get-tuple-element.79), channel_id=1, source_target_pairs={{2,4},{3,5},{4,2},{5,3},{6,8},{7,9},{8,6},{9,7},{10,12},{11,13},{1... | collective-permute-start | bytes 24584 | tf_op jit(solution)/shard_map/ppermute | solution.py:472
  51.2 9.8 %collective-permute-start.8 = (f32[96,256]{1,0:T(8,128)}, f32[96,256]{1,0:T(8,128)S(1)}, u32[]{:S(2)}, u32[]{:S(2)}) collective-permute-start(f32[96,256]{1,0:T(8,128)} %get-tuple-element.89), channel_id=1, source_target_pairs={{0,1},{1,0},{2,3},{3,2},{4,5},{5,4},{6,7},{7,6},{8,9},{9,8},{10,11... | collective-permute-start | bytes 294920 | tf_op jit(solution)/shard_map/ppermute | solution.py:472
  51.2 9.8 %collective-permute-start.9 = (f32[96,256]{1,0:T(8,128)}, f32[96,256]{1,0:T(8,128)S(1)}, u32[]{:S(2)}, u32[]{:S(2)}) collective-permute-start(f32[96,256]{1,0:T(8,128)} %get-tuple-element.90), channel_id=1, source_target_pairs={{1,2},{2,1},{3,4},{4,3},{5,6},{6,5},{7,8},{8,7},{9,10},{10,9},{11,... | collective-permute-start | bytes 294920 | tf_op jit(solution)/shard_map/ppermute | solution.py:472
  81.3 12.1 %collective-permute-start.12 = (f32[96,256]{1,0:T(8,128)}, f32[96,256]{1,0:T(8,128)S(1)}, u32[]{:S(2)}, u32[]{:S(2)}) collective-permute-start(f32[96,256]{1,0:T(8,128)} %get-tuple-element.99), channel_id=1, source_target_pairs={{0,1},{1,0},{2,3},{3,2},{4,5},{5,4},{6,7},{7,6},{8,9},{9,8},{10,11... | collective-permute-start | bytes 294920 | tf_op jit(solution)/shard_map/ppermute | solution.py:472
  81.4 12.0 %collective-permute-start.13 = (f32[96,256]{1,0:T(8,128)}, f32[96,256]{1,0:T(8,128)S(1)}, u32[]{:S(2)}, u32[]{:S(2)}) collective-permute-start(f32[96,256]{1,0:T(8,128)} %get-tuple-element.100), channel_id=1, source_target_pairs={{1,2},{2,1},{3,4},{4,3},{5,6},{6,5},{7,8},{8,7},{9,10},{10,9},{11,... | collective-permute-start | bytes 294920 | tf_op jit(solution)/shard_map/ppermute | solution.py:472
  86.0 8.9 %collective-permute-start.14 = (f32[96,256]{1,0:T(8,128)}, f32[96,256]{1,0:T(8,128)S(1)}, u32[]{:S(2)}, u32[]{:S(2)}) collective-permute-start(f32[96,256]{1,0:T(8,128)} %get-tuple-element.101), channel_id=1, source_target_pairs={{0,2},{1,3},{2,0},{3,1},{4,6},{5,7},{6,4},{7,5},{8,10},{9,11},{10,... | collective-permute-start | bytes 294920 | tf_op jit(solution)/shard_map/ppermute | solution.py:472
  98.7 10.3 %collective-permute-start.16 = (f32[96,256]{1,0:T(8,128)}, f32[96,256]{1,0:T(8,128)S(1)}, u32[]{:S(2)}, u32[]{:S(2)}) collective-permute-start(f32[96,256]{1,0:T(8,128)} %get-tuple-element.104), channel_id=1, source_target_pairs={{0,1},{1,0},{2,3},{3,2},{4,5},{5,4},{6,7},{7,6},{8,9},{9,8},{10,11... | collective-permute-start | bytes 294920 | tf_op jit(solution)/shard_map/ppermute | solution.py:472
  98.7 10.3 %collective-permute-start.17 = (f32[96,256]{1,0:T(8,128)}, f32[96,256]{1,0:T(8,128)S(1)}, u32[]{:S(2)}, u32[]{:S(2)}) collective-permute-start(f32[96,256]{1,0:T(8,128)} %get-tuple-element.105), channel_id=1, source_target_pairs={{1,2},{2,1},{3,4},{4,3},{5,6},{6,5},{7,8},{8,7},{9,10},{10,9},{11,... | collective-permute-start | bytes 294920 | tf_op jit(solution)/shard_map/ppermute | solution.py:472
  130.7 13.1 %collective-permute-start.20 = (f32[96,256]{1,0:T(8,128)}, f32[96,256]{1,0:T(8,128)S(1)}, u32[]{:S(2)}, u32[]{:S(2)}) collective-permute-start(f32[96,256]{1,0:T(8,128)} %get-tuple-element.116), channel_id=1, source_target_pairs={{0,1},{1,0},{2,3},{3,2},{4,5},{5,4},{6,7},{7,6},{8,9},{9,8},{10,11... | collective-permute-start | bytes 294920 | tf_op jit(solution)/shard_map/ppermute | solution.py:472
  130.8 13.0 %collective-permute-start.21 = (f32[96,256]{1,0:T(8,128)}, f32[96,256]{1,0:T(8,128)S(1)}, u32[]{:S(2)}, u32[]{:S(2)}) collective-permute-start(f32[96,256]{1,0:T(8,128)} %get-tuple-element.117), channel_id=1, source_target_pairs={{1,2},{2,1},{3,4},{4,3},{5,6},{6,5},{7,8},{8,7},{9,10},{10,9},{11,... | collective-permute-start | bytes 294920 | tf_op jit(solution)/shard_map/ppermute | solution.py:472
  134.6 10.7 %collective-permute-start.22 = (f32[96,256]{1,0:T(8,128)}, f32[96,256]{1,0:T(8,128)S(1)}, u32[]{:S(2)}, u32[]{:S(2)}) collective-permute-start(f32[96,256]{1,0:T(8,128)} %get-tuple-element.118), channel_id=1, source_target_pairs={{0,2},{1,3},{2,0},{3,1},{4,6},{5,7},{6,4},{7,5},{8,10},{9,11},{10,... | collective-permute-start | bytes 294920 | tf_op jit(solution)/shard_map/ppermute | solution.py:472
  149.0 9.8 %collective-permute-start.24 = (f32[96,256]{1,0:T(8,128)}, f32[96,256]{1,0:T(8,128)S(1)}, u32[]{:S(2)}, u32[]{:S(2)}) collective-permute-start(f32[96,256]{1,0:T(8,128)} %get-tuple-element.121), channel_id=1, source_target_pairs={{0,1},{1,0},{2,3},{3,2},{4,5},{5,4},{6,7},{7,6},{8,9},{9,8},{10,11... | collective-permute-start | bytes 294920 | tf_op jit(solution)/shard_map/ppermute | solution.py:472
  149.0 9.9 %collective-permute-start.25 = (f32[96,256]{1,0:T(8,128)}, f32[96,256]{1,0:T(8,128)S(1)}, u32[]{:S(2)}, u32[]{:S(2)}) collective-permute-start(f32[96,256]{1,0:T(8,128)} %get-tuple-element.122), channel_id=1, source_target_pairs={{1,2},{2,1},{3,4},{4,3},{5,6},{6,5},{7,8},{8,7},{9,10},{10,9},{11,... | collective-permute-start | bytes 294920 | tf_op jit(solution)/shard_map/ppermute | solution.py:472
  179.8 12.3 %collective-permute-start.28 = (f32[96,256]{1,0:T(8,128)}, f32[96,256]{1,0:T(8,128)S(1)}, u32[]{:S(2)}, u32[]{:S(2)}) collective-permute-start(f32[96,256]{1,0:T(8,128)} %get-tuple-element.131), channel_id=1, source_target_pairs={{0,1},{1,0},{2,3},{3,2},{4,5},{5,4},{6,7},{7,6},{8,9},{9,8},{10,11... | collective-permute-start | bytes 294920 | tf_op jit(solution)/shard_map/ppermute | solution.py:472
  179.9 12.2 %collective-permute-start.29 = (f32[96,256]{1,0:T(8,128)}, f32[96,256]{1,0:T(8,128)S(1)}, u32[]{:S(2)}, u32[]{:S(2)}) collective-permute-start(f32[96,256]{1,0:T(8,128)} %get-tuple-element.132), channel_id=1, source_target_pairs={{1,2},{2,1},{3,4},{4,3},{5,6},{6,5},{7,8},{8,7},{9,10},{10,9},{11,... | collective-permute-start | bytes 294920 | tf_op jit(solution)/shard_map/ppermute | solution.py:472
  184.7 8.9 %collective-permute-start.30 = (f32[96,256]{1,0:T(8,128)}, f32[96,256]{1,0:T(8,128)S(1)}, u32[]{:S(2)}, u32[]{:S(2)}) collective-permute-start(f32[96,256]{1,0:T(8,128)} %get-tuple-element.133), channel_id=1, source_target_pairs={{0,2},{1,3},{2,0},{3,1},{4,6},{5,7},{6,4},{7,5},{8,10},{9,11},{10,... | collective-permute-start | bytes 294920 | tf_op jit(solution)/shard_map/ppermute | solution.py:472
  197.3 82.1 %collective-permute-start.32 = (f32[96,256]{1,0:T(8,128)}, f32[96,256]{1,0:T(8,128)S(1)}, u32[]{:S(2)}, u32[]{:S(2)}) collective-permute-start(f32[96,256]{1,0:T(8,128)} %get-tuple-element.136), channel_id=1, source_target_pairs={{0,1},{1,0},{2,3},{3,2},{4,5},{5,4},{6,7},{7,6},{8,9},{9,8},{10,11... | collective-permute-start | bytes 294920 | tf_op jit(solution)/shard_map/ppermute | solution.py:472
  197.3 82.1 %collective-permute-start.33 = (f32[96,256]{1,0:T(8,128)}, f32[96,256]{1,0:T(8,128)S(1)}, u32[]{:S(2)}, u32[]{:S(2)}) collective-permute-start(f32[96,256]{1,0:T(8,128)} %get-tuple-element.137), channel_id=1, source_target_pairs={{1,2},{2,1},{3,4},{4,3},{5,6},{6,5},{7,8},{8,7},{9,10},{10,9},{11,... | collective-permute-start | bytes 294920 | tf_op jit(solution)/shard_map/ppermute | solution.py:472
  204.5 75.0 %collective-permute-start.34 = (f32[96,256]{1,0:T(8,128)}, f32[96,256]{1,0:T(8,128)S(1)}, u32[]{:S(2)}, u32[]{:S(2)}) collective-permute-start(f32[96,256]{1,0:T(8,128)} %get-tuple-element.138), channel_id=1, source_target_pairs={{0,2},{1,3},{2,0},{3,1},{4,6},{5,7},{6,4},{7,5},{8,10},{9,11},{10,... | collective-permute-start | bytes 294920 | tf_op jit(solution)/shard_map/ppermute | solution.py:472
  206.3 73.2 %collective-permute-start.35 = (f32[96,256]{1,0:T(8,128)}, f32[96,256]{1,0:T(8,128)S(1)}, u32[]{:S(2)}, u32[]{:S(2)}) collective-permute-start(f32[96,256]{1,0:T(8,128)} %get-tuple-element.139), channel_id=1, source_target_pairs={{2,4},{3,5},{4,2},{5,3},{6,8},{7,9},{8,6},{9,7},{10,12},{11,13},{1... | collective-permute-start | bytes 294920 | tf_op jit(solution)/shard_map/ppermute | solution.py:472
  208.2 13.4 %collective-permute-start.41 = (f32[8,128]{1,0:T(8,128)S(1)}, f32[8,128]{1,0:T(8,128)S(1)}, u32[]{:S(2)}, u32[]{:S(2)}) collective-permute-start(f32[8,128]{1,0:T(8,128)S(1)} %add.83), channel_id=1, source_target_pairs={{0,2},{1,3},{2,0},{3,1},{4,6},{5,7},{6,4},{7,5},{8,10},{9,11},{10,... | collective-permute-start | bytes 12296 | tf_op jit(solution)/shard_map/ppermute | solution.py:479
  225.6 14.0 %collective-permute-start.43 = (f32[8,128]{1,0:T(8,128)S(1)}, f32[8,128]{1,0:T(8,128)S(1)}, u32[]{:S(2)}, u32[]{:S(2)}) collective-permute-start(f32[8,128]{1,0:T(8,128)S(1)} %add.85), channel_id=1, source_target_pairs={{0,8},{1,9},{2,10},{3,11},{4,12},{5,13},{6,14},{7,15},{8,0},{9,1},... | collective-permute-start | bytes 12296 | tf_op jit(solution)/shard_map/ppermute | solution.py:479
  239.6 22.5 %collective-permute-start.44 = (f32[8,128]{1,0:T(8,128)S(1)}, f32[8,128]{1,0:T(8,128)S(1)}, u32[]{:S(2)}, u32[]{:S(2)}) collective-permute-start(f32[8,128]{1,0:T(8,128)S(1)} %add.86), channel_id=1, source_target_pairs={{0,16},{1,17},{2,18},{3,19},{4,20},{5,21},{6,22},{7,23},{8,24},{9,... | collective-permute-start | bytes 12296 | tf_op jit(solution)/shard_map/ppermute | solution.py:479
  262.1 41.0 %collective-permute-start.45 = (f32[8,128]{1,0:T(8,128)S(1)}, f32[8,128]{1,0:T(8,128)S(1)}, u32[]{:S(2)}, u32[]{:S(2)}) collective-permute-start(f32[8,128]{1,0:T(8,128)S(1)} %add.87), channel_id=1, source_target_pairs={{0,32},{1,33},{2,34},{3,35},{4,36},{5,37},{6,38},{7,39},{8,40},{9,... | collective-permute-start | bytes 12296 | tf_op jit(solution)/shard_map/ppermute | solution.py:479
  293.5 45.8 %collective-permute-start.36 = (f32[8,256]{1,0:T(8,128)}, f32[8,256]{1,0:T(8,128)S(1)}, u32[]{:S(2)}, u32[]{:S(2)}) collective-permute-start(f32[8,256]{1,0:T(8,128)} %get-tuple-element.145), channel_id=1, source_target_pairs={{0,1},{1,0},{2,3},{3,2},{4,5},{5,4},{6,7},{7,6},{8,9},{9,8},{10,11... | collective-permute-start | bytes 24584 | tf_op jit(solution)/shard_map/ppermute | solution.py:472
  294.5 44.8 %collective-permute-start.37 = (f32[8,256]{1,0:T(8,128)}, f32[8,256]{1,0:T(8,128)S(1)}, u32[]{:S(2)}, u32[]{:S(2)}) collective-permute-start(f32[8,256]{1,0:T(8,128)} %get-tuple-element.146), channel_id=1, source_target_pairs={{1,2},{2,1},{3,4},{4,3},{5,6},{6,5},{7,8},{8,7},{9,10},{10,9},{11,... | collective-permute-start | bytes 24584 | tf_op jit(solution)/shard_map/ppermute | solution.py:472
  299.5 39.8 %collective-permute-start.38 = (f32[8,256]{1,0:T(8,128)}, f32[8,256]{1,0:T(8,128)S(1)}, u32[]{:S(2)}, u32[]{:S(2)}) collective-permute-start(f32[8,256]{1,0:T(8,128)} %get-tuple-element.147), channel_id=1, source_target_pairs={{0,2},{1,3},{2,0},{3,1},{4,6},{5,7},{6,4},{7,5},{8,10},{9,11},{10,... | collective-permute-start | bytes 24584 | tf_op jit(solution)/shard_map/ppermute | solution.py:472
  302.4 37.0 %collective-permute-start.39 = (f32[8,256]{1,0:T(8,128)}, f32[8,256]{1,0:T(8,128)S(1)}, u32[]{:S(2)}, u32[]{:S(2)}) collective-permute-start(f32[8,256]{1,0:T(8,128)} %get-tuple-element.148), channel_id=1, source_target_pairs={{2,4},{3,5},{4,2},{5,3},{6,8},{7,9},{8,6},{9,7},{10,12},{11,13},{1... | collective-permute-start | bytes 24584 | tf_op jit(solution)/shard_map/ppermute | solution.py:472
  303.1 35.0 %collective-permute-start.46 = (f32[8,128]{1,0:T(8,128)S(1)}, f32[8,128]{1,0:T(8,128)S(1)}, u32[]{:S(2)}, u32[]{:S(2)}) collective-permute-start(f32[8,128]{1,0:T(8,128)S(1)} %add.88), channel_id=1, source_target_pairs={{0,64},{1,65},{2,66},{3,67},{4,68},{5,69},{6,70},{7,71},{8,72},{9,... | collective-permute-start | bytes 12296 | tf_op jit(solution)/shard_map/ppermute | solution.py:479
  (57 other events, 152.1 us)

commit v2 on v1

--- a/solution.py
+++ b/solution.py
@@ -26,10 +26,11 @@
 WIN = 256
 BRICK_BLOCKS = 48
 PAIRS = BRICK_BLOCKS * 128
-CHUNK = 512
-CHUNKS = PAIRS // CHUNK
-
-VMEM_LIMIT = 56 * 1024 * 1024
+CHUNK = 2048
+CHUNK_BLOCKS = CHUNK // 128
+WIDE = 128
+
+VMEM_LIMIT = 12 * 1024 * 1024
 
 
 def fit_trig():
@@ -79,6 +80,12 @@
     return jnp.concatenate([hi, lo], axis=0)
 
 
+def spread2(x):
+    hi, lo = split2(x)
+    pad = jnp.zeros((WIDE - x.shape[0], x.shape[1]), BF16)
+    return jnp.concatenate([hi, pad, lo, pad], axis=0)
+
+
 def weight3(w):
     hi, lo = split2(w)
     return jnp.concatenate([hi.astype(F32), hi.astype(F32), lo.astype(F32)], axis=1).astype(BF16)
@@ -90,7 +97,7 @@
 
 
 def sigmoid(x):
-    return 1.0 / (1.0 + jnp.exp(-x))
+    return 0.5 * jnp.tanh(0.5 * x) + 0.5
 
 
 def silu_and_slope(x):
@@ -99,18 +106,14 @@
     return y, s + y * (1.0 - s)
 
 
-def hot(ids, start, rows):
+def hot(ids, rows):
     at = lax.broadcasted_iota(jnp.int32, (rows, ids.shape[1]), 0)
-    return jnp.where(at == ids - start, 1.0, 0.0)
-
-
-def hot_first(first):
-    return hot(first, 0, OWN).astype(BF16)
-
-
-def incidence(first, second):
-    own = hot(first, 0, OWN) - hot(second, 0, OWN)
-    return jnp.concatenate([own.astype(BF16), (-hot(second, OWN, 4 * GHOST)).astype(BF16)], axis=0)
+    return jnp.where(at == ids, 1.0, 0.0).astype(BF16)
+
+
+def window_hot(ids, window, value, at):
+    local = jnp.clip(ids - window * WIN, -1, WIN).astype(F32).astype(BF16)
+    return jnp.where(at == local, jnp.full((), value, BF16), jnp.zeros((), BF16))
 
 
 def fold2(x):
@@ -128,14 +131,6 @@
 
 def lanes(c):
     return pl.ds(pl.multiple_of(c * CHUNK, CHUNK), CHUNK)
-
-
-def ids_of(ref, c):
-    return ref[0:1, lanes(c)]
-
-
-def gap_vectors(table_ref, oh):
-    return fold2(dot(table_ref[...], oh))
 
 
 def weigh(geo, values):
@@ -173,15 +168,43 @@
         table_ref[VEC:, at : at + GHOST] = lo
 
 
+def gather(table_ref, oh):
+    return fold2(dot(table_ref[...], oh))
+
+
+def scatter(acc_ref, vectors, oh):
+    acc_ref[...] += dot_nt(oh, spread2(vectors))
+
+
 def emit(acc_ref, own_out, ghost_outs):
-    own_out[...] = acc_ref[:, :OWN]
+    rows = own_out.shape[0]
+    own_out[...] = (acc_ref[:OWN, :WIDE] + acc_ref[:OWN, WIDE:]).T[:rows]
     for m, out in enumerate(ghost_outs):
         at = OWN + m * GHOST
-        out[...] = acc_ref[:, at : at + GHOST]
-
-
-def send_kernel(pos_ref, spec_ref, send_ref, m0, m1, m2, m3, ohs_ref):
-    oh = jnp.concatenate([hot(send_ref[m : m + 1, :], 0, OWN).astype(BF16) for m in range(4)], axis=1)
+        out[...] = (acc_ref[at : at + GHOST, :WIDE] + acc_ref[at : at + GHOST, WIDE:]).T[:rows]
+
+
+def fetch(sources, targets, sems):
+    copies = [pltpu.make_async_copy(a, b, sems.at[i]) for i, (a, b) in enumerate(zip(sources, targets))]
+    for copy in copies:
+        copy.start()
+    for copy in copies:
+        copy.wait()
+
+
+def send_kernel(
+    flip_ref, pos_in, spec_in, send_in, valid_in, m0, m1, m2, m3, ohs_ref, live_ref, atoms_ref,
+    pos_ref, spec_ref, send_ref, valid_ref, sems,
+):
+    fetch((pos_in, spec_in, send_in, valid_in), (pos_ref, spec_ref, send_ref, valid_ref), sems)
+    live = jnp.sum(valid_ref[:, 0:1].astype(F32)).astype(jnp.int32)
+    live_ref[0, 0] = (live + CHUNK_BLOCKS - 1) // CHUNK_BLOCKS
+    columns = []
+    for m in range(4):
+        other = jnp.full((1, GHOST), flip_ref[0, m // 2], jnp.int32) == 1
+        ids = jnp.where(other, send_ref[m ^ 1 : (m ^ 1) + 1, :], send_ref[m : m + 1, :])
+        columns.append(hot(ids, OWN))
+    oh = jnp.concatenate(columns, axis=1)
     ohs_ref[...] = oh
     hi, mid, lo = split3(pos_ref[...])
     rows = jnp.concatenate(
@@ -193,64 +216,96 @@
         ],
         axis=0,
     ).astype(BF16)
+    atoms_ref[...] = rows
     got = dot(rows, oh)
     got = got[0:8] + got[8:16] + got[16:24]
     for m, out in enumerate((m0, m1, m2, m3)):
         out[...] = got[:, m * GHOST : (m + 1) * GHOST]
 
 
-def weights_kernel(
-    w_radial, w_first, w_second, w_value, w_env, w_latent, w_tensor, w_mix, w_read, embed, evl, tens, mix, read, read_t,
-    mix_t, lt_t, val_t, env_t, rad_t,
-):
+def prepare_kernel(
+    flip_ref, live_ref, *refs
+):
+    sources, refs = refs[:14], refs[14:]
+    oh_ref, info_ref, embed, evl, tens, mix, read, read_t, mix_t, lt_t, val_t, env_t, rad_t, column = refs[:14]
+    fetch(sources, refs[14:28], refs[28])
+    (
+        spec_ref, first_ref, second_ref, valid_ref,
+        w_radial_t, w_first_t, w_second_t, w_value, w_env, w_latent, w_tensor_t, w_mix, w_read, read_vec,
+    ) = refs[14:28]
+
     def parts(w):
         hi, lo = split2(w)
         return hi.astype(F32), lo.astype(F32)
 
-    rh, rl = parts(w_radial[...])
-    fh, fl = parts(w_first[...])
-    sh, sl = parts(w_second[...])
+    rh, rl = parts(w_radial_t[...].T)
+    fh, fl = parts(w_first_t[...].T)
+    sh, sl = parts(w_second_t[...].T)
     embed[...] = jnp.concatenate([rh, rh, rl, fh, sh, fl, sl, jnp.zeros_like(rh)], axis=1).astype(BF16)
     for l in range(2):
         evl[l] = weight3(jnp.concatenate([w_env[l], w_value[l], w_latent[l]], axis=0))
-        tens[l] = weight3(w_tensor[l])
+        tens[l] = weight3(w_tensor_t[l].T)
         mix[l] = weight3(w_mix[l])
         mix_t[l] = weight3(w_mix[l].T)
-        lt_t[l] = weight3(jnp.concatenate([w_latent[l].T, w_tensor[l].T], axis=0))
+        lt_t[l] = weight3(jnp.concatenate([w_latent[l].T, w_tensor_t[l]], axis=0))
         val_t[l] = weight3(w_value[l].T)
         env_t[l] = weight3(w_env[l].T)
     read[...] = weight3(w_read[...])
     read_t[...] = weight3(w_read[...].T)
-    rad_t[...] = weight3(w_radial[...].T)
+    rad_t[...] = weight3(w_radial_t[...])
+    diagonal = lax.broadcasted_iota(jnp.int32, (LAT, LAT), 0) == lax.broadcasted_iota(jnp.int32, (LAT, LAT), 1)
+    column[...] = jnp.sum(jnp.where(diagonal, read_vec[...], 0.0), axis=1, keepdims=True)
+
+    own_kinds = jnp.broadcast_to(spec_ref[...], (16, OWN)).astype(F32).astype(BF16)
+    span = 512
+    at = lax.broadcasted_iota(jnp.int32, (WIN, span), 0).astype(F32).astype(BF16)
+    near, far = 1 - flip_ref[0, 0], 1 - flip_ref[0, 1]
+
+    def body(c, carry):
+        blocks = [pl.ds(c * (span // 128) + i, 1) for i in range(span // 128)]
+        first = jnp.concatenate([first_ref[b, :] for b in blocks], axis=1)
+        second = jnp.concatenate([second_ref[b, :] for b in blocks], axis=1)
+        slot = second - OWN
+        group = slot >> 8
+        group = group ^ jnp.where(group < 2, near, far)
+        second = jnp.where(second < OWN, second, OWN + group * GHOST + (slot & (GHOST - 1)))
+        out = pl.ds(pl.multiple_of(c * span, span), span)
+        firsts = []
+        for w in range(ROWS // WIN):
+            tile = window_hot(second, w, -1.0, at)
+            if w < OWN // WIN:
+                firsts.append(window_hot(first, w, 1.0, at))
+                tile = tile + firsts[-1]
+            oh_ref[w * WIN : (w + 1) * WIN, out] = tile
+        info_ref[0:8, out] = dot(own_kinds, jnp.concatenate(firsts, axis=0))[0:8]
+        valid = jnp.concatenate([valid_ref[b, :] for b in blocks], axis=1).astype(F32)
+        info_ref[8:16, out] = jnp.broadcast_to(valid, (8, span))
+        return carry
+
+    lax.fori_loop(0, live_ref[0, 0] * (CHUNK // span), body, 0)
 
 
 def embed_kernel(
-    live_ref, pos_ref, spec_ref, c0, c1, c2, c3, first_ref, second_ref, valid_ref, w_embed, w_evl,
+    live_ref, own_ref, c0, c1, c2, c3, oh_ref, info_ref, w_embed, w_evl,
     geo_out, slope_out, lat_out, evh_out, own_out, g0, g1, g2, g3, atoms_ref, acc_ref,
 ):
     def put(at, width, coords):
         hi, mid, lo = split3(coords)
         atoms_ref[:, at : at + width] = jnp.concatenate([hi, mid, lo, jnp.zeros_like(hi)], axis=0).astype(BF16)
 
-    put(0, OWN, put_rows([pos_ref[i : i + 1, :] for i in range(3)] + [spec_ref[...].astype(F32)], OWN))
+    atoms_ref[:, :OWN] = own_ref[...]
     for m, c in enumerate((c0, c1, c2, c3)):
         put(OWN + m * GHOST, GHOST, c[...])
     acc_ref[...] = jnp.zeros_like(acc_ref)
 
     def body(c, carry):
         at = lanes(c)
-        first, second = first_ref[0:1, at], second_ref[0:1, at]
-        mask = valid_ref[0:1, at].astype(F32)
-        hf = hot(first, 0, OWN)
-        hs = hot(second, 0, OWN)
-        ghost = hot(second, OWN, 4 * GHOST).astype(BF16)
-        oh = jnp.concatenate([(hf - hs).astype(BF16), -ghost], axis=0)
-        a = dot(atoms_ref[:, :OWN], hf.astype(BF16))
-        b = dot(atoms_ref[...], jnp.concatenate([hs.astype(BF16), ghost], axis=0))
-        a = a[0:8] + a[8:16] + a[16:24]
-        b = b[0:8] + b[8:16] + b[16:24]
+        mask = info_ref[8:9, at]
+        oh = oh_ref[:, at]
+        gap = dot(atoms_ref[...], oh)
+        gap = gap[0:8] + gap[8:16] + gap[16:24]
         row = lax.broadcasted_iota(jnp.int32, (8, CHUNK), 0)
-        diff = jnp.where(row < 3, b - a, 0.0)
+        diff = jnp.where(row < 3, -gap, 0.0)
         sq = jnp.sum(diff * diff, axis=0, keepdims=True) + SOFTENING
         dist = jnp.sqrt(sq)
         inv = 1.0 / dist
@@ -266,8 +321,9 @@
         bh = basis.astype(BF16).astype(F32)
         bl = basis - bh
         rowf = row.astype(F32)
-        sf = jnp.where(rowf == a[3:4], 1.0, 0.0)
-        ss = jnp.where(rowf == b[3:4], 1.0, 0.0)
+        kind = info_ref[0:8, at]
+        sf = jnp.where(rowf == kind, 1.0, 0.0)
+        ss = jnp.where(rowf == kind - gap[3:4], 1.0, 0.0)
         pre = dot(
             w_embed[...],
             jnp.concatenate([bh, bl, bh, sf, ss, sf, ss, jnp.zeros_like(bh)], axis=0).astype(BF16),
@@ -277,13 +333,11 @@
         lat_out[:, at] = lat
         evh = dense(w_evl[0], lat)
         evh_out[:, at] = evh
-        vec = weigh(geo, evh[:CH] * weight)
-        acc_ref[...] += fold2(dot_nt(stack2(vec), oh))
+        scatter(acc_ref, weigh(geo, evh[:CH] * weight), oh)
         return carry
 
     lax.fori_loop(0, live_ref[0, 0], body, 0)
     emit(acc_ref, own_out, (g0, g1, g2, g3))
-
 
 def combine_kernel(own_ref, r0, r1, r2, r3, ohs_ref, own_out, g0, g1, g2, g3):
     arrived = jnp.concatenate([r[...] for r in (r0, r1, r2, r3)], axis=1)
@@ -295,7 +349,7 @@
 
 
 def middle_kernel(
-    live_ref, own_ref, t0, t1, t2, t3, first_ref, second_ref, geo_ref, lat_ref, evh_ref, w_evl, w_tens, w_mix,
+    live_ref, own_ref, t0, t1, t2, t3, oh_ref, geo_ref, lat_ref, evh_ref, w_evl, w_tens, w_mix,
     gap_out, hid_out, lat_out, evh_out, own_out, g0, g1, g2, g3, table_ref, acc_ref,
 ):
     fill_table(table_ref, own_ref, (t0, t1, t2, t3))
@@ -303,8 +357,8 @@
 
     def body(c, carry):
         at = lanes(c)
-        oh = incidence(first_ref[0:1, at], second_ref[0:1, at])
-        gap = gap_vectors(table_ref, oh)
+        oh = oh_ref[:, at]
+        gap = gather(table_ref, oh)
         gap_out[:, at] = gap
         geo = geo_ref[:, at]
         scalars = (ENV_SCALE * evh_ref[CH : 2 * CH, at]) * project(geo, gap)
@@ -315,7 +369,7 @@
         evh = dense(w_evl[1], lat)
         evh_out[:, at] = evh
         vec = weigh(geo, evh[:CH] * geo[3:4])
-        acc_ref[...] += fold2(dot_nt(stack2(vec), oh))
+        scatter(acc_ref, vec, oh)
         return carry
 
     lax.fori_loop(0, live_ref[0, 0], body, 0)
@@ -332,7 +386,7 @@
 
 
 def turn_kernel(
-    live_ref, own_ref, t0, t1, t2, t3, first_ref, second_ref, geo_ref, lat_ref, evh_ref, read_vec, w_tens, w_mix, w_read,
+    live_ref, own_ref, t0, t1, t2, t3, oh_ref, geo_ref, lat_ref, evh_ref, read_vec, w_tens, w_mix, w_read,
     w_read_t, w_mix_t, w_lt_t, w_val_t,
     energy_out, dlat_out, dgeo_out, own_out, g0, g1, g2, g3, table_ref, acc_ref,
 ):
@@ -342,8 +396,8 @@
 
     def body(c, energy):
         at = lanes(c)
-        oh = incidence(first_ref[0:1, at], second_ref[0:1, at])
-        gap = gap_vectors(table_ref, oh)
+        oh = oh_ref[:, at]
+        gap = gather(table_ref, oh)
         geo = geo_ref[:, at]
         weight = geo[3:4]
         values = evh_ref[CH : 2 * CH, at]
@@ -357,7 +411,7 @@
         dlat, dq = update_back(geo, gap, values, hid_slope, dlat, w_mix_t[1], w_lt_t[1], w_val_t[1])
         dlat_out[:, at] = dlat
         dgeo_out[:, at] = put_rows(dir_grad(dq, gap) + [pair_energy], CHUNK)
-        acc_ref[...] += fold2(dot_nt(stack2(weigh(geo, dq)), oh))
+        scatter(acc_ref, weigh(geo, dq), oh)
         return energy + pair_energy * weight
 
     energy = lax.fori_loop(0, live_ref[0, 0], body, jnp.zeros((1, CHUNK), F32))
@@ -374,7 +428,7 @@
 
 
 def back_kernel(
-    live_ref, own_ref, t0, t1, t2, t3, first_ref, second_ref, geo_ref, evh1_ref, dlat_ref, dgeo_ref, gap_ref, hid_ref,
+    live_ref, own_ref, t0, t1, t2, t3, oh_ref, geo_ref, evh1_ref, dlat_ref, dgeo_ref, gap_ref, hid_ref,
     evh0_ref, w_mix_t, w_lt_t, w_val_t, w_env_t,
     dlat_out, dgeo_out, own_out, g0, g1, g2, g3, table_ref, acc_ref,
 ):
@@ -383,8 +437,8 @@
 
     def body(c, carry):
         at = lanes(c)
-        oh = incidence(first_ref[0:1, at], second_ref[0:1, at])
-        dvec = gap_vectors(table_ref, oh)
+        oh = oh_ref[:, at]
+        dvec = gather(table_ref, oh)
         geo = geo_ref[:, at]
         dlat, dgeo = environment_back(geo, dvec, evh1_ref[:CH, at], dlat_ref[:, at], dgeo_ref[:, at], w_env_t[1])
         gap = gap_ref[:, at]
@@ -392,7 +446,7 @@
         dlat, dq = update_back(geo, gap, evh0_ref[CH : 2 * CH, at], hid_slope, dlat, w_mix_t[0], w_lt_t[0], w_val_t[0])
         dlat_out[:, at] = dlat
         dgeo_out[:, at] = dgeo + put_rows(dir_grad(dq, gap), CHUNK)
-        acc_ref[...] += fold2(dot_nt(stack2(weigh(geo, dq)), oh))
+        scatter(acc_ref, weigh(geo, dq), oh)
         return carry
 
     lax.fori_loop(0, live_ref[0, 0], body, 0)
@@ -400,7 +454,7 @@
 
 
 def force_kernel(
-    live_ref, own_ref, t0, t1, t2, t3, first_ref, second_ref, geo_ref, evh0_ref, dlat_ref, dgeo_ref, slope_ref,
+    live_ref, own_ref, t0, t1, t2, t3, oh_ref, geo_ref, evh0_ref, dlat_ref, dgeo_ref, slope_ref,
     w_env_t, w_rad_t,
     own_out, g0, g1, g2, g3, table_ref, acc_ref,
 ):
@@ -409,8 +463,8 @@
 
     def body(c, carry):
         at = lanes(c)
-        oh = incidence(first_ref[0:1, at], second_ref[0:1, at])
-        dvec = gap_vectors(table_ref, oh)
+        oh = oh_ref[:, at]
+        dvec = gather(table_ref, oh)
         geo = geo_ref[:, at]
         dlat, dgeo = environment_back(geo, dvec, evh0_ref[:CH, at], dlat_ref[:, at], dgeo_ref[:, at], w_env_t[0])
         dbasis = dense(w_rad_t[...], dlat * slope_ref[:, at])
@@ -434,7 +488,10 @@
         return carry
 
     lax.fori_loop(0, live_ref[0, 0], body, 0)
-    emit(acc_ref, own_out, (g0, g1, g2, g3))
+    own_out[...] = acc_ref[:, :OWN]
+    for m, out in enumerate((g0, g1, g2, g3)):
+        at = OWN + m * GHOST
+        out[...] = acc_ref[:, at : at + GHOST]
 
 
 def final_kernel(own_ref, r0, r1, r2, r3, ohs_ref, out_ref):
@@ -445,15 +502,21 @@
     out_ref[...] = (own_ref[...] + got[0:8] + got[8:16] + got[16:24])[0:3]
 
 
-def call(kernel, outs, *args, scratch=(), smem=0):
+def call(kernel, outs, *args, scratch=(), smem=0, fetched=0):
     vmem = pl.BlockSpec(memory_space=pltpu.VMEM)
-    specs = [pl.BlockSpec(memory_space=pltpu.SMEM)] * smem + [vmem] * (len(args) - smem)
+    scalar = pl.BlockSpec(memory_space=pltpu.SMEM)
+    anywhere = pl.BlockSpec(memory_space=pltpu.HBM)
+    held = len(args) - fetched
+    args = args[:held] + tuple(pltpu.with_memory_space_constraint(a, pltpu.HBM) for a in args[held:])
+    buffers = [pltpu.VMEM(a.shape, a.dtype) for a in args[len(args) - fetched :]]
+    if fetched:
+        buffers.append(pltpu.SemaphoreType.DMA((fetched,)))
     return pl.pallas_call(
         kernel,
         out_shape=[jax.ShapeDtypeStruct(s, d) for s, d in outs],
-        in_specs=specs,
-        out_specs=[vmem] * len(outs),
-        scratch_shapes=[pltpu.VMEM(s, d) for s, d in scratch],
+        in_specs=[scalar] * smem + [vmem] * (len(args) - smem - fetched) + [anywhere] * fetched,
+        out_specs=[scalar if d == jnp.int32 else vmem for _, d in outs],
+        scratch_shapes=buffers + [pltpu.VMEM(s, d) for s, d in scratch],
         compiler_params=pltpu.CompilerParams(vmem_limit_bytes=VMEM_LIMIT),
     )(*args)
 
@@ -467,18 +530,25 @@
     return pairs
 
 
-def swap(blocks):
+def exchange(blocks):
     count = lax.axis_size("brick")
-    return [lax.ppermute(block, "brick", matching(m, count)) for m, block in enumerate(blocks)]
-
-
-def total_of(value):
+    got = [None] * 4
+    for m in (2, 3, 1, 0):
+        got[m] = lax.ppermute(blocks[m], "brick", matching(m, count))
+    return got
+
+
+def exchange_and_add(blocks, energy, step):
+    blocks, energy = lax.optimization_barrier((blocks, energy))
+    energy = add_across(energy, step)
+    return exchange(blocks), energy
+
+
+def add_across(value, step):
     count = lax.axis_size("brick")
-    step = 1
-    while step < count:
-        value = value + lax.ppermute(value, "brick", [(i, i ^ step) for i in range(count)])
-        step *= 2
-    return value
+    if step >= count:
+        return value
+    return value + lax.ppermute(value, "brick", [(i, i ^ step) for i in range(count)])
 
 
 def per_device(
@@ -486,88 +556,89 @@
     w_latent, w_tensor, w_mix, w_read, read_vec,
 ):
     brick = lax.axis_index("brick")
-    flip_near = brick & 1
-    flip_far = (brick >> 1) & 1
-    send = jnp.concatenate(
-        [
-            jnp.where(flip_near == 1, send_list[1::-1], send_list[0:2]),
-            jnp.where(flip_far == 1, send_list[3:1:-1], send_list[2:4]),
-        ],
-        axis=0,
-    )
+    flips = jnp.stack([brick & 1, (brick >> 1) & 1]).reshape(1, 2)
     spec = species[None, :]
-    first = pair_first.reshape(1, PAIRS)
-    second = pair_second.reshape(1, PAIRS)
-    valid = pair_valid.reshape(1, PAIRS)
-    slot = second - OWN
-    group = slot // GHOST
-    group = group ^ jnp.where(group < 2, 1 - flip_near, 1 - flip_far)
-    second = jnp.where(second < OWN, second, OWN + group * GHOST + slot % GHOST)
-    live_blocks = jnp.sum(pair_valid[:, 0])
-    live = ((live_blocks * 128 + CHUNK - 1) // CHUNK).reshape(1, 1)
 
     message = ((8, GHOST), F32)
-    *messages, ohs = call(send_kernel, [message] * 4 + [((OWN, 4 * GHOST), BF16)], positions, spec, send)
-    coords = swap(messages)
-    embed, evl, tens, mix, read, read_t, mix_t, lt_t, val_t, env_t, rad_t = call(
-        weights_kernel,
-        [
-            (s, BF16)
-            for s in (
-                (LAT, 64), (2, 2 * CH + LAT, 3 * LAT), (2, LAT, 3 * CH), (2, LAT, 3 * LAT), (LAT, 3 * LAT), (LAT, 3 * LAT),
-                (2, LAT, 3 * LAT), (2, LAT + CH, 3 * LAT), (2, LAT, 3 * CH), (2, LAT, 3 * CH), (NB, 3 * LAT),
-            )
-        ],
-        w_radial, w_first, w_second, w_value, w_env, w_latent, w_tensor, w_mix, w_read,
+    *messages, ohs, live, atoms = call(
+        send_kernel,
+        [message] * 4 + [((OWN, 4 * GHOST), BF16), ((1, 1), jnp.int32), ((32, OWN), BF16)],
+        flips, positions, spec, send_list, pair_valid, smem=1, fetched=4,
+    )
+    coords = exchange(messages)
+    shapes = (
+        (LAT, 64), (2, 2 * CH + LAT, 3 * LAT), (2, LAT, 3 * CH), (2, LAT, 3 * LAT), (LAT, 3 * LAT), (LAT, 3 * LAT),
+        (2, LAT, 3 * LAT), (2, LAT + CH, 3 * LAT), (2, LAT, 3 * CH), (2, LAT, 3 * CH), (NB, 3 * LAT),
+    )
+    oh, info, embed, evl, tens, mix, read, read_t, mix_t, lt_t, val_t, env_t, rad_t, column = call(
+        prepare_kernel,
+        [((ROWS, PAIRS), BF16), ((16, PAIRS), F32)]
+        + [(s, BF16) for s in shapes]
+        + [((LAT, 1), F32)],
+        flips, live, spec, pair_first, pair_second, pair_valid, w_radial.T, w_first.T, w_second.T, w_value, w_env, w_latent,
+        jnp.swapaxes(w_tensor, 1, 2), w_mix, w_read, read_vec[None, :],
+        smem=2, fetched=14,
     )
 
     def rows(n):
         return ((n, PAIRS), F32)
 
     partials = [((VEC, OWN), F32)] + [((VEC, GHOST), F32)] * 4
-    scratch = [((2 * VEC, ROWS), BF16), ((VEC, ROWS), F32)]
+    scratch = [((2 * VEC, ROWS), BF16), ((ROWS, 2 * WIDE), F32)]
+
+    def combine(own, arrived):
+        own, *listed = call(combine_kernel, partials, own, *arrived, ohs)
+        return own, listed
 
     def complete(own, ghosts):
-        own, *listed = call(combine_kernel, partials, own, *swap(ghosts), ohs)
-        return [own] + swap(listed)
+        own, listed = combine(own, exchange(ghosts))
+        return [own] + exchange(listed)
+
+    def complete_and_add(own, ghosts, energy, steps):
+        arrived, energy = exchange_and_add(ghosts, energy, steps[0])
+        own, listed = combine(own, arrived)
+        listed, energy = exchange_and_add(listed, energy, steps[1])
+        return [own] + listed, energy
 
     geo, slope, lat0, evh0, own, *ghosts = call(
         embed_kernel,
         [rows(8), rows(LAT), rows(LAT), rows(2 * CH + LAT)] + partials,
-        live, positions, spec, *coords, first, second, valid, embed, evl,
-        scratch=[((32, ROWS), BF16), ((VEC, ROWS), F32)],
+        live, atoms, *coords, oh, info, embed, evl,
+        scratch=[((32, ROWS), BF16), scratch[1]],
         smem=1,
     )
     table = complete(own, ghosts)
     gap0, hid0, lat1, evh1, own, *ghosts = call(
         middle_kernel,
         [rows(VEC), rows(LAT), rows(LAT), rows(2 * CH + LAT)] + partials,
-        live, *table, first, second, geo, lat0, evh0, evl, tens, mix,
+        live, *table, oh, geo, lat0, evh0, evl, tens, mix,
         scratch=scratch, smem=1,
     )
     table = complete(own, ghosts)
     energy, dlat, dgeo, own, *ghosts = call(
         turn_kernel,
         [((8, 128), F32), rows(LAT), rows(8)] + partials,
-        live, *table, first, second, geo, lat1, evh1, read_vec[:, None], tens, mix, read, read_t, mix_t, lt_t, val_t,
+        live, *table, oh, geo, lat1, evh1, column, tens, mix, read, read_t, mix_t, lt_t, val_t,
         scratch=scratch, smem=1,
     )
-    table = complete(own, ghosts)
+    energy = add_across(energy, 1)
+    table, energy = complete_and_add(own, ghosts, energy, (2, 4))
     dlat, dgeo, own, *ghosts = call(
         back_kernel,
         [rows(LAT), rows(8)] + partials,
-        live, *table, first, second, geo, evh1, dlat, dgeo, gap0, hid0, evh0, mix_t, lt_t, val_t, env_t,
+        live, *table, oh, geo, evh1, dlat, dgeo, gap0, hid0, evh0, mix_t, lt_t, val_t, env_t,
         scratch=scratch, smem=1,
     )
-    table = complete(own, ghosts)
+    table, energy = complete_and_add(own, ghosts, energy, (8, 16))
     own, *ghosts = call(
         force_kernel,
         [((8, OWN), F32)] + [((8, GHOST), F32)] * 4,
-        live, *table, first, second, geo, evh0, dlat, dgeo, slope, env_t, rad_t,
+        live, *table, oh, geo, evh0, dlat, dgeo, slope, env_t, rad_t,
         scratch=[scratch[0], ((8, ROWS), F32)], smem=1,
     )
-    (forces,) = call(final_kernel, [((3, OWN), F32)], own, *swap(ghosts), ohs)
-    total = total_of(energy)
+    arrived, energy = exchange_and_add(ghosts, energy, 32)
+    (forces,) = call(final_kernel, [((3, OWN), F32)], own, *arrived, ohs)
+    total = add_across(energy, 64)
     return (forces, total[0, 0] / (lax.axis_size("brick") * PAIRS))
 
 

time: 342 us -> 235 us (0.69)
  starting transfers between devices: 201 us -> 155 us
  Pallas kernels: 102 us -> 56.6 us
  local copies, waits for them, and re-layouts: 14.3 us -> 0.51 us
  other arithmetic: 4.35 us -> 0.1 us
    ppermute x47, starting transfers between devices: 201 us -> 155 us  [the longest x7 78.5 us: add_across(): lax.ppermute(value, 'brick', [(i, i ^ step) for i in range(count)])]
    pallas_call x12, Pallas kernels: 102 us -> 56.6 us  [call(): pl.pallas_call(kernel, out_shape=[jax.ShapeDtypeStruct(s, d) for s, d in...]
    unnamed x88 -> x0, local copies, waits for them, and re-layouts: 12.2 us -> none
  transfers between devices with their start and end apart: 47 -> 47, of which waited for: 13 -> 14; matrix products, arithmetic and copies ran while one was open for 3% -> 0% of each run, Pallas kernels for 4% -> 3%
where the time goes in v2:
time: 235 us; the launch traced here: 234 us
  starting transfers between devices  155 us (66%)
  Pallas kernels  56.6 us (24%)
  waiting for transfers between devices  18.9 us (8%)
  between operations  2.88 us (1%)
    ppermute x7, starting transfers between devices, add_across(): lax.ppermute(value, 'brick', [(i, i ^ step) for i in range(count)])  78.5 us
    ppermute x40, starting transfers between devices, exchange(): got[m] = lax.ppermute(blocks[m], 'brick', matching(m, count))  77 us
    pallas_call x12, Pallas kernels, call(): pl.pallas_call(kernel, out_shape=[jax.ShapeDtypeStruct(s, d) for s, d in...  56.6 us
    ppermute x40, waiting for transfers between devices, exchange(): got[m] = lax.ppermute(blocks[m], 'brick', matching(m, count))  11.7 us
    ppermute x7, waiting for transfers between devices, add_across(): lax.ppermute(value, 'brick', [(i, i ^ step) for i in range(count)])  7.17 us
  transfers between devices with their start and end apart: 47, of which 14 were waited for; matrix products, arithmetic and copies ran while one was open for 0% of the time, Pallas kernels for 3%

profile of v2, /device:TPU:1, one launch (start us, length us, event | category | flops | bytes accessed | tf_op | source)
XLA Modules:
  0.0 234.4 jit_solution(17842365430419587116)
XLA Ops:
  0.7 2.2 shard_map.167
  2.9 1.5 collective-permute-start
  4.4 3.2 %collective-permute-start.1 = (f32[8,256]{1,0:T(8,128)S(1)}, f32[8,256]{1,0:T(8,128)S(1)}, u32[]{:S(2)}, u32[]{:S(2)}) collective-permute-start(f32[8,256]{1,0:T(8,128)S(1)} %get-tuple-element.109), channel_id=1, source_target_pairs={{1,2},{2,1},{3,4},{4,3},{5,6},{6,5},{7,8},{8,7},{9,10},{10,9},{11,... | collective-permute-start | bytes 24584 | tf_op jit(solution)/shard_map/ppermute | solution.py:537
  9.7 6.3 %shard_map.168 = (bf16[1536,6144]{1,0:T(8,128)(2,1)S(1)}, f32[16,6144]{1,0:T(8,128)S(1)}, bf16[64,64]{1,0:T(8,128)(2,1)S(1)}, bf16[2,128,192]{2,1,0:T(8,128)(2,1...) custom-call(s32[1,2]{1,0:T(1,128)S(1)} %add_bitcast_fusion.flip_ref,, ...), custom_call_target="tpu_custom_call" | custom-call | tf_op jit(solution)/shard_map/pallas_call | solution.py:514
  16.0 7.8 %shard_map.169 = (f32[8,6144]{1,0:T(8,128)S(1)}, f32[64,6144]{1,0:T(8,128)S(1)}, f32[64,6144]{1,0:T(8,128)S(1)}, f32[128,6144]{1,0:T(8,128)S(1)}, f32[96,512]{1,...) custom-call(s32[1,1]{1,0:T(1,128)} %get-tuple-element.106.live_ref, ...), custom_call_target="tpu_custom_call" | custom-call | tf_op jit(solution)/shard_map/pallas_call | solution.py:514
  23.9 5.5 %collective-permute-start.5 = (f32[96,256]{1,0:T(8,128)S(1)}, f32[96,256]{1,0:T(8,128)S(1)}, u32[]{:S(2)}, u32[]{:S(2)}) collective-permute-start(f32[96,256]{1,0:T(8,128)S(1)} %get-tuple-element.118), channel_id=1, source_target_pairs={{1,2},{2,1},{3,4},{4,3},{5,6},{6,5},{7,8},{8,7},{9,10},{10,9},{11,... | collective-permute-start | bytes 294920 | tf_op jit(solution)/shard_map/ppermute | solution.py:537
  31.8 2.2 collective-permute-done.6.r2
  35.2 5.4 %collective-permute-start.9 = (f32[96,256]{1,0:T(8,128)S(1)}, f32[96,256]{1,0:T(8,128)S(1)}, u32[]{:S(2)}, u32[]{:S(2)}) collective-permute-start(f32[96,256]{1,0:T(8,128)S(1)} %get-tuple-element.124), channel_id=1, source_target_pairs={{1,2},{2,1},{3,4},{4,3},{5,6},{6,5},{7,8},{8,7},{9,10},{10,9},{11,... | collective-permute-start | bytes 294920 | tf_op jit(solution)/shard_map/ppermute | solution.py:537
  40.7 1.6 collective-permute-start.10
  43.0 2.1 collective-permute-done.10.t2
  45.1 8.5 %shard_map.171 = (f32[96,6144]{1,0:T(8,128)S(1)}, f32[64,6144]{1,0:T(8,128)S(1)}, f32[64,6144]{1,0:T(8,128)S(1)}, f32[128,6144]{1,0:T(8,128)S(1)}, f32[96,512]{1...) custom-call(s32[1,1]{1,0:T(1,128)} %get-tuple-element.106.live_ref, ...), custom_call_target="tpu_custom_call" | custom-call | tf_op jit(solution)/shard_map/pallas_call | solution.py:514
  54.1 7.1 %collective-permute-start.13 = (f32[96,256]{1,0:T(8,128)S(1)}, f32[96,256]{1,0:T(8,128)S(1)}, u32[]{:S(2)}, u32[]{:S(2)}) collective-permute-start(f32[96,256]{1,0:T(8,128)S(1)} %get-tuple-element.134), channel_id=1, source_target_pairs={{1,2},{2,1},{3,4},{4,3},{5,6},{6,5},{7,8},{8,7},{9,10},{10,9},{11,... | collective-permute-start | bytes 294920 | tf_op jit(solution)/shard_map/ppermute | solution.py:537
  63.5 2.2 collective-permute-done.14.r2
  67.0 9.3 %collective-permute-start.17 = (f32[96,256]{1,0:T(8,128)S(1)}, f32[96,256]{1,0:T(8,128)S(1)}, u32[]{:S(2)}, u32[]{:S(2)}) collective-permute-start(f32[96,256]{1,0:T(8,128)S(1)} %get-tuple-element.139), channel_id=1, source_target_pairs={{1,2},{2,1},{3,4},{4,3},{5,6},{6,5},{7,8},{8,7},{9,10},{10,9},{11,... | collective-permute-start | bytes 294920 | tf_op jit(solution)/shard_map/ppermute | solution.py:537
  76.3 1.5 collective-permute-start.18
  78.5 2.2 collective-permute-done.18.t2
  80.7 10.5 %shard_map.173 = (f32[8,128]{1,0:T(8,128)S(1)}, f32[64,6144]{1,0:T(8,128)S(1)}, f32[8,6144]{1,0:T(8,128)S(1)}, f32[96,512]{1,0:T(8,128)S(1)}, f32[96,256]{1,0:T(...) custom-call(s32[1,1]{1,0:T(1,128)} %get-tuple-element.106.live_ref, ...), custom_call_target="tpu_custom_call" | custom-call | tf_op jit(solution)/shard_map/pallas_call | solution.py:514
  92.9 5.9 %collective-permute-start.22 = (f32[96,256]{1,0:T(8,128)S(1)}, f32[96,256]{1,0:T(8,128)S(1)}, u32[]{:S(2)}, u32[]{:S(2)}) collective-permute-start(f32[96,256]{1,0:T(8,128)S(1)} %get-tuple-element.157), channel_id=1, source_target_pairs={{1,2},{2,1},{3,4},{4,3},{5,6},{6,5},{7,8},{8,7},{9,10},{10,9},{11,... | collective-permute-start | bytes 294920 | tf_op jit(solution)/shard_map/ppermute | solution.py:537
  99.6 9.8 %collective-permute-start.25 = (f32[8,128]{1,0:T(8,128)S(1)}, f32[8,128]{1,0:T(8,128)S(1)}, u32[]{:S(2)}, u32[]{:S(2)}) collective-permute-start(f32[8,128]{1,0:T(8,128)S(1)} %add.21), channel_id=1, source_target_pairs={{0,2},{1,3},{2,0},{3,1},{4,6},{5,7},{6,4},{7,5},{8,10},{9,11},{10,... | collective-permute-start | bytes 12296 | tf_op jit(solution)/shard_map/ppermute | solution.py:551
  111.4 3.8 %collective-permute-start.27 = (f32[96,256]{1,0:T(8,128)S(1)}, f32[96,256]{1,0:T(8,128)S(1)}, u32[]{:S(2)}, u32[]{:S(2)}) collective-permute-start(f32[96,256]{1,0:T(8,128)S(1)} %get-tuple-element.167), channel_id=1, source_target_pairs={{1,2},{2,1},{3,4},{4,3},{5,6},{6,5},{7,8},{8,7},{9,10},{10,9},{11,... | collective-permute-start | bytes 294920 | tf_op jit(solution)/shard_map/ppermute | solution.py:537
  117.2 6.1 %collective-permute-start.30 = (f32[8,128]{1,0:T(8,128)S(1)}, f32[8,128]{1,0:T(8,128)S(1)}, u32[]{:S(2)}, u32[]{:S(2)}) collective-permute-start(f32[8,128]{1,0:T(8,128)S(1)} %add.22), channel_id=1, source_target_pairs={{0,4},{1,5},{2,6},{3,7},{4,0},{5,1},{6,2},{7,3},{8,12},{9,13},{10,... | collective-permute-start | bytes 12296 | tf_op jit(solution)/shard_map/ppermute | solution.py:551
  124.3 9.2 %shard_map.175 = (f32[64,6144]{1,0:T(8,128)S(1)}, f32[8,6144]{1,0:T(8,128)S(1)}, f32[96,512]{1,0:T(8,128)S(1)}, f32[96,256]{1,0:T(8,128)S(1)}, f32[96,256]{1,0:T...) custom-call(s32[1,1]{1,0:T(1,128)} %get-tuple-element.106.live_ref, f32[96,512]{1,0:T(8,128)S(1)} %get-tuple-element.160.own_ref, ...), custom_call_target="tpu_custom_call" | custom-call | tf_op jit(solution)/shard_map/pallas_call | solution.py:514
  133.6 4.5 %collective-permute-start.32 = (f32[96,256]{1,0:T(8,128)S(1)}, f32[96,256]{1,0:T(8,128)S(1)}, u32[]{:S(2)}, u32[]{:S(2)}) collective-permute-start(f32[96,256]{1,0:T(8,128)S(1)} %get-tuple-element.182), channel_id=1, source_target_pairs={{1,2},{2,1},{3,4},{4,3},{5,6},{6,5},{7,8},{8,7},{9,10},{10,9},{11,... | collective-permute-start | bytes 294920 | tf_op jit(solution)/shard_map/ppermute | solution.py:537
  139.0 7.6 %collective-permute-start.35 = (f32[8,128]{1,0:T(8,128)S(1)}, f32[8,128]{1,0:T(8,128)S(1)}, u32[]{:S(2)}, u32[]{:S(2)}) collective-permute-start(f32[8,128]{1,0:T(8,128)S(1)} %add.23), channel_id=1, source_target_pairs={{0,8},{1,9},{2,10},{3,11},{4,12},{5,13},{6,14},{7,15},{8,0},{9,1},... | collective-permute-start | bytes 12296 | tf_op jit(solution)/shard_map/ppermute | solution.py:551
  146.6 2.3 collective-permute-done.35
  151.0 7.6 %collective-permute-start.37 = (f32[96,256]{1,0:T(8,128)S(1)}, f32[96,256]{1,0:T(8,128)S(1)}, u32[]{:S(2)}, u32[]{:S(2)}) collective-permute-start(f32[96,256]{1,0:T(8,128)S(1)} %get-tuple-element.192), channel_id=1, source_target_pairs={{1,2},{2,1},{3,4},{4,3},{5,6},{6,5},{7,8},{8,7},{9,10},{10,9},{11,... | collective-permute-start | bytes 294920 | tf_op jit(solution)/shard_map/ppermute | solution.py:537
  159.4 14.3 %collective-permute-start.40 = (f32[8,128]{1,0:T(8,128)S(1)}, f32[8,128]{1,0:T(8,128)S(1)}, u32[]{:S(2)}, u32[]{:S(2)}) collective-permute-start(f32[8,128]{1,0:T(8,128)S(1)} %add.24), channel_id=1, source_target_pairs={{0,16},{1,17},{2,18},{3,19},{4,20},{5,21},{6,22},{7,23},{8,24},{9,... | collective-permute-start | bytes 12296 | tf_op jit(solution)/shard_map/ppermute | solution.py:551
  174.8 7.7 %shard_map.177 = (f32[8,512]{1,0:T(8,128)S(1)}, f32[8,256]{1,0:T(8,128)S(1)}, f32[8,256]{1,0:T(8,128)S(1)}, f32[8,256]{1,0:T(8,128)S(1)}, f32[8,256]{1,0:T(8,128)S(1)}) custom-call(s32[1,1]{1,0:T(1,128)} %get-tuple-element.106.live_ref, f32[96,512]{1,0:T(8,128)S(1)} %get-tuple-element.185.own_ref, f32[96,256]{1,0:T(8,128)S(1)} %collective-permute-done.36.t0, ...), custom_call_target="tpu_custom_call" | custom-call | tf_op jit(solution)/shard_map/pallas_call | solution.py:514
  182.5 17.2 %collective-permute-start.45 = (f32[8,128]{1,0:T(8,128)S(1)}, f32[8,128]{1,0:T(8,128)S(1)}, u32[]{:S(2)}, u32[]{:S(2)}) collective-permute-start(f32[8,128]{1,0:T(8,128)S(1)} %add.25), channel_id=1, source_target_pairs={{0,32},{1,33},{2,34},{3,35},{4,36},{5,37},{6,38},{7,39},{8,40},{9,... | collective-permute-start | bytes 12296 | tf_op jit(solution)/shard_map/ppermute | solution.py:551
  199.7 1.6 collective-permute-start.41
  201.2 4.9 %collective-permute-start.42 = (f32[8,256]{1,0:T(8,128)S(1)}, f32[8,256]{1,0:T(8,128)S(1)}, u32[]{:S(2)}, u32[]{:S(2)}) collective-permute-start(f32[8,256]{1,0:T(8,128)S(1)} %get-tuple-element.206), channel_id=1, source_target_pairs={{1,2},{2,1},{3,4},{4,3},{5,6},{6,5},{7,8},{8,7},{9,10},{10,9},{11,... | collective-permute-start | bytes 24584 | tf_op jit(solution)/shard_map/ppermute | solution.py:537
  207.0 23.0 %collective-permute-start.46 = (f32[8,128]{1,0:T(8,128)S(1)}, f32[8,128]{1,0:T(8,128)S(1)}, u32[]{:S(2)}, u32[]{:S(2)}) collective-permute-start(f32[8,128]{1,0:T(8,128)S(1)} %add.26), channel_id=1, source_target_pairs={{0,64},{1,65},{2,66},{3,67},{4,68},{5,69},{6,70},{7,71},{8,72},{9,... | collective-permute-start | bytes 12296 | tf_op jit(solution)/shard_map/ppermute | solution.py:551
  (83 shorter events, 26.9 us)
Async XLA Ops:
  2.9 13.0 %collective-permute-start = (f32[8,256]{1,0:T(8,128)S(1)}, f32[8,256]{1,0:T(8,128)S(1)}, u32[]{:S(2)}, u32[]{:S(2)}) collective-permute-start(f32[8,256]{1,0:T(8,128)S(1)} %get-tuple-element.108), channel_id=1, source_target_pairs={{0,1},{1,0},{2,3},{3,2},{4,5},{5,4},{6,7},{7,6},{8,9},{9,8},{10,11... | collective-permute-start | bytes 24584 | tf_op jit(solution)/shard_map/ppermute | solution.py:537
  4.4 11.5 %collective-permute-start.1 = (f32[8,256]{1,0:T(8,128)S(1)}, f32[8,256]{1,0:T(8,128)S(1)}, u32[]{:S(2)}, u32[]{:S(2)}) collective-permute-start(f32[8,256]{1,0:T(8,128)S(1)} %get-tuple-element.109), channel_id=1, source_target_pairs={{1,2},{2,1},{3,4},{4,3},{5,6},{6,5},{7,8},{8,7},{9,10},{10,9},{11,... | collective-permute-start | bytes 24584 | tf_op jit(solution)/shard_map/ppermute | solution.py:537
  7.6 8.3 %collective-permute-start.2 = (f32[8,256]{1,0:T(8,128)S(1)}, f32[8,256]{1,0:T(8,128)S(1)}, u32[]{:S(2)}, u32[]{:S(2)}) collective-permute-start(f32[8,256]{1,0:T(8,128)S(1)} %get-tuple-element.110), channel_id=1, source_target_pairs={{0,2},{1,3},{2,0},{3,1},{4,6},{5,7},{6,4},{7,5},{8,10},{9,11},{10,... | collective-permute-start | bytes 24584 | tf_op jit(solution)/shard_map/ppermute | solution.py:537
  34.8 8.1 %collective-permute-start.8 = (f32[96,256]{1,0:T(8,128)S(1)}, f32[96,256]{1,0:T(8,128)S(1)}, u32[]{:S(2)}, u32[]{:S(2)}) collective-permute-start(f32[96,256]{1,0:T(8,128)S(1)} %get-tuple-element.123), channel_id=1, source_target_pairs={{0,1},{1,0},{2,3},{3,2},{4,5},{5,4},{6,7},{7,6},{8,9},{9,8},{10,11... | collective-permute-start | bytes 294920 | tf_op jit(solution)/shard_map/ppermute | solution.py:537
  53.7 8.4 %collective-permute-start.12 = (f32[96,256]{1,0:T(8,128)S(1)}, f32[96,256]{1,0:T(8,128)S(1)}, u32[]{:S(2)}, u32[]{:S(2)}) collective-permute-start(f32[96,256]{1,0:T(8,128)S(1)} %get-tuple-element.133), channel_id=1, source_target_pairs={{0,1},{1,0},{2,3},{3,2},{4,5},{5,4},{6,7},{7,6},{8,9},{9,8},{10,11... | collective-permute-start | bytes 294920 | tf_op jit(solution)/shard_map/ppermute | solution.py:537
  54.1 9.4 %collective-permute-start.13 = (f32[96,256]{1,0:T(8,128)S(1)}, f32[96,256]{1,0:T(8,128)S(1)}, u32[]{:S(2)}, u32[]{:S(2)}) collective-permute-start(f32[96,256]{1,0:T(8,128)S(1)} %get-tuple-element.134), channel_id=1, source_target_pairs={{1,2},{2,1},{3,4},{4,3},{5,6},{6,5},{7,8},{8,7},{9,10},{10,9},{11,... | collective-permute-start | bytes 294920 | tf_op jit(solution)/shard_map/ppermute | solution.py:537
  66.5 11.9 %collective-permute-start.16 = (f32[96,256]{1,0:T(8,128)S(1)}, f32[96,256]{1,0:T(8,128)S(1)}, u32[]{:S(2)}, u32[]{:S(2)}) collective-permute-start(f32[96,256]{1,0:T(8,128)S(1)} %get-tuple-element.138), channel_id=1, source_target_pairs={{0,1},{1,0},{2,3},{3,2},{4,5},{5,4},{6,7},{7,6},{8,9},{9,8},{10,11... | collective-permute-start | bytes 294920 | tf_op jit(solution)/shard_map/ppermute | solution.py:537
  67.0 11.6 %collective-permute-start.17 = (f32[96,256]{1,0:T(8,128)S(1)}, f32[96,256]{1,0:T(8,128)S(1)}, u32[]{:S(2)}, u32[]{:S(2)}) collective-permute-start(f32[96,256]{1,0:T(8,128)S(1)} %get-tuple-element.139), channel_id=1, source_target_pairs={{1,2},{2,1},{3,4},{4,3},{5,6},{6,5},{7,8},{8,7},{9,10},{10,9},{11,... | collective-permute-start | bytes 294920 | tf_op jit(solution)/shard_map/ppermute | solution.py:537
  92.5 17.9 %collective-permute-start.21 = (f32[96,256]{1,0:T(8,128)S(1)}, f32[96,256]{1,0:T(8,128)S(1)}, u32[]{:S(2)}, u32[]{:S(2)}) collective-permute-start(f32[96,256]{1,0:T(8,128)S(1)} %get-tuple-element.156), channel_id=1, source_target_pairs={{0,1},{1,0},{2,3},{3,2},{4,5},{5,4},{6,7},{7,6},{8,9},{9,8},{10,11... | collective-permute-start | bytes 294920 | tf_op jit(solution)/shard_map/ppermute | solution.py:537
  92.9 17.6 %collective-permute-start.22 = (f32[96,256]{1,0:T(8,128)S(1)}, f32[96,256]{1,0:T(8,128)S(1)}, u32[]{:S(2)}, u32[]{:S(2)}) collective-permute-start(f32[96,256]{1,0:T(8,128)S(1)} %get-tuple-element.157), channel_id=1, source_target_pairs={{1,2},{2,1},{3,4},{4,3},{5,6},{6,5},{7,8},{8,7},{9,10},{10,9},{11,... | collective-permute-start | bytes 294920 | tf_op jit(solution)/shard_map/ppermute | solution.py:537
  98.8 11.6 %collective-permute-start.23 = (f32[96,256]{1,0:T(8,128)S(1)}, f32[96,256]{1,0:T(8,128)S(1)}, u32[]{:S(2)}, u32[]{:S(2)}) collective-permute-start(f32[96,256]{1,0:T(8,128)S(1)} %get-tuple-element.158), channel_id=1, source_target_pairs={{0,2},{1,3},{2,0},{3,1},{4,6},{5,7},{6,4},{7,5},{8,10},{9,11},{10,... | collective-permute-start | bytes 294920 | tf_op jit(solution)/shard_map/ppermute | solution.py:537
  98.9 11.5 %collective-permute-start.24 = (f32[96,256]{1,0:T(8,128)S(1)}, f32[96,256]{1,0:T(8,128)S(1)}, u32[]{:S(2)}, u32[]{:S(2)}) collective-permute-start(f32[96,256]{1,0:T(8,128)S(1)} %get-tuple-element.159), channel_id=1, source_target_pairs={{2,4},{3,5},{4,2},{5,3},{6,8},{7,9},{8,6},{9,7},{10,12},{11,13},{1... | collective-permute-start | bytes 294920 | tf_op jit(solution)/shard_map/ppermute | solution.py:537
  99.6 10.8 %collective-permute-start.25 = (f32[8,128]{1,0:T(8,128)S(1)}, f32[8,128]{1,0:T(8,128)S(1)}, u32[]{:S(2)}, u32[]{:S(2)}) collective-permute-start(f32[8,128]{1,0:T(8,128)S(1)} %add.21), channel_id=1, source_target_pairs={{0,2},{1,3},{2,0},{3,1},{4,6},{5,7},{6,4},{7,5},{8,10},{9,11},{10,... | collective-permute-start | bytes 12296 | tf_op jit(solution)/shard_map/ppermute | solution.py:551
  111.3 13.0 %collective-permute-start.26 = (f32[96,256]{1,0:T(8,128)S(1)}, f32[96,256]{1,0:T(8,128)S(1)}, u32[]{:S(2)}, u32[]{:S(2)}) collective-permute-start(f32[96,256]{1,0:T(8,128)S(1)} %get-tuple-element.166), channel_id=1, source_target_pairs={{0,1},{1,0},{2,3},{3,2},{4,5},{5,4},{6,7},{7,6},{8,9},{9,8},{10,11... | collective-permute-start | bytes 294920 | tf_op jit(solution)/shard_map/ppermute | solution.py:537
  111.4 12.9 %collective-permute-start.27 = (f32[96,256]{1,0:T(8,128)S(1)}, f32[96,256]{1,0:T(8,128)S(1)}, u32[]{:S(2)}, u32[]{:S(2)}) collective-permute-start(f32[96,256]{1,0:T(8,128)S(1)} %get-tuple-element.167), channel_id=1, source_target_pairs={{1,2},{2,1},{3,4},{4,3},{5,6},{6,5},{7,8},{8,7},{9,10},{10,9},{11,... | collective-permute-start | bytes 294920 | tf_op jit(solution)/shard_map/ppermute | solution.py:537
  115.1 9.2 %collective-permute-start.28 = (f32[96,256]{1,0:T(8,128)S(1)}, f32[96,256]{1,0:T(8,128)S(1)}, u32[]{:S(2)}, u32[]{:S(2)}) collective-permute-start(f32[96,256]{1,0:T(8,128)S(1)} %get-tuple-element.168), channel_id=1, source_target_pairs={{0,2},{1,3},{2,0},{3,1},{4,6},{5,7},{6,4},{7,5},{8,10},{9,11},{10,... | collective-permute-start | bytes 294920 | tf_op jit(solution)/shard_map/ppermute | solution.py:537
  133.5 15.4 %collective-permute-start.31 = (f32[96,256]{1,0:T(8,128)S(1)}, f32[96,256]{1,0:T(8,128)S(1)}, u32[]{:S(2)}, u32[]{:S(2)}) collective-permute-start(f32[96,256]{1,0:T(8,128)S(1)} %get-tuple-element.181), channel_id=1, source_target_pairs={{0,1},{1,0},{2,3},{3,2},{4,5},{5,4},{6,7},{7,6},{8,9},{9,8},{10,11... | collective-permute-start | bytes 294920 | tf_op jit(solution)/shard_map/ppermute | solution.py:537
  133.6 15.3 %collective-permute-start.32 = (f32[96,256]{1,0:T(8,128)S(1)}, f32[96,256]{1,0:T(8,128)S(1)}, u32[]{:S(2)}, u32[]{:S(2)}) collective-permute-start(f32[96,256]{1,0:T(8,128)S(1)} %get-tuple-element.182), channel_id=1, source_target_pairs={{1,2},{2,1},{3,4},{4,3},{5,6},{6,5},{7,8},{8,7},{9,10},{10,9},{11,... | collective-permute-start | bytes 294920 | tf_op jit(solution)/shard_map/ppermute | solution.py:537
  138.2 10.8 %collective-permute-start.33 = (f32[96,256]{1,0:T(8,128)S(1)}, f32[96,256]{1,0:T(8,128)S(1)}, u32[]{:S(2)}, u32[]{:S(2)}) collective-permute-start(f32[96,256]{1,0:T(8,128)S(1)} %get-tuple-element.183), channel_id=1, source_target_pairs={{0,2},{1,3},{2,0},{3,1},{4,6},{5,7},{6,4},{7,5},{8,10},{9,11},{10,... | collective-permute-start | bytes 294920 | tf_op jit(solution)/shard_map/ppermute | solution.py:537
  138.3 10.6 %collective-permute-start.34 = (f32[96,256]{1,0:T(8,128)S(1)}, f32[96,256]{1,0:T(8,128)S(1)}, u32[]{:S(2)}, u32[]{:S(2)}) collective-permute-start(f32[96,256]{1,0:T(8,128)S(1)} %get-tuple-element.184), channel_id=1, source_target_pairs={{2,4},{3,5},{4,2},{5,3},{6,8},{7,9},{8,6},{9,7},{10,12},{11,13},{1... | collective-permute-start | bytes 294920 | tf_op jit(solution)/shard_map/ppermute | solution.py:537
  139.0 9.9 %collective-permute-start.35 = (f32[8,128]{1,0:T(8,128)S(1)}, f32[8,128]{1,0:T(8,128)S(1)}, u32[]{:S(2)}, u32[]{:S(2)}) collective-permute-start(f32[8,128]{1,0:T(8,128)S(1)} %add.23), channel_id=1, source_target_pairs={{0,8},{1,9},{2,10},{3,11},{4,12},{5,13},{6,14},{7,15},{8,0},{9,1},... | collective-permute-start | bytes 12296 | tf_op jit(solution)/shard_map/ppermute | solution.py:551
  149.8 25.0 %collective-permute-start.36 = (f32[96,256]{1,0:T(8,128)S(1)}, f32[96,256]{1,0:T(8,128)S(1)}, u32[]{:S(2)}, u32[]{:S(2)}) collective-permute-start(f32[96,256]{1,0:T(8,128)S(1)} %get-tuple-element.191), channel_id=1, source_target_pairs={{0,1},{1,0},{2,3},{3,2},{4,5},{5,4},{6,7},{7,6},{8,9},{9,8},{10,11... | collective-permute-start | bytes 294920 | tf_op jit(solution)/shard_map/ppermute | solution.py:537
  151.0 23.7 %collective-permute-start.37 = (f32[96,256]{1,0:T(8,128)S(1)}, f32[96,256]{1,0:T(8,128)S(1)}, u32[]{:S(2)}, u32[]{:S(2)}) collective-permute-start(f32[96,256]{1,0:T(8,128)S(1)} %get-tuple-element.192), channel_id=1, source_target_pairs={{1,2},{2,1},{3,4},{4,3},{5,6},{6,5},{7,8},{8,7},{9,10},{10,9},{11,... | collective-permute-start | bytes 294920 | tf_op jit(solution)/shard_map/ppermute | solution.py:537
  158.7 16.1 %collective-permute-start.38 = (f32[96,256]{1,0:T(8,128)S(1)}, f32[96,256]{1,0:T(8,128)S(1)}, u32[]{:S(2)}, u32[]{:S(2)}) collective-permute-start(f32[96,256]{1,0:T(8,128)S(1)} %get-tuple-element.193), channel_id=1, source_target_pairs={{0,2},{1,3},{2,0},{3,1},{4,6},{5,7},{6,4},{7,5},{8,10},{9,11},{10,... | collective-permute-start | bytes 294920 | tf_op jit(solution)/shard_map/ppermute | solution.py:537
  158.8 16.0 %collective-permute-start.39 = (f32[96,256]{1,0:T(8,128)S(1)}, f32[96,256]{1,0:T(8,128)S(1)}, u32[]{:S(2)}, u32[]{:S(2)}) collective-permute-start(f32[96,256]{1,0:T(8,128)S(1)} %get-tuple-element.194), channel_id=1, source_target_pairs={{2,4},{3,5},{4,2},{5,3},{6,8},{7,9},{8,6},{9,7},{10,12},{11,13},{1... | collective-permute-start | bytes 294920 | tf_op jit(solution)/shard_map/ppermute | solution.py:537
  159.4 15.3 %collective-permute-start.40 = (f32[8,128]{1,0:T(8,128)S(1)}, f32[8,128]{1,0:T(8,128)S(1)}, u32[]{:S(2)}, u32[]{:S(2)}) collective-permute-start(f32[8,128]{1,0:T(8,128)S(1)} %add.24), channel_id=1, source_target_pairs={{0,16},{1,17},{2,18},{3,19},{4,20},{5,21},{6,22},{7,23},{8,24},{9,... | collective-permute-start | bytes 12296 | tf_op jit(solution)/shard_map/ppermute | solution.py:551
  182.5 24.5 %collective-permute-start.45 = (f32[8,128]{1,0:T(8,128)S(1)}, f32[8,128]{1,0:T(8,128)S(1)}, u32[]{:S(2)}, u32[]{:S(2)}) collective-permute-start(f32[8,128]{1,0:T(8,128)S(1)} %add.25), channel_id=1, source_target_pairs={{0,32},{1,33},{2,34},{3,35},{4,36},{5,37},{6,38},{7,39},{8,40},{9,... | collective-permute-start | bytes 12296 | tf_op jit(solution)/shard_map/ppermute | solution.py:551
  199.7 32.6 %collective-permute-start.41 = (f32[8,256]{1,0:T(8,128)S(1)}, f32[8,256]{1,0:T(8,128)S(1)}, u32[]{:S(2)}, u32[]{:S(2)}) collective-permute-start(f32[8,256]{1,0:T(8,128)S(1)} %get-tuple-element.205), channel_id=1, source_target_pairs={{0,1},{1,0},{2,3},{3,2},{4,5},{5,4},{6,7},{7,6},{8,9},{9,8},{10,11... | collective-permute-start | bytes 24584 | tf_op jit(solution)/shard_map/ppermute | solution.py:537
  201.2 31.0 %collective-permute-start.42 = (f32[8,256]{1,0:T(8,128)S(1)}, f32[8,256]{1,0:T(8,128)S(1)}, u32[]{:S(2)}, u32[]{:S(2)}) collective-permute-start(f32[8,256]{1,0:T(8,128)S(1)} %get-tuple-element.206), channel_id=1, source_target_pairs={{1,2},{2,1},{3,4},{4,3},{5,6},{6,5},{7,8},{8,7},{9,10},{10,9},{11,... | collective-permute-start | bytes 24584 | tf_op jit(solution)/shard_map/ppermute | solution.py:537
  206.2 26.1 %collective-permute-start.43 = (f32[8,256]{1,0:T(8,128)S(1)}, f32[8,256]{1,0:T(8,128)S(1)}, u32[]{:S(2)}, u32[]{:S(2)}) collective-permute-start(f32[8,256]{1,0:T(8,128)S(1)} %get-tuple-element.207), channel_id=1, source_target_pairs={{0,2},{1,3},{2,0},{3,1},{4,6},{5,7},{6,4},{7,5},{8,10},{9,11},{10,... | collective-permute-start | bytes 24584 | tf_op jit(solution)/shard_map/ppermute | solution.py:537
  206.4 25.9 %collective-permute-start.44 = (f32[8,256]{1,0:T(8,128)S(1)}, f32[8,256]{1,0:T(8,128)S(1)}, u32[]{:S(2)}, u32[]{:S(2)}) collective-permute-start(f32[8,256]{1,0:T(8,128)S(1)} %get-tuple-element.208), channel_id=1, source_target_pairs={{2,4},{3,5},{4,2},{5,3},{6,8},{7,9},{8,6},{9,7},{10,12},{11,13},{1... | collective-permute-start | bytes 24584 | tf_op jit(solution)/shard_map/ppermute | solution.py:537
  207.0 24.0 %collective-permute-start.46 = (f32[8,128]{1,0:T(8,128)S(1)}, f32[8,128]{1,0:T(8,128)S(1)}, u32[]{:S(2)}, u32[]{:S(2)}) collective-permute-start(f32[8,128]{1,0:T(8,128)S(1)} %add.26), channel_id=1, source_target_pairs={{0,64},{1,65},{2,66},{3,67},{4,68},{5,69},{6,70},{7,71},{8,72},{9,... | collective-permute-start | bytes 12296 | tf_op jit(solution)/shard_map/ppermute | solution.py:551
  (15 other events, 77.4 us)

commit v3 on v2

--- a/solution.py
+++ b/solution.py
@@ -10,6 +10,7 @@
 
 F32 = jnp.float32
 BF16 = jnp.bfloat16
+ID = jnp.int32
 
 CUTOFF = 6.0
 SOFTENING = 0.25
@@ -30,7 +31,7 @@
 CHUNK_BLOCKS = CHUNK // 128
 WIDE = 128
 
-VMEM_LIMIT = 12 * 1024 * 1024
+VMEM_LIMIT = 7 * 1024 * 1024
 
 
 def fit_trig():
@@ -157,31 +158,33 @@
     return [jnp.sum(dq * vectors[m * CH : (m + 1) * CH], axis=0, keepdims=True) for m in range(3)]
 
 
-def fill_table(table_ref, own_ref, ghost_refs):
-    hi, lo = split2(own_ref[...])
-    table_ref[:VEC, :OWN] = hi
-    table_ref[VEC:, :OWN] = lo
+def fill_table(table_ref, ghost_refs):
     for m, ghost in enumerate(ghost_refs):
         hi, lo = split2(ghost[...])
-        at = OWN + m * GHOST
+        at = m * GHOST
         table_ref[:VEC, at : at + GHOST] = hi
         table_ref[VEC:, at : at + GHOST] = lo
 
 
-def gather(table_ref, oh):
-    return fold2(dot(table_ref[...], oh))
-
-
-def scatter(acc_ref, vectors, oh):
-    acc_ref[...] += dot_nt(oh, spread2(vectors))
-
-
-def emit(acc_ref, own_out, ghost_outs):
-    rows = own_out.shape[0]
-    own_out[...] = (acc_ref[:OWN, :WIDE] + acc_ref[:OWN, WIDE:]).T[:rows]
+def gather_ghosts(own_gap_ref, table_ref, oh_ref, at):
+    return own_gap_ref[:, at] + fold2(dot(table_ref[...], oh_ref[OWN:, at]))
+
+
+def scatter_ghosts(acc_ref, parts_out, parts, oh_ref, at):
+    parts_out[:, at] = parts
+    acc_ref[...] += dot_nt(oh_ref[OWN:, at], parts)
+
+
+def emit(acc_ref, ghost_outs):
     for m, out in enumerate(ghost_outs):
-        at = OWN + m * GHOST
-        out[...] = (acc_ref[at : at + GHOST, :WIDE] + acc_ref[at : at + GHOST, WIDE:]).T[:rows]
+        out[...] = join_parts(acc_ref[m * GHOST : (m + 1) * GHOST, :], out.shape[0])
+
+
+def join_parts(acc, rows):
+    if acc.shape[1] == WIDE:
+        turned = acc.T
+        return turned[:rows] + turned[rows : 2 * rows]
+    return (acc[:, :WIDE] + acc[:, WIDE:]).T[:rows]
 
 
 def fetch(sources, targets, sems):
@@ -206,18 +209,10 @@
         columns.append(hot(ids, OWN))
     oh = jnp.concatenate(columns, axis=1)
     ohs_ref[...] = oh
-    hi, mid, lo = split3(pos_ref[...])
-    rows = jnp.concatenate(
-        [
-            put_rows([hi[i : i + 1] for i in range(3)] + [spec_ref[...].astype(F32)], OWN),
-            put_rows([mid[i : i + 1] for i in range(3)], OWN),
-            put_rows([lo[i : i + 1] for i in range(3)], OWN),
-            jnp.zeros((8, OWN), F32),
-        ],
-        axis=0,
-    ).astype(BF16)
-    atoms_ref[...] = rows
-    got = dot(rows, oh)
+    atoms = put_rows([pos_ref[i : i + 1, :] for i in range(3)] + [spec_ref[...].astype(F32)], OWN)
+    atoms_ref[...] = atoms
+    hi, mid, lo = split3(atoms)
+    got = dot(jnp.concatenate([hi, mid, lo, jnp.zeros_like(hi)], axis=0).astype(BF16), oh)
     got = got[0:8] + got[8:16] + got[16:24]
     for m, out in enumerate((m0, m1, m2, m3)):
         out[...] = got[:, m * GHOST : (m + 1) * GHOST]
@@ -226,13 +221,13 @@
 def prepare_kernel(
     flip_ref, live_ref, *refs
 ):
-    sources, refs = refs[:14], refs[14:]
-    oh_ref, info_ref, embed, evl, tens, mix, read, read_t, mix_t, lt_t, val_t, env_t, rad_t, column = refs[:14]
-    fetch(sources, refs[14:28], refs[28])
+    sources, refs = refs[:13], refs[13:]
+    oh_ref, ids_ref, mask_ref, embed, evl, tens, mix, read, read_t, mix_t, lt_t, val_t, env_t, rad_t, column = refs[:15]
+    fetch(sources, refs[15:28], refs[28])
     (
-        spec_ref, first_ref, second_ref, valid_ref,
+        first_ref, second_ref, valid_ref,
         w_radial_t, w_first_t, w_second_t, w_value, w_env, w_latent, w_tensor_t, w_mix, w_read, read_vec,
-    ) = refs[14:28]
+    ) = refs[15:28]
 
     def parts(w):
         hi, lo = split2(w)
@@ -256,74 +251,98 @@
     diagonal = lax.broadcasted_iota(jnp.int32, (LAT, LAT), 0) == lax.broadcasted_iota(jnp.int32, (LAT, LAT), 1)
     column[...] = jnp.sum(jnp.where(diagonal, read_vec[...], 0.0), axis=1, keepdims=True)
 
-    own_kinds = jnp.broadcast_to(spec_ref[...], (16, OWN)).astype(F32).astype(BF16)
+    near, far = 1 - flip_ref[0, 0], 1 - flip_ref[0, 1]
+    slot = second_ref[...] - OWN
+    group = slot >> 8
+    group = group ^ jnp.where(group < 2, near, far)
+    ids_ref[0] = first_ref[...]
+    ids_ref[1] = jnp.where(slot < 0, second_ref[...], OWN + group * GHOST + (slot & (GHOST - 1)))
+    mask_ref[...] = valid_ref[...].astype(F32)
     span = 512
     at = lax.broadcasted_iota(jnp.int32, (WIN, span), 0).astype(F32).astype(BF16)
-    near, far = 1 - flip_ref[0, 0], 1 - flip_ref[0, 1]
 
     def body(c, carry):
         blocks = [pl.ds(c * (span // 128) + i, 1) for i in range(span // 128)]
-        first = jnp.concatenate([first_ref[b, :] for b in blocks], axis=1)
-        second = jnp.concatenate([second_ref[b, :] for b in blocks], axis=1)
-        slot = second - OWN
-        group = slot >> 8
-        group = group ^ jnp.where(group < 2, near, far)
-        second = jnp.where(second < OWN, second, OWN + group * GHOST + (slot & (GHOST - 1)))
+        first = jnp.concatenate([ids_ref[0, b, :] for b in blocks], axis=1)
+        second = jnp.concatenate([ids_ref[1, b, :] for b in blocks], axis=1)
         out = pl.ds(pl.multiple_of(c * span, span), span)
-        firsts = []
         for w in range(ROWS // WIN):
             tile = window_hot(second, w, -1.0, at)
             if w < OWN // WIN:
-                firsts.append(window_hot(first, w, 1.0, at))
-                tile = tile + firsts[-1]
+                tile = tile + window_hot(first, w, 1.0, at)
             oh_ref[w * WIN : (w + 1) * WIN, out] = tile
-        info_ref[0:8, out] = dot(own_kinds, jnp.concatenate(firsts, axis=0))[0:8]
-        valid = jnp.concatenate([valid_ref[b, :] for b in blocks], axis=1).astype(F32)
-        info_ref[8:16, out] = jnp.broadcast_to(valid, (8, span))
         return carry
 
     lax.fori_loop(0, live_ref[0, 0] * (CHUNK // span), body, 0)
 
 
-def embed_kernel(
-    live_ref, own_ref, c0, c1, c2, c3, oh_ref, info_ref, w_embed, w_evl,
-    geo_out, slope_out, lat_out, evh_out, own_out, g0, g1, g2, g3, atoms_ref, acc_ref,
-):
-    def put(at, width, coords):
-        hi, mid, lo = split3(coords)
-        atoms_ref[:, at : at + width] = jnp.concatenate([hi, mid, lo, jnp.zeros_like(hi)], axis=0).astype(BF16)
-
-    atoms_ref[:, :OWN] = own_ref[...]
-    for m, c in enumerate((c0, c1, c2, c3)):
-        put(OWN + m * GHOST, GHOST, c[...])
-    acc_ref[...] = jnp.zeros_like(acc_ref)
+def own_gather_kernel(live_ref, own_ref, oh_ref, gap_out):
+    table = stack2(own_ref[...])
 
     def body(c, carry):
         at = lanes(c)
-        mask = info_ref[8:9, at]
-        oh = oh_ref[:, at]
-        gap = dot(atoms_ref[...], oh)
-        gap = gap[0:8] + gap[8:16] + gap[16:24]
-        row = lax.broadcasted_iota(jnp.int32, (8, CHUNK), 0)
-        diff = jnp.where(row < 3, -gap, 0.0)
-        sq = jnp.sum(diff * diff, axis=0, keepdims=True) + SOFTENING
-        dist = jnp.sqrt(sq)
-        inv = 1.0 / dist
-        shrink = 1.0 - sq * (1.0 / CUTOFF**2)
-        env = shrink * shrink
-        direction = diff * inv
-        weight = env * mask
-        geo = direction + jnp.where(row == 3, weight, 0.0) + jnp.where(row == 4, dist, 0.0)
-        geo = geo + jnp.where(row == 5, mask, 0.0)
-        geo_out[:, at] = geo
-        sines, _, _ = radial(dist)
-        basis = sines * (inv * env)
+        gap_out[:, at] = fold2(dot(table, oh_ref[:OWN, at]))
+        return carry
+
+    lax.fori_loop(0, live_ref[0, 0], body, 0)
+
+
+def own_scatter_kernel(live_ref, parts_ref, oh_ref, own_out, acc_ref):
+    acc_ref[...] = jnp.zeros_like(acc_ref)
+
+    def body(c, carry):
+        at = lanes(c)
+        acc_ref[...] += dot_nt(oh_ref[:OWN, at], parts_ref[:, at])
+        return carry
+
+    lax.fori_loop(0, live_ref[0, 0], body, 0)
+    own_out[...] = join_parts(acc_ref[...], own_out.shape[0])
+
+
+def embed_kernel(
+    live_ref, own_ref, c0, c1, c2, c3, ids_ref, mask_ref, oh_ref, w_embed, w_evl,
+    geo_out, slope_out, lat_out, evh_out, parts_out, g0, g1, g2, g3, acc_ref,
+):
+    tables = [(own_ref, w * 128) for w in range(OWN // 128)]
+    tables += [(c, w * 128) for c in (c0, c1, c2, c3) for w in range(GHOST // 128)]
+
+    def pick(ids, count):
+        block, place = ids >> 7, ids & 127
+        found = [jnp.zeros(ids.shape, F32)] * 4
+        for w, (ref, at) in enumerate(tables[:count]):
+            here = block == w
+            for k in range(4):
+                row = jnp.broadcast_to(ref[k : k + 1, at : at + 128], ids.shape)
+                value = jnp.take_along_axis(row, place, axis=1, mode="promise_in_bounds")
+                found[k] = jnp.where(here, value, found[k])
+        return found
+
+    one = pick(ids_ref[0], OWN // 128)
+    two = pick(ids_ref[1], ROWS // 128)
+    mask = mask_ref[...]
+    diff = [two[k] - one[k] for k in range(3)]
+    sq = diff[0] * diff[0] + diff[1] * diff[1] + diff[2] * diff[2] + SOFTENING
+    dist = jnp.sqrt(sq)
+    inv = 1.0 / dist
+    shrink = 1.0 - sq * (1.0 / CUTOFF**2)
+    env = shrink * shrink
+    columns = [d * inv for d in diff] + [env * mask, dist, mask, env * inv, one[3] + 8.0 * two[3]]
+    for b in range(BRICK_BLOCKS):
+        geo_out[:, b * 128 : (b + 1) * 128] = jnp.concatenate([column[b : b + 1] for column in columns], axis=0)
+    acc_ref[...] = jnp.zeros_like(acc_ref)
+
+    def body(c, carry):
+        at = lanes(c)
+        geo = geo_out[:, at]
+        sines, _, _ = radial(geo[4:5])
+        basis = sines * geo[6:7]
         bh = basis.astype(BF16).astype(F32)
         bl = basis - bh
-        rowf = row.astype(F32)
-        kind = info_ref[0:8, at]
-        sf = jnp.where(rowf == kind, 1.0, 0.0)
-        ss = jnp.where(rowf == kind - gap[3:4], 1.0, 0.0)
+        row = lax.broadcasted_iota(jnp.int32, (8, CHUNK), 0).astype(F32)
+        code = geo[7:8]
+        other = jnp.floor(code * 0.125)
+        sf = jnp.where(row == code - 8.0 * other, 1.0, 0.0)
+        ss = jnp.where(row == other, 1.0, 0.0)
         pre = dot(
             w_embed[...],
             jnp.concatenate([bh, bl, bh, sf, ss, sf, ss, jnp.zeros_like(bh)], axis=0).astype(BF16),
@@ -333,11 +352,12 @@
         lat_out[:, at] = lat
         evh = dense(w_evl[0], lat)
         evh_out[:, at] = evh
-        scatter(acc_ref, weigh(geo, evh[:CH] * weight), oh)
+        scatter_ghosts(acc_ref, parts_out, spread2(weigh(geo, evh[:CH] * geo[3:4])), oh_ref, at)
         return carry
 
     lax.fori_loop(0, live_ref[0, 0], body, 0)
-    emit(acc_ref, own_out, (g0, g1, g2, g3))
+    emit(acc_ref, (g0, g1, g2, g3))
+
 
 def combine_kernel(own_ref, r0, r1, r2, r3, ohs_ref, own_out, g0, g1, g2, g3):
     arrived = jnp.concatenate([r[...] for r in (r0, r1, r2, r3)], axis=1)
@@ -349,16 +369,15 @@
 
 
 def middle_kernel(
-    live_ref, own_ref, t0, t1, t2, t3, oh_ref, geo_ref, lat_ref, evh_ref, w_evl, w_tens, w_mix,
-    gap_out, hid_out, lat_out, evh_out, own_out, g0, g1, g2, g3, table_ref, acc_ref,
-):
-    fill_table(table_ref, own_ref, (t0, t1, t2, t3))
+    live_ref, own_gap_ref, t0, t1, t2, t3, oh_ref, geo_ref, lat_ref, evh_ref, w_evl, w_tens, w_mix,
+    gap_out, hid_out, lat_out, evh_out, parts_out, g0, g1, g2, g3, table_ref, acc_ref,
+):
+    fill_table(table_ref, (t0, t1, t2, t3))
     acc_ref[...] = jnp.zeros_like(acc_ref)
 
     def body(c, carry):
         at = lanes(c)
-        oh = oh_ref[:, at]
-        gap = gather(table_ref, oh)
+        gap = gather_ghosts(own_gap_ref, table_ref, oh_ref, at)
         gap_out[:, at] = gap
         geo = geo_ref[:, at]
         scalars = (ENV_SCALE * evh_ref[CH : 2 * CH, at]) * project(geo, gap)
@@ -369,11 +388,11 @@
         evh = dense(w_evl[1], lat)
         evh_out[:, at] = evh
         vec = weigh(geo, evh[:CH] * geo[3:4])
-        scatter(acc_ref, vec, oh)
+        scatter_ghosts(acc_ref, parts_out, spread2(vec), oh_ref, at)
         return carry
 
     lax.fori_loop(0, live_ref[0, 0], body, 0)
-    emit(acc_ref, own_out, (g0, g1, g2, g3))
+    emit(acc_ref, (g0, g1, g2, g3))
 
 
 def update_back(geo, gap, values, hid_slope, dlat, w_mix_t, w_lt_t, w_val_t):
@@ -386,18 +405,17 @@
 
 
 def turn_kernel(
-    live_ref, own_ref, t0, t1, t2, t3, oh_ref, geo_ref, lat_ref, evh_ref, read_vec, w_tens, w_mix, w_read,
+    live_ref, own_gap_ref, t0, t1, t2, t3, oh_ref, geo_ref, lat_ref, evh_ref, read_vec, w_tens, w_mix, w_read,
     w_read_t, w_mix_t, w_lt_t, w_val_t,
-    energy_out, dlat_out, dgeo_out, own_out, g0, g1, g2, g3, table_ref, acc_ref,
-):
-    fill_table(table_ref, own_ref, (t0, t1, t2, t3))
+    energy_out, dlat_out, dgeo_out, parts_out, g0, g1, g2, g3, table_ref, acc_ref,
+):
+    fill_table(table_ref, (t0, t1, t2, t3))
     acc_ref[...] = jnp.zeros_like(acc_ref)
     rv = read_vec[...]
 
     def body(c, energy):
         at = lanes(c)
-        oh = oh_ref[:, at]
-        gap = gather(table_ref, oh)
+        gap = gather_ghosts(own_gap_ref, table_ref, oh_ref, at)
         geo = geo_ref[:, at]
         weight = geo[3:4]
         values = evh_ref[CH : 2 * CH, at]
@@ -411,12 +429,12 @@
         dlat, dq = update_back(geo, gap, values, hid_slope, dlat, w_mix_t[1], w_lt_t[1], w_val_t[1])
         dlat_out[:, at] = dlat
         dgeo_out[:, at] = put_rows(dir_grad(dq, gap) + [pair_energy], CHUNK)
-        scatter(acc_ref, weigh(geo, dq), oh)
+        scatter_ghosts(acc_ref, parts_out, spread2(weigh(geo, dq)), oh_ref, at)
         return energy + pair_energy * weight
 
     energy = lax.fori_loop(0, live_ref[0, 0], body, jnp.zeros((1, CHUNK), F32))
     energy_out[...] = jnp.broadcast_to(jnp.sum(energy, axis=1, keepdims=True), energy_out.shape)
-    emit(acc_ref, own_out, (g0, g1, g2, g3))
+    emit(acc_ref, (g0, g1, g2, g3))
 
 
 def environment_back(geo, dvec, env_values, dlat, dgeo, w_env_t):
@@ -428,17 +446,16 @@
 
 
 def back_kernel(
-    live_ref, own_ref, t0, t1, t2, t3, oh_ref, geo_ref, evh1_ref, dlat_ref, dgeo_ref, gap_ref, hid_ref,
+    live_ref, own_gap_ref, t0, t1, t2, t3, oh_ref, geo_ref, evh1_ref, dlat_ref, dgeo_ref, gap_ref, hid_ref,
     evh0_ref, w_mix_t, w_lt_t, w_val_t, w_env_t,
-    dlat_out, dgeo_out, own_out, g0, g1, g2, g3, table_ref, acc_ref,
-):
-    fill_table(table_ref, own_ref, (t0, t1, t2, t3))
+    dlat_out, dgeo_out, parts_out, g0, g1, g2, g3, table_ref, acc_ref,
+):
+    fill_table(table_ref, (t0, t1, t2, t3))
     acc_ref[...] = jnp.zeros_like(acc_ref)
 
     def body(c, carry):
         at = lanes(c)
-        oh = oh_ref[:, at]
-        dvec = gather(table_ref, oh)
+        dvec = gather_ghosts(own_gap_ref, table_ref, oh_ref, at)
         geo = geo_ref[:, at]
         dlat, dgeo = environment_back(geo, dvec, evh1_ref[:CH, at], dlat_ref[:, at], dgeo_ref[:, at], w_env_t[1])
         gap = gap_ref[:, at]
@@ -446,25 +463,24 @@
         dlat, dq = update_back(geo, gap, evh0_ref[CH : 2 * CH, at], hid_slope, dlat, w_mix_t[0], w_lt_t[0], w_val_t[0])
         dlat_out[:, at] = dlat
         dgeo_out[:, at] = dgeo + put_rows(dir_grad(dq, gap), CHUNK)
-        scatter(acc_ref, weigh(geo, dq), oh)
+        scatter_ghosts(acc_ref, parts_out, spread2(weigh(geo, dq)), oh_ref, at)
         return carry
 
     lax.fori_loop(0, live_ref[0, 0], body, 0)
-    emit(acc_ref, own_out, (g0, g1, g2, g3))
+    emit(acc_ref, (g0, g1, g2, g3))
 
 
 def force_kernel(
-    live_ref, own_ref, t0, t1, t2, t3, oh_ref, geo_ref, evh0_ref, dlat_ref, dgeo_ref, slope_ref,
+    live_ref, own_gap_ref, t0, t1, t2, t3, oh_ref, geo_ref, evh0_ref, dlat_ref, dgeo_ref, slope_ref,
     w_env_t, w_rad_t,
-    own_out, g0, g1, g2, g3, table_ref, acc_ref,
-):
-    fill_table(table_ref, own_ref, (t0, t1, t2, t3))
+    parts_out, g0, g1, g2, g3, table_ref, acc_ref,
+):
+    fill_table(table_ref, (t0, t1, t2, t3))
     acc_ref[...] = jnp.zeros_like(acc_ref)
 
     def body(c, carry):
         at = lanes(c)
-        oh = oh_ref[:, at]
-        dvec = gather(table_ref, oh)
+        dvec = gather_ghosts(own_gap_ref, table_ref, oh_ref, at)
         geo = geo_ref[:, at]
         dlat, dgeo = environment_back(geo, dvec, evh0_ref[:CH, at], dlat_ref[:, at], dgeo_ref[:, at], w_env_t[0])
         dbasis = dense(w_rad_t[...], dlat * slope_ref[:, at])
@@ -484,14 +500,12 @@
         ddiff = dunit * inv + unit * radial_part
         hi = ddiff.astype(BF16).astype(F32)
         both = jnp.concatenate([hi, ddiff - hi], axis=0).astype(BF16)
-        acc_ref[...] += fold2(dot_nt(both, oh))
+        parts = jnp.concatenate([both, jnp.zeros((WIDE - 16, CHUNK), BF16)], axis=0)
+        scatter_ghosts(acc_ref, parts_out, parts, oh_ref, at)
         return carry
 
     lax.fori_loop(0, live_ref[0, 0], body, 0)
-    own_out[...] = acc_ref[:, :OWN]
-    for m, out in enumerate((g0, g1, g2, g3)):
-        at = OWN + m * GHOST
-        out[...] = acc_ref[:, at : at + GHOST]
+    emit(acc_ref, (g0, g1, g2, g3))
 
 
 def final_kernel(own_ref, r0, r1, r2, r3, ohs_ref, out_ref):
@@ -515,7 +529,7 @@
         kernel,
         out_shape=[jax.ShapeDtypeStruct(s, d) for s, d in outs],
         in_specs=[scalar] * smem + [vmem] * (len(args) - smem - fetched) + [anywhere] * fetched,
-        out_specs=[scalar if d == jnp.int32 else vmem for _, d in outs],
+        out_specs=[scalar if s == (1, 1) else vmem for s, _ in outs],
         scratch_shapes=buffers + [pltpu.VMEM(s, d) for s, d in scratch],
         compiler_params=pltpu.CompilerParams(vmem_limit_bytes=VMEM_LIMIT),
     )(*args)
@@ -562,7 +576,7 @@
     message = ((8, GHOST), F32)
     *messages, ohs, live, atoms = call(
         send_kernel,
-        [message] * 4 + [((OWN, 4 * GHOST), BF16), ((1, 1), jnp.int32), ((32, OWN), BF16)],
+        [message] * 4 + [((OWN, 4 * GHOST), BF16), ((1, 1), jnp.int32), ((8, OWN), F32)],
         flips, positions, spec, send_list, pair_valid, smem=1, fetched=4,
     )
     coords = exchange(messages)
@@ -570,73 +584,85 @@
         (LAT, 64), (2, 2 * CH + LAT, 3 * LAT), (2, LAT, 3 * CH), (2, LAT, 3 * LAT), (LAT, 3 * LAT), (LAT, 3 * LAT),
         (2, LAT, 3 * LAT), (2, LAT + CH, 3 * LAT), (2, LAT, 3 * CH), (2, LAT, 3 * CH), (NB, 3 * LAT),
     )
-    oh, info, embed, evl, tens, mix, read, read_t, mix_t, lt_t, val_t, env_t, rad_t, column = call(
+    oh, ids, mask, embed, evl, tens, mix, read, read_t, mix_t, lt_t, val_t, env_t, rad_t, column = call(
         prepare_kernel,
-        [((ROWS, PAIRS), BF16), ((16, PAIRS), F32)]
+        [((ROWS, PAIRS), BF16), ((2, BRICK_BLOCKS, 128), ID), ((BRICK_BLOCKS, 128), F32)]
         + [(s, BF16) for s in shapes]
         + [((LAT, 1), F32)],
-        flips, live, spec, pair_first, pair_second, pair_valid, w_radial.T, w_first.T, w_second.T, w_value, w_env, w_latent,
+        flips, live, pair_first, pair_second, pair_valid, w_radial.T, w_first.T, w_second.T, w_value, w_env, w_latent,
         jnp.swapaxes(w_tensor, 1, 2), w_mix, w_read, read_vec[None, :],
-        smem=2, fetched=14,
+        smem=2, fetched=13,
     )
 
     def rows(n):
         return ((n, PAIRS), F32)
 
-    partials = [((VEC, OWN), F32)] + [((VEC, GHOST), F32)] * 4
-    scratch = [((2 * VEC, ROWS), BF16), ((ROWS, 2 * WIDE), F32)]
+    owned = ((VEC, OWN), F32)
+    ghosted = [((VEC, GHOST), F32)] * 4
+    partials = [((2 * WIDE, PAIRS), BF16)] + ghosted
+    table = ((2 * VEC, 4 * GHOST), BF16)
+    acc = ((4 * GHOST, 2 * WIDE), F32)
+
+    def own_part(parts, out):
+        return call(own_scatter_kernel, [out], live, parts, oh, scratch=[((OWN, parts.shape[0]), F32)], smem=1)[0]
+
+    def gathered(own, listed):
+        (gap,) = call(own_gather_kernel, [rows(VEC)], live, own, oh, smem=1)
+        return [gap] + listed
 
     def combine(own, arrived):
-        own, *listed = call(combine_kernel, partials, own, *arrived, ohs)
+        own, *listed = call(combine_kernel, [owned] + ghosted, own, *arrived, ohs)
         return own, listed
 
-    def complete(own, ghosts):
-        own, listed = combine(own, exchange(ghosts))
-        return [own] + exchange(listed)
-
-    def complete_and_add(own, ghosts, energy, steps):
+    def complete(parts, ghosts):
+        arrived = exchange(ghosts)
+        own, listed = combine(own_part(parts, owned), arrived)
+        return gathered(own, exchange(listed))
+
+    def complete_and_add(parts, ghosts, energy, steps):
         arrived, energy = exchange_and_add(ghosts, energy, steps[0])
-        own, listed = combine(own, arrived)
+        own, listed = combine(own_part(parts, owned), arrived)
         listed, energy = exchange_and_add(listed, energy, steps[1])
-        return [own] + listed, energy
-
-    geo, slope, lat0, evh0, own, *ghosts = call(
+        return gathered(own, listed), energy
+
+    geo, slope, lat0, evh0, parts, *ghosts = call(
         embed_kernel,
         [rows(8), rows(LAT), rows(LAT), rows(2 * CH + LAT)] + partials,
-        live, atoms, *coords, oh, info, embed, evl,
-        scratch=[((32, ROWS), BF16), scratch[1]],
+        live, atoms, *coords, ids, mask, oh, embed, evl,
+        scratch=[acc],
         smem=1,
     )
-    table = complete(own, ghosts)
-    gap0, hid0, lat1, evh1, own, *ghosts = call(
+    given = complete(parts, ghosts)
+    gap0, hid0, lat1, evh1, parts, *ghosts = call(
         middle_kernel,
         [rows(VEC), rows(LAT), rows(LAT), rows(2 * CH + LAT)] + partials,
-        live, *table, oh, geo, lat0, evh0, evl, tens, mix,
-        scratch=scratch, smem=1,
-    )
-    table = complete(own, ghosts)
-    energy, dlat, dgeo, own, *ghosts = call(
+        live, *given, oh, geo, lat0, evh0, evl, tens, mix,
+        scratch=[table, acc], smem=1,
+    )
+    given = complete(parts, ghosts)
+    energy, dlat, dgeo, parts, *ghosts = call(
         turn_kernel,
         [((8, 128), F32), rows(LAT), rows(8)] + partials,
-        live, *table, oh, geo, lat1, evh1, column, tens, mix, read, read_t, mix_t, lt_t, val_t,
-        scratch=scratch, smem=1,
+        live, *given, oh, geo, lat1, evh1, column, tens, mix, read, read_t, mix_t, lt_t, val_t,
+        scratch=[table, acc], smem=1,
     )
     energy = add_across(energy, 1)
-    table, energy = complete_and_add(own, ghosts, energy, (2, 4))
-    dlat, dgeo, own, *ghosts = call(
+    given, energy = complete_and_add(parts, ghosts, energy, (2, 4))
+    dlat, dgeo, parts, *ghosts = call(
         back_kernel,
         [rows(LAT), rows(8)] + partials,
-        live, *table, oh, geo, evh1, dlat, dgeo, gap0, hid0, evh0, mix_t, lt_t, val_t, env_t,
-        scratch=scratch, smem=1,
-    )
-    table, energy = complete_and_add(own, ghosts, energy, (8, 16))
-    own, *ghosts = call(
+        live, *given, oh, geo, evh1, dlat, dgeo, gap0, hid0, evh0, mix_t, lt_t, val_t, env_t,
+        scratch=[table, acc], smem=1,
+    )
+    given, energy = complete_and_add(parts, ghosts, energy, (8, 16))
+    parts, *ghosts = call(
         force_kernel,
-        [((8, OWN), F32)] + [((8, GHOST), F32)] * 4,
-        live, *table, oh, geo, evh0, dlat, dgeo, slope, env_t, rad_t,
-        scratch=[scratch[0], ((8, ROWS), F32)], smem=1,
+        [((WIDE, PAIRS), BF16)] + [((8, GHOST), F32)] * 4,
+        live, *given, oh, geo, evh0, dlat, dgeo, slope, env_t, rad_t,
+        scratch=[table, ((4 * GHOST, WIDE), F32)], smem=1,
     )
     arrived, energy = exchange_and_add(ghosts, energy, 32)
+    own = own_part(parts, ((8, OWN), F32))
     (forces,) = call(final_kernel, [((3, OWN), F32)], own, *arrived, ohs)
     total = add_across(energy, 64)
     return (forces, total[0, 0] / (lax.axis_size("brick") * PAIRS))

time: 235 us -> 218 us (0.928)
  waiting for transfers between devices: 18.9 us -> 1.48 us
  starting transfers between devices: 155 us -> 146 us
  Pallas kernels: 56.6 us -> 64.6 us
    ppermute x7, starting transfers between devices: 78.5 us -> 59.8 us  [add_across(): lax.ppermute(value, 'brick', [(i, i ^ step) for i in range(count)])]
    ppermute x40, waiting for transfers between devices: 11.7 us -> 0.28 us  [exchange(): got[m] = lax.ppermute(blocks[m], 'brick', matching(m, count))]
    ppermute x40, starting transfers between devices: 77 us -> 86.6 us  [exchange(): got[m] = lax.ppermute(blocks[m], 'brick', matching(m, count))]
    pallas_call x12 -> x21, Pallas kernels: 56.6 us -> 64.6 us  [call(): pl.pallas_call(kernel, out_shape=[jax.ShapeDtypeStruct(s, d) for s, d in...]
    ppermute x7, waiting for transfers between devices: 7.17 us -> 1.2 us  [add_across(): lax.ppermute(value, 'brick', [(i, i ^ step) for i in range(count)])]
  transfers between devices with their start and end apart: 47 -> 47, of which waited for: 14 -> 3; matrix products, arithmetic and copies ran while one was open for 0% -> 0% of each run, Pallas kernels for 3% -> 11%
where the time goes in v3:
time: 218 us; the launch traced here: 216 us
  starting transfers between devices  146 us (67%)
  Pallas kernels  64.6 us (30%)
  between operations  3.08 us (1%)
    ppermute x40, starting transfers between devices, exchange(): got[m] = lax.ppermute(blocks[m], 'brick', matching(m, count))  86.6 us
    pallas_call x21, Pallas kernels, call(): pl.pallas_call(kernel, out_shape=[jax.ShapeDtypeStruct(s, d) for s, d in...  64.6 us
    ppermute x7, starting transfers between devices, add_across(): lax.ppermute(value, 'brick', [(i, i ^ step) for i in range(count)])  59.8 us
  transfers between devices with their start and end apart: 47, of which 3 were waited for; matrix products, arithmetic and copies ran while one was open for 0% of the time, Pallas kernels for 11%

profile of v3, /device:TPU:1, one launch (start us, length us, event | category | flops | bytes accessed | tf_op | source)
XLA Modules:
  0.0 216.1 jit_solution(8610099777312479825)
XLA Ops:
  0.7 2.2 %shard_map.167 = (f32[8,256]{1,0:T(8,128)S(1)}, f32[8,256]{1,0:T(8,128)S(1)}, f32[8,256]{1,0:T(8,128)S(1)}, f32[8,256]{1,0:T(8,128)S(1)}, bf16[512,1024]{1,0:T(8...) custom-call(s32[1,2]{1,0:T(1,128)S(1)} %add_bitcast_fusion.flip_ref, f32[3,512]{1,0:T(4,128)} %pos_in.1, ...), custom_call_target="tpu_custom_call" | custom-call | tf_op jit(solution)/shard_map/pallas_call | solution.py:528
  4.4 3.2 %collective-permute-start.1 = (f32[8,256]{1,0:T(8,128)S(1)}, f32[8,256]{1,0:T(8,128)S(1)}, u32[]{:S(2)}, u32[]{:S(2)}) collective-permute-start(f32[8,256]{1,0:T(8,128)S(1)} %get-tuple-element.110), channel_id=1, source_target_pairs={{1,2},{2,1},{3,4},{4,3},{5,6},{6,5},{7,8},{8,7},{9,10},{10,9},{11,... | collective-permute-start | bytes 24584 | tf_op jit(solution)/shard_map/ppermute | solution.py:551
  9.7 4.7 %shard_map.168 = (bf16[1536,6144]{1,0:T(8,128)(2,1)S(1)}, s32[2,48,128]{2,1,0:T(8,128)S(1)}, f32[48,128]{1,0:T(8,128)S(1)}, bf16[64,64]{1,0:T(8,128)(2,1)S(1)}, ...) custom-call(s32[1,2]{1,0:T(1,128)S(1)} %add_bitcast_fusion.flip_ref,, ...), custom_call_target="tpu_custom_call" | custom-call | tf_op jit(solution)/shard_map/pallas_call | solution.py:528
  14.4 5.7 %shard_map.169 = (f32[8,6144]{1,0:T(8,128)S(1)}, f32[64,6144]{1,0:T(8,128)S(1)}, f32[64,6144]{1,0:T(8,128)S(1)}, f32[128,6144]{1,0:T(8,128)S(1)}, bf16[256,6144]...) custom-call(s32[1,1]{1,0:T(1,128)} %get-tuple-element.107.live_ref, ...), custom_call_target="tpu_custom_call" | custom-call | tf_op jit(solution)/shard_map/pallas_call | solution.py:528
  20.2 2.8 %collective-permute-start.5 = (f32[96,256]{1,0:T(8,128)S(1)}, f32[96,256]{1,0:T(8,128)S(1)}, u32[]{:S(2)}, u32[]{:S(2)}) collective-permute-start(f32[96,256]{1,0:T(8,128)S(1)} %get-tuple-element.120), channel_id=1, source_target_pairs={{1,2},{2,1},{3,4},{4,3},{5,6},{6,5},{7,8},{8,7},{9,10},{10,9},{11,... | collective-permute-start | bytes 294920 | tf_op jit(solution)/shard_map/ppermute | solution.py:551
  23.0 2.7 %collective-permute-start.6 = (f32[96,256]{1,0:T(8,128)S(1)}, f32[96,256]{1,0:T(8,128)S(1)}, u32[]{:S(2)}, u32[]{:S(2)}) collective-permute-start(f32[96,256]{1,0:T(8,128)S(1)} %get-tuple-element.121), channel_id=1, source_target_pairs={{0,2},{1,3},{2,0},{3,1},{4,6},{5,7},{6,4},{7,5},{8,10},{9,11},{10,... | collective-permute-start | bytes 294920 | tf_op jit(solution)/shard_map/ppermute | solution.py:551
  26.4 2.3 %shard_map.170.own_ref = f32[96,512]{1,0:T(8,128)S(1)} custom-call(s32[1,1]{1,0:T(1,128)} %get-tuple-element.107.live_ref, bf16[256,6144]{1,0:T(8,128)(2,1)S(1)} %get-tuple-element.118.parts_ref, bf16[1536,6144]{1,0:T(8,128)(2,1)S(1)} %get-tuple-element.115.oh_ref), custom_call_target="tpu_custom_call" | custom-call | tf_op jit(solution)/shard_map/pallas_call | solution.py:528
  29.6 7.8 %collective-permute-start.9 = (f32[96,256]{1,0:T(8,128)S(1)}, f32[96,256]{1,0:T(8,128)S(1)}, u32[]{:S(2)}, u32[]{:S(2)}) collective-permute-start(f32[96,256]{1,0:T(8,128)S(1)} %get-tuple-element.126), channel_id=1, source_target_pairs={{1,2},{2,1},{3,4},{4,3},{5,6},{6,5},{7,8},{8,7},{9,10},{10,9},{11,... | collective-permute-start | bytes 294920 | tf_op jit(solution)/shard_map/ppermute | solution.py:551
  41.8 6.6 %shard_map.173 = (f32[96,6144]{1,0:T(8,128)S(1)}, f32[64,6144]{1,0:T(8,128)S(1)}, f32[64,6144]{1,0:T(8,128)S(1)}, f32[128,6144]{1,0:T(8,128)S(1)}, bf16[256,6144...) custom-call(s32[1,1]{1,0:T(1,128)} %get-tuple-element.107.live_ref, ...), custom_call_target="tpu_custom_call" | custom-call | tf_op jit(solution)/shard_map/pallas_call | solution.py:528
  48.7 5.6 %collective-permute-start.13 = (f32[96,256]{1,0:T(8,128)S(1)}, f32[96,256]{1,0:T(8,128)S(1)}, u32[]{:S(2)}, u32[]{:S(2)}) collective-permute-start(f32[96,256]{1,0:T(8,128)S(1)} %get-tuple-element.136), channel_id=1, source_target_pairs={{1,2},{2,1},{3,4},{4,3},{5,6},{6,5},{7,8},{8,7},{9,10},{10,9},{11,... | collective-permute-start | bytes 294920 | tf_op jit(solution)/shard_map/ppermute | solution.py:551
  54.3 4.4 %collective-permute-start.14 = (f32[96,256]{1,0:T(8,128)S(1)}, f32[96,256]{1,0:T(8,128)S(1)}, u32[]{:S(2)}, u32[]{:S(2)}) collective-permute-start(f32[96,256]{1,0:T(8,128)S(1)} %get-tuple-element.137), channel_id=1, source_target_pairs={{0,2},{1,3},{2,0},{3,1},{4,6},{5,7},{6,4},{7,5},{8,10},{9,11},{10,... | collective-permute-start | bytes 294920 | tf_op jit(solution)/shard_map/ppermute | solution.py:551
  59.3 2.3 %shard_map.174.own_ref = f32[96,512]{1,0:T(8,128)S(1)} custom-call(s32[1,1]{1,0:T(1,128)} %get-tuple-element.107.live_ref, bf16[256,6144]{1,0:T(8,128)(2,1)S(1)} %get-tuple-element.134.parts_ref, bf16[1536,6144]{1,0:T(8,128)(2,1)S(1)} %get-tuple-element.115.oh_ref), custom_call_target="tpu_custom_call" | custom-call | tf_op jit(solution)/shard_map/pallas_call | solution.py:528
  62.5 8.2 %collective-permute-start.17 = (f32[96,256]{1,0:T(8,128)S(1)}, f32[96,256]{1,0:T(8,128)S(1)}, u32[]{:S(2)}, u32[]{:S(2)}) collective-permute-start(f32[96,256]{1,0:T(8,128)S(1)} %get-tuple-element.141), channel_id=1, source_target_pairs={{1,2},{2,1},{3,4},{4,3},{5,6},{6,5},{7,8},{8,7},{9,10},{10,9},{11,... | collective-permute-start | bytes 294920 | tf_op jit(solution)/shard_map/ppermute | solution.py:551
  75.1 8.7 %shard_map.177 = (f32[8,128]{1,0:T(8,128)S(1)}, f32[64,6144]{1,0:T(8,128)S(1)}, f32[8,6144]{1,0:T(8,128)S(1)}, bf16[256,6144]{1,0:T(8,128)(2,1)S(1)}, f32[96,256...) custom-call(s32[1,1]{1,0:T(1,128)} %get-tuple-element.107.live_ref, ...), custom_call_target="tpu_custom_call" | custom-call | tf_op jit(solution)/shard_map/pallas_call | solution.py:528
  85.3 4.4 %collective-permute-start.22 = (f32[96,256]{1,0:T(8,128)S(1)}, f32[96,256]{1,0:T(8,128)S(1)}, u32[]{:S(2)}, u32[]{:S(2)}) collective-permute-start(f32[96,256]{1,0:T(8,128)S(1)} %get-tuple-element.159), channel_id=1, source_target_pairs={{1,2},{2,1},{3,4},{4,3},{5,6},{6,5},{7,8},{8,7},{9,10},{10,9},{11,... | collective-permute-start | bytes 294920 | tf_op jit(solution)/shard_map/ppermute | solution.py:551
  89.7 5.4 %collective-permute-start.23 = (f32[96,256]{1,0:T(8,128)S(1)}, f32[96,256]{1,0:T(8,128)S(1)}, u32[]{:S(2)}, u32[]{:S(2)}) collective-permute-start(f32[96,256]{1,0:T(8,128)S(1)} %get-tuple-element.160), channel_id=1, source_target_pairs={{0,2},{1,3},{2,0},{3,1},{4,6},{5,7},{6,4},{7,5},{8,10},{9,11},{10,... | collective-permute-start | bytes 294920 | tf_op jit(solution)/shard_map/ppermute | solution.py:551
  95.8 6.5 %collective-permute-start.25 = (f32[8,128]{1,0:T(8,128)S(1)}, f32[8,128]{1,0:T(8,128)S(1)}, u32[]{:S(2)}, u32[]{:S(2)}) collective-permute-start(f32[8,128]{1,0:T(8,128)S(1)} %add.21), channel_id=1, source_target_pairs={{0,2},{1,3},{2,0},{3,1},{4,6},{5,7},{6,4},{7,5},{8,10},{9,11},{10,... | collective-permute-start | bytes 12296 | tf_op jit(solution)/shard_map/ppermute | solution.py:565
  102.2 2.3 %shard_map.178.own_ref = f32[96,512]{1,0:T(8,128)S(1)} custom-call(s32[1,1]{1,0:T(1,128)} %get-tuple-element.107.live_ref, bf16[256,6144]{1,0:T(8,128)(2,1)S(1)} %get-tuple-element.152.parts_ref, bf16[1536,6144]{1,0:T(8,128)(2,1)S(1)} %get-tuple-element.115.oh_ref), custom_call_target="tpu_custom_call" | custom-call | tf_op jit(solution)/shard_map/pallas_call | solution.py:528
  105.5 2.4 %collective-permute-start.27 = (f32[96,256]{1,0:T(8,128)S(1)}, f32[96,256]{1,0:T(8,128)S(1)}, u32[]{:S(2)}, u32[]{:S(2)}) collective-permute-start(f32[96,256]{1,0:T(8,128)S(1)} %get-tuple-element.169), channel_id=1, source_target_pairs={{1,2},{2,1},{3,4},{4,3},{5,6},{6,5},{7,8},{8,7},{9,10},{10,9},{11,... | collective-permute-start | bytes 294920 | tf_op jit(solution)/shard_map/ppermute | solution.py:551
  107.9 2.1 collective-permute-start.28
  110.7 5.4 %collective-permute-start.30 = (f32[8,128]{1,0:T(8,128)S(1)}, f32[8,128]{1,0:T(8,128)S(1)}, u32[]{:S(2)}, u32[]{:S(2)}) collective-permute-start(f32[8,128]{1,0:T(8,128)S(1)} %add.22), channel_id=1, source_target_pairs={{0,4},{1,5},{2,6},{3,7},{4,0},{5,1},{6,2},{7,3},{8,12},{9,13},{10,... | collective-permute-start | bytes 12296 | tf_op jit(solution)/shard_map/ppermute | solution.py:565
  118.0 7.3 %shard_map.181 = (f32[64,6144]{1,0:T(8,128)S(1)}, f32[8,6144]{1,0:T(8,128)S(1)}, bf16[256,6144]{1,0:T(8,128)(2,1)S(1)}, f32[96,256]{1,0:T(8,128)S(1)}, f32[96,25...) custom-call(s32[1,1]{1,0:T(1,128)} %get-tuple-element.107.live_ref, ...), custom_call_target="tpu_custom_call" | custom-call | tf_op jit(solution)/shard_map/pallas_call | solution.py:528
  127.3 2.2 %collective-permute-start.33 = (f32[96,256]{1,0:T(8,128)S(1)}, f32[96,256]{1,0:T(8,128)S(1)}, u32[]{:S(2)}, u32[]{:S(2)}) collective-permute-start(f32[96,256]{1,0:T(8,128)S(1)} %get-tuple-element.185), channel_id=1, source_target_pairs={{0,2},{1,3},{2,0},{3,1},{4,6},{5,7},{6,4},{7,5},{8,10},{9,11},{10,... | collective-permute-start | bytes 294920 | tf_op jit(solution)/shard_map/ppermute | solution.py:551
  130.1 8.0 %collective-permute-start.35 = (f32[8,128]{1,0:T(8,128)S(1)}, f32[8,128]{1,0:T(8,128)S(1)}, u32[]{:S(2)}, u32[]{:S(2)}) collective-permute-start(f32[8,128]{1,0:T(8,128)S(1)} %add.23), channel_id=1, source_target_pairs={{0,8},{1,9},{2,10},{3,11},{4,12},{5,13},{6,14},{7,15},{8,0},{9,1},... | collective-permute-start | bytes 12296 | tf_op jit(solution)/shard_map/ppermute | solution.py:565
  138.1 2.5 %shard_map.182.own_ref = f32[96,512]{1,0:T(8,128)S(1)} custom-call(s32[1,1]{1,0:T(1,128)} %get-tuple-element.107.live_ref, bf16[256,6144]{1,0:T(8,128)(2,1)S(1)} %get-tuple-element.177.parts_ref, bf16[1536,6144]{1,0:T(8,128)(2,1)S(1)} %get-tuple-element.115.oh_ref), custom_call_target="tpu_custom_call" | custom-call | tf_op jit(solution)/shard_map/pallas_call | solution.py:528
  142.2 9.3 %collective-permute-start.37 = (f32[96,256]{1,0:T(8,128)S(1)}, f32[96,256]{1,0:T(8,128)S(1)}, u32[]{:S(2)}, u32[]{:S(2)}) collective-permute-start(f32[96,256]{1,0:T(8,128)S(1)} %get-tuple-element.194), channel_id=1, source_target_pairs={{1,2},{2,1},{3,4},{4,3},{5,6},{6,5},{7,8},{8,7},{9,10},{10,9},{11,... | collective-permute-start | bytes 294920 | tf_op jit(solution)/shard_map/ppermute | solution.py:551
  153.0 11.4 %collective-permute-start.40 = (f32[8,128]{1,0:T(8,128)S(1)}, f32[8,128]{1,0:T(8,128)S(1)}, u32[]{:S(2)}, u32[]{:S(2)}) collective-permute-start(f32[8,128]{1,0:T(8,128)S(1)} %add.24), channel_id=1, source_target_pairs={{0,16},{1,17},{2,18},{3,19},{4,20},{5,21},{6,22},{7,23},{8,24},{9,... | collective-permute-start | bytes 12296 | tf_op jit(solution)/shard_map/ppermute | solution.py:565
  166.4 6.1 %shard_map.185 = (bf16[128,6144]{1,0:T(8,128)(2,1)S(1)}, f32[8,256]{1,0:T(8,128)S(1)}, f32[8,256]{1,0:T(8,128)S(1)}, f32[8,256]{1,0:T(8,128)S(1)}, f32[8,256]{1,0:T(8,128)S(1)}) custom-call(s32[1,1]{1,0:T(1,128)} %get-tuple-element.107.live_ref, f32[96,6144]{1,0:T(8,128)S(1)} %shard_map.184.own_gap_ref, f32[96,256]{1,0:T(8,128)S(1)} %collective-permute-done.36.t0, ...), custom_call_target="tpu_custom_call" | custom-call | tf_op jit(solution)/shard_map/pallas_call | solution.py:528
  172.4 11.0 %collective-permute-start.45 = (f32[8,128]{1,0:T(8,128)S(1)}, f32[8,128]{1,0:T(8,128)S(1)}, u32[]{:S(2)}, u32[]{:S(2)}) collective-permute-start(f32[8,128]{1,0:T(8,128)S(1)} %add.25), channel_id=1, source_target_pairs={{0,32},{1,33},{2,34},{3,35},{4,36},{5,37},{6,38},{7,39},{8,40},{9,... | collective-permute-start | bytes 12296 | tf_op jit(solution)/shard_map/ppermute | solution.py:565
  184.4 8.1 %collective-permute-start.42 = (f32[8,256]{1,0:T(8,128)S(1)}, f32[8,256]{1,0:T(8,128)S(1)}, u32[]{:S(2)}, u32[]{:S(2)}) collective-permute-start(f32[8,256]{1,0:T(8,128)S(1)} %get-tuple-element.208), channel_id=1, source_target_pairs={{1,2},{2,1},{3,4},{4,3},{5,6},{6,5},{7,8},{8,7},{9,10},{10,9},{11,... | collective-permute-start | bytes 24584 | tf_op jit(solution)/shard_map/ppermute | solution.py:551
  193.3 17.3 %collective-permute-start.46 = (f32[8,128]{1,0:T(8,128)S(1)}, f32[8,128]{1,0:T(8,128)S(1)}, u32[]{:S(2)}, u32[]{:S(2)}) collective-permute-start(f32[8,128]{1,0:T(8,128)S(1)} %add.26), channel_id=1, source_target_pairs={{0,64},{1,65},{2,66},{3,67},{4,68},{5,69},{6,70},{7,71},{8,72},{9,... | collective-permute-start | bytes 12296 | tf_op jit(solution)/shard_map/ppermute | solution.py:565
  210.6 2.2 %shard_map.186.own_ref = f32[8,512]{1,0:T(8,128)S(1)} custom-call(s32[1,1]{1,0:T(1,128)} %get-tuple-element.107.live_ref, bf16[128,6144]{1,0:T(8,128)(2,1)S(1)} %get-tuple-element.201.parts_ref, bf16[1536,6144]{1,0:T(8,128)(2,1)S(1)} %get-tuple-element.115.oh_ref), custom_call_target="tpu_custom_call" | custom-call | tf_op jit(solution)/shard_map/pallas_call | solution.py:528
  (92 shorter events, 32.3 us)
Async XLA Ops:
  2.9 11.5 %collective-permute-start = (f32[8,256]{1,0:T(8,128)S(1)}, f32[8,256]{1,0:T(8,128)S(1)}, u32[]{:S(2)}, u32[]{:S(2)}) collective-permute-start(f32[8,256]{1,0:T(8,128)S(1)} %get-tuple-element.109), channel_id=1, source_target_pairs={{0,1},{1,0},{2,3},{3,2},{4,5},{5,4},{6,7},{7,6},{8,9},{9,8},{10,11... | collective-permute-start | bytes 24584 | tf_op jit(solution)/shard_map/ppermute | solution.py:551
  4.4 10.0 %collective-permute-start.1 = (f32[8,256]{1,0:T(8,128)S(1)}, f32[8,256]{1,0:T(8,128)S(1)}, u32[]{:S(2)}, u32[]{:S(2)}) collective-permute-start(f32[8,256]{1,0:T(8,128)S(1)} %get-tuple-element.110), channel_id=1, source_target_pairs={{1,2},{2,1},{3,4},{4,3},{5,6},{6,5},{7,8},{8,7},{9,10},{10,9},{11,... | collective-permute-start | bytes 24584 | tf_op jit(solution)/shard_map/ppermute | solution.py:551
  29.6 12.2 %collective-permute-start.8 = (f32[96,256]{1,0:T(8,128)S(1)}, f32[96,256]{1,0:T(8,128)S(1)}, u32[]{:S(2)}, u32[]{:S(2)}) collective-permute-start(f32[96,256]{1,0:T(8,128)S(1)} %get-tuple-element.125), channel_id=1, source_target_pairs={{0,1},{1,0},{2,3},{3,2},{4,5},{5,4},{6,7},{7,6},{8,9},{9,8},{10,11... | collective-permute-start | bytes 294920 | tf_op jit(solution)/shard_map/ppermute | solution.py:551
  29.6 12.1 %collective-permute-start.9 = (f32[96,256]{1,0:T(8,128)S(1)}, f32[96,256]{1,0:T(8,128)S(1)}, u32[]{:S(2)}, u32[]{:S(2)}) collective-permute-start(f32[96,256]{1,0:T(8,128)S(1)} %get-tuple-element.126), channel_id=1, source_target_pairs={{1,2},{2,1},{3,4},{4,3},{5,6},{6,5},{7,8},{8,7},{9,10},{10,9},{11,... | collective-permute-start | bytes 294920 | tf_op jit(solution)/shard_map/ppermute | solution.py:551
  48.4 13.1 %collective-permute-start.12 = (f32[96,256]{1,0:T(8,128)S(1)}, f32[96,256]{1,0:T(8,128)S(1)}, u32[]{:S(2)}, u32[]{:S(2)}) collective-permute-start(f32[96,256]{1,0:T(8,128)S(1)} %get-tuple-element.135), channel_id=1, source_target_pairs={{0,1},{1,0},{2,3},{3,2},{4,5},{5,4},{6,7},{7,6},{8,9},{9,8},{10,11... | collective-permute-start | bytes 294920 | tf_op jit(solution)/shard_map/ppermute | solution.py:551
  48.7 12.9 %collective-permute-start.13 = (f32[96,256]{1,0:T(8,128)S(1)}, f32[96,256]{1,0:T(8,128)S(1)}, u32[]{:S(2)}, u32[]{:S(2)}) collective-permute-start(f32[96,256]{1,0:T(8,128)S(1)} %get-tuple-element.136), channel_id=1, source_target_pairs={{1,2},{2,1},{3,4},{4,3},{5,6},{6,5},{7,8},{8,7},{9,10},{10,9},{11,... | collective-permute-start | bytes 294920 | tf_op jit(solution)/shard_map/ppermute | solution.py:551
  62.4 12.5 %collective-permute-start.16 = (f32[96,256]{1,0:T(8,128)S(1)}, f32[96,256]{1,0:T(8,128)S(1)}, u32[]{:S(2)}, u32[]{:S(2)}) collective-permute-start(f32[96,256]{1,0:T(8,128)S(1)} %get-tuple-element.140), channel_id=1, source_target_pairs={{0,1},{1,0},{2,3},{3,2},{4,5},{5,4},{6,7},{7,6},{8,9},{9,8},{10,11... | collective-permute-start | bytes 294920 | tf_op jit(solution)/shard_map/ppermute | solution.py:551
  62.5 12.4 %collective-permute-start.17 = (f32[96,256]{1,0:T(8,128)S(1)}, f32[96,256]{1,0:T(8,128)S(1)}, u32[]{:S(2)}, u32[]{:S(2)}) collective-permute-start(f32[96,256]{1,0:T(8,128)S(1)} %get-tuple-element.141), channel_id=1, source_target_pairs={{1,2},{2,1},{3,4},{4,3},{5,6},{6,5},{7,8},{8,7},{9,10},{10,9},{11,... | collective-permute-start | bytes 294920 | tf_op jit(solution)/shard_map/ppermute | solution.py:551
  85.0 19.5 %collective-permute-start.21 = (f32[96,256]{1,0:T(8,128)S(1)}, f32[96,256]{1,0:T(8,128)S(1)}, u32[]{:S(2)}, u32[]{:S(2)}) collective-permute-start(f32[96,256]{1,0:T(8,128)S(1)} %get-tuple-element.158), channel_id=1, source_target_pairs={{0,1},{1,0},{2,3},{3,2},{4,5},{5,4},{6,7},{7,6},{8,9},{9,8},{10,11... | collective-permute-start | bytes 294920 | tf_op jit(solution)/shard_map/ppermute | solution.py:551
  85.3 19.3 %collective-permute-start.22 = (f32[96,256]{1,0:T(8,128)S(1)}, f32[96,256]{1,0:T(8,128)S(1)}, u32[]{:S(2)}, u32[]{:S(2)}) collective-permute-start(f32[96,256]{1,0:T(8,128)S(1)} %get-tuple-element.159), channel_id=1, source_target_pairs={{1,2},{2,1},{3,4},{4,3},{5,6},{6,5},{7,8},{8,7},{9,10},{10,9},{11,... | collective-permute-start | bytes 294920 | tf_op jit(solution)/shard_map/ppermute | solution.py:551
  89.7 14.9 %collective-permute-start.23 = (f32[96,256]{1,0:T(8,128)S(1)}, f32[96,256]{1,0:T(8,128)S(1)}, u32[]{:S(2)}, u32[]{:S(2)}) collective-permute-start(f32[96,256]{1,0:T(8,128)S(1)} %get-tuple-element.160), channel_id=1, source_target_pairs={{0,2},{1,3},{2,0},{3,1},{4,6},{5,7},{6,4},{7,5},{8,10},{9,11},{10,... | collective-permute-start | bytes 294920 | tf_op jit(solution)/shard_map/ppermute | solution.py:551
  95.1 9.5 %collective-permute-start.24 = (f32[96,256]{1,0:T(8,128)S(1)}, f32[96,256]{1,0:T(8,128)S(1)}, u32[]{:S(2)}, u32[]{:S(2)}) collective-permute-start(f32[96,256]{1,0:T(8,128)S(1)} %get-tuple-element.161), channel_id=1, source_target_pairs={{2,4},{3,5},{4,2},{5,3},{6,8},{7,9},{8,6},{9,7},{10,12},{11,13},{1... | collective-permute-start | bytes 294920 | tf_op jit(solution)/shard_map/ppermute | solution.py:551
  95.8 8.8 %collective-permute-start.25 = (f32[8,128]{1,0:T(8,128)S(1)}, f32[8,128]{1,0:T(8,128)S(1)}, u32[]{:S(2)}, u32[]{:S(2)}) collective-permute-start(f32[8,128]{1,0:T(8,128)S(1)} %add.21), channel_id=1, source_target_pairs={{0,2},{1,3},{2,0},{3,1},{4,6},{5,7},{6,4},{7,5},{8,10},{9,11},{10,... | collective-permute-start | bytes 12296 | tf_op jit(solution)/shard_map/ppermute | solution.py:565
  105.4 12.5 %collective-permute-start.26 = (f32[96,256]{1,0:T(8,128)S(1)}, f32[96,256]{1,0:T(8,128)S(1)}, u32[]{:S(2)}, u32[]{:S(2)}) collective-permute-start(f32[96,256]{1,0:T(8,128)S(1)} %get-tuple-element.168), channel_id=1, source_target_pairs={{0,1},{1,0},{2,3},{3,2},{4,5},{5,4},{6,7},{7,6},{8,9},{9,8},{10,11... | collective-permute-start | bytes 294920 | tf_op jit(solution)/shard_map/ppermute | solution.py:551
  105.5 12.4 %collective-permute-start.27 = (f32[96,256]{1,0:T(8,128)S(1)}, f32[96,256]{1,0:T(8,128)S(1)}, u32[]{:S(2)}, u32[]{:S(2)}) collective-permute-start(f32[96,256]{1,0:T(8,128)S(1)} %get-tuple-element.169), channel_id=1, source_target_pairs={{1,2},{2,1},{3,4},{4,3},{5,6},{6,5},{7,8},{8,7},{9,10},{10,9},{11,... | collective-permute-start | bytes 294920 | tf_op jit(solution)/shard_map/ppermute | solution.py:551
  107.9 10.0 %collective-permute-start.28 = (f32[96,256]{1,0:T(8,128)S(1)}, f32[96,256]{1,0:T(8,128)S(1)}, u32[]{:S(2)}, u32[]{:S(2)}) collective-permute-start(f32[96,256]{1,0:T(8,128)S(1)} %get-tuple-element.170), channel_id=1, source_target_pairs={{0,2},{1,3},{2,0},{3,1},{4,6},{5,7},{6,4},{7,5},{8,10},{9,11},{10,... | collective-permute-start | bytes 294920 | tf_op jit(solution)/shard_map/ppermute | solution.py:551
  125.3 15.6 %collective-permute-start.31 = (f32[96,256]{1,0:T(8,128)S(1)}, f32[96,256]{1,0:T(8,128)S(1)}, u32[]{:S(2)}, u32[]{:S(2)}) collective-permute-start(f32[96,256]{1,0:T(8,128)S(1)} %get-tuple-element.183), channel_id=1, source_target_pairs={{0,1},{1,0},{2,3},{3,2},{4,5},{5,4},{6,7},{7,6},{8,9},{9,8},{10,11... | collective-permute-start | bytes 294920 | tf_op jit(solution)/shard_map/ppermute | solution.py:551
  125.4 15.5 %collective-permute-start.32 = (f32[96,256]{1,0:T(8,128)S(1)}, f32[96,256]{1,0:T(8,128)S(1)}, u32[]{:S(2)}, u32[]{:S(2)}) collective-permute-start(f32[96,256]{1,0:T(8,128)S(1)} %get-tuple-element.184), channel_id=1, source_target_pairs={{1,2},{2,1},{3,4},{4,3},{5,6},{6,5},{7,8},{8,7},{9,10},{10,9},{11,... | collective-permute-start | bytes 294920 | tf_op jit(solution)/shard_map/ppermute | solution.py:551
  127.3 13.6 %collective-permute-start.33 = (f32[96,256]{1,0:T(8,128)S(1)}, f32[96,256]{1,0:T(8,128)S(1)}, u32[]{:S(2)}, u32[]{:S(2)}) collective-permute-start(f32[96,256]{1,0:T(8,128)S(1)} %get-tuple-element.185), channel_id=1, source_target_pairs={{0,2},{1,3},{2,0},{3,1},{4,6},{5,7},{6,4},{7,5},{8,10},{9,11},{10,... | collective-permute-start | bytes 294920 | tf_op jit(solution)/shard_map/ppermute | solution.py:551
  129.5 11.4 %collective-permute-start.34 = (f32[96,256]{1,0:T(8,128)S(1)}, f32[96,256]{1,0:T(8,128)S(1)}, u32[]{:S(2)}, u32[]{:S(2)}) collective-permute-start(f32[96,256]{1,0:T(8,128)S(1)} %get-tuple-element.186), channel_id=1, source_target_pairs={{2,4},{3,5},{4,2},{5,3},{6,8},{7,9},{8,6},{9,7},{10,12},{11,13},{1... | collective-permute-start | bytes 294920 | tf_op jit(solution)/shard_map/ppermute | solution.py:551
  130.1 10.7 %collective-permute-start.35 = (f32[8,128]{1,0:T(8,128)S(1)}, f32[8,128]{1,0:T(8,128)S(1)}, u32[]{:S(2)}, u32[]{:S(2)}) collective-permute-start(f32[8,128]{1,0:T(8,128)S(1)} %add.23), channel_id=1, source_target_pairs={{0,8},{1,9},{2,10},{3,11},{4,12},{5,13},{6,14},{7,15},{8,0},{9,1},... | collective-permute-start | bytes 12296 | tf_op jit(solution)/shard_map/ppermute | solution.py:565
  141.7 24.6 %collective-permute-start.36 = (f32[96,256]{1,0:T(8,128)S(1)}, f32[96,256]{1,0:T(8,128)S(1)}, u32[]{:S(2)}, u32[]{:S(2)}) collective-permute-start(f32[96,256]{1,0:T(8,128)S(1)} %get-tuple-element.193), channel_id=1, source_target_pairs={{0,1},{1,0},{2,3},{3,2},{4,5},{5,4},{6,7},{7,6},{8,9},{9,8},{10,11... | collective-permute-start | bytes 294920 | tf_op jit(solution)/shard_map/ppermute | solution.py:551
  142.2 24.1 %collective-permute-start.37 = (f32[96,256]{1,0:T(8,128)S(1)}, f32[96,256]{1,0:T(8,128)S(1)}, u32[]{:S(2)}, u32[]{:S(2)}) collective-permute-start(f32[96,256]{1,0:T(8,128)S(1)} %get-tuple-element.194), channel_id=1, source_target_pairs={{1,2},{2,1},{3,4},{4,3},{5,6},{6,5},{7,8},{8,7},{9,10},{10,9},{11,... | collective-permute-start | bytes 294920 | tf_op jit(solution)/shard_map/ppermute | solution.py:551
  151.5 14.8 %collective-permute-start.38 = (f32[96,256]{1,0:T(8,128)S(1)}, f32[96,256]{1,0:T(8,128)S(1)}, u32[]{:S(2)}, u32[]{:S(2)}) collective-permute-start(f32[96,256]{1,0:T(8,128)S(1)} %get-tuple-element.195), channel_id=1, source_target_pairs={{0,2},{1,3},{2,0},{3,1},{4,6},{5,7},{6,4},{7,5},{8,10},{9,11},{10,... | collective-permute-start | bytes 294920 | tf_op jit(solution)/shard_map/ppermute | solution.py:551
  152.4 14.0 %collective-permute-start.39 = (f32[96,256]{1,0:T(8,128)S(1)}, f32[96,256]{1,0:T(8,128)S(1)}, u32[]{:S(2)}, u32[]{:S(2)}) collective-permute-start(f32[96,256]{1,0:T(8,128)S(1)} %get-tuple-element.196), channel_id=1, source_target_pairs={{2,4},{3,5},{4,2},{5,3},{6,8},{7,9},{8,6},{9,7},{10,12},{11,13},{1... | collective-permute-start | bytes 294920 | tf_op jit(solution)/shard_map/ppermute | solution.py:551
  153.0 13.3 %collective-permute-start.40 = (f32[8,128]{1,0:T(8,128)S(1)}, f32[8,128]{1,0:T(8,128)S(1)}, u32[]{:S(2)}, u32[]{:S(2)}) collective-permute-start(f32[8,128]{1,0:T(8,128)S(1)} %add.24), channel_id=1, source_target_pairs={{0,16},{1,17},{2,18},{3,19},{4,20},{5,21},{6,22},{7,23},{8,24},{9,... | collective-permute-start | bytes 12296 | tf_op jit(solution)/shard_map/ppermute | solution.py:565
  172.4 20.8 %collective-permute-start.45 = (f32[8,128]{1,0:T(8,128)S(1)}, f32[8,128]{1,0:T(8,128)S(1)}, u32[]{:S(2)}, u32[]{:S(2)}) collective-permute-start(f32[8,128]{1,0:T(8,128)S(1)} %add.25), channel_id=1, source_target_pairs={{0,32},{1,33},{2,34},{3,35},{4,36},{5,37},{6,38},{7,39},{8,40},{9,... | collective-permute-start | bytes 12296 | tf_op jit(solution)/shard_map/ppermute | solution.py:565
  183.5 30.5 %collective-permute-start.41 = (f32[8,256]{1,0:T(8,128)S(1)}, f32[8,256]{1,0:T(8,128)S(1)}, u32[]{:S(2)}, u32[]{:S(2)}) collective-permute-start(f32[8,256]{1,0:T(8,128)S(1)} %get-tuple-element.207), channel_id=1, source_target_pairs={{0,1},{1,0},{2,3},{3,2},{4,5},{5,4},{6,7},{7,6},{8,9},{9,8},{10,11... | collective-permute-start | bytes 24584 | tf_op jit(solution)/shard_map/ppermute | solution.py:551
  184.4 29.6 %collective-permute-start.42 = (f32[8,256]{1,0:T(8,128)S(1)}, f32[8,256]{1,0:T(8,128)S(1)}, u32[]{:S(2)}, u32[]{:S(2)}) collective-permute-start(f32[8,256]{1,0:T(8,128)S(1)} %get-tuple-element.208), channel_id=1, source_target_pairs={{1,2},{2,1},{3,4},{4,3},{5,6},{6,5},{7,8},{8,7},{9,10},{10,9},{11,... | collective-permute-start | bytes 24584 | tf_op jit(solution)/shard_map/ppermute | solution.py:551
  192.5 21.5 %collective-permute-start.43 = (f32[8,256]{1,0:T(8,128)S(1)}, f32[8,256]{1,0:T(8,128)S(1)}, u32[]{:S(2)}, u32[]{:S(2)}) collective-permute-start(f32[8,256]{1,0:T(8,128)S(1)} %get-tuple-element.209), channel_id=1, source_target_pairs={{0,2},{1,3},{2,0},{3,1},{4,6},{5,7},{6,4},{7,5},{8,10},{9,11},{10,... | collective-permute-start | bytes 24584 | tf_op jit(solution)/shard_map/ppermute | solution.py:551
  192.6 21.4 %collective-permute-start.44 = (f32[8,256]{1,0:T(8,128)S(1)}, f32[8,256]{1,0:T(8,128)S(1)}, u32[]{:S(2)}, u32[]{:S(2)}) collective-permute-start(f32[8,256]{1,0:T(8,128)S(1)} %get-tuple-element.210), channel_id=1, source_target_pairs={{2,4},{3,5},{4,2},{5,3},{6,8},{7,9},{8,6},{9,7},{10,12},{11,13},{1... | collective-permute-start | bytes 24584 | tf_op jit(solution)/shard_map/ppermute | solution.py:551
  193.3 19.5 %collective-permute-start.46 = (f32[8,128]{1,0:T(8,128)S(1)}, f32[8,128]{1,0:T(8,128)S(1)}, u32[]{:S(2)}, u32[]{:S(2)}) collective-permute-start(f32[8,128]{1,0:T(8,128)S(1)} %add.26), channel_id=1, source_target_pairs={{0,64},{1,65},{2,66},{3,67},{4,68},{5,69},{6,70},{7,71},{8,72},{9,... | collective-permute-start | bytes 12296 | tf_op jit(solution)/shard_map/ppermute | solution.py:565
  (15 other events, 78.7 us)
